TPU v7x, 256 devices: a whole 4x4x8 slice. The times are simulated.
256 devices in a mesh: pts: 128 (over y, z_lo, x, core), lab: 2 (over z_hi).
Axes of the slice: x: 4, y: 4, z: 8 (z_hi: 2, z_lo: 4; z = z_hi * 4 + z_lo), core: 2. Of those that a mesh axis runs over, the one named last changes fastest.
Arguments:
- slab_points: bfloat16 [8192, 128], P('pts'), may hold values from -6 to 6
- key_points: bfloat16 [131072, 128], P('pts'), may hold values from -6 to 6
- length_weights: float32 [128], replicated, may hold values from 0.5 to 2
- adjoint: bfloat16 [131072, 256], P('pts', 'lab'), may hold values from -0.875 to 0.875
- label_cov: float32 [256, 256], P('lab'), may hold values from -0.375 to 0.375
- cotangent: bfloat16 [8192, 256], P('pts', 'lab'), may hold values from -0.0625 to 0.0625
Outputs:
- mixed_rows: bfloat16 [8192, 256], P('pts', 'lab')
- cov_grad: float32 [256, 256], P('lab')
All inputs are finite; a program needn't handle non-finite values.
Results may differ from a plain program's by a relative error of at most 0.005.
Values may be sent and summed in bfloat16 or wider, within the bound.
No kernel may reach another device: no remote copies, remote signals or barrier semaphores. Data moves between devices by JAX's collectives and lax.ppermute only.
A program may use at most 64 MiB of HBM per device.

v0:
```python
import jax
import jax.numpy as jnp
from jax import lax
from jax.sharding import PartitionSpec as P


def sq_norms(rows, weights):
    wide = rows.astype(jnp.float32)
    return jnp.sum(wide * wide * weights, axis=1)


def kernel_tile(slab_rows, slab_sq, scaled_keys, key_sq, width):
    inner = lax.dot_general(
        slab_rows, scaled_keys, (((1,), (1,)), ((), ())), preferred_element_type=jnp.float32
    )
    dist = slab_sq[:, None] + key_sq[None, :] - 2.0 * inner
    return jnp.exp(dist * (-2.0 / width)).astype(jnp.bfloat16)


def local(slab_points, key_points, length_weights, adjoint, label_cov, cotangent):
    width = slab_points.shape[1]
    half_labels = cotangent.shape[1]
    lab_place = lax.axis_index("lab")
    whole_slab = lax.all_gather(slab_points, "pts", axis=0, tiled=True)
    slab_sq = sq_norms(whole_slab, length_weights)
    scaled = (key_points.astype(jnp.float32) * length_weights).astype(jnp.bfloat16)
    key_sq = sq_norms(key_points, length_weights)
    full_cov = lax.all_gather(label_cov, "lab", axis=0, tiled=True)
    tile = kernel_tile(whole_slab, slab_sq, scaled, key_sq, width)
    cross_own = lax.psum_scatter(
        jnp.dot(tile, adjoint, preferred_element_type=jnp.float32),
        "pts",
        scatter_dimension=0,
        tiled=True,
    )
    cross_full, cot_full = (
        lax.all_gather(cross_own, "lab", axis=1, tiled=True),
        lax.all_gather(cotangent.astype(jnp.float32), "lab", axis=1, tiled=True),
    )
    columns = lax.dynamic_slice_in_dim(full_cov, lab_place * half_labels, half_labels, 1)
    mixed = jnp.dot(
        cross_full, columns, precision=lax.Precision.HIGHEST, preferred_element_type=jnp.float32
    ).astype(jnp.bfloat16)
    partial_grad = jnp.dot(
        cross_own.T, cot_full, precision=lax.Precision.HIGHEST, preferred_element_type=jnp.float32
    )
    grad = lax.psum(partial_grad, "pts")
    return (mixed, grad)


def solution(mesh):
    placed = (P("pts", None), P("pts", None), P(), P("pts", "lab"), P("lab", None), P("pts", "lab"))
    return jax.shard_map(
        local,
        mesh=mesh,
        in_specs=placed,
        out_specs=(P("pts", "lab"), P("lab", None)),
        check_vma=False,
    )
```

profile of v0, /device:TPU:1, one launch (start us, length us, event | category | flops | bytes accessed | tf_op | source)
XLA Modules:
  0.0 2061.3 jit_solution(6185736459932588253)
XLA Ops:
  7.2 0.0 copy-start
  7.2 0.0 all-gather.2.cloned.1.call-start
  7.2 0.7 all-gather.2.cloned.1.call-update
  7.9 0.0 reduce-scatter.2.cloned.1.call-start
  8.0 1.2 fusion.5
  9.1 201.4 %all-gather.2.cloned.1.call-done = bf16[8192,128]{1,0:T(8,128)(2,1)} async-done(((bf16[64,128]{1,0:T(8,128)(2,1)}), bf16[8192,128]{1,0:T(8,128)(2,1)}) %all-gather.2.cloned.1.call-update) | async-done | bytes 2097168 | tf_op jit(solution)/shard_map/all_gather | solution.py:24
  210.6 2.7 multiply_reduce_fusion
  213.3 0.0 copy-done
  213.3 11.9 fusion.3
  225.2 0.0 copy-start.2
  225.2 0.0 copy-start.1
  225.2 0.0 reduce-scatter.2.cloned.1.call-update
  225.3 0.0 all-reduce.2.cloned.1.call-start
  225.3 0.6 copy-done.2
  226.0 7.3 all_gather.15
  233.3 0.0 copy-done.1
  233.3 8.7 all_gather.14
  242.0 660.3 %reduce-scatter.2.cloned.1.call-done = f32[64,128]{1,0:T(8,128)} async-done(((f32[8192,128]{1,0:T(8,128)}), f32[64,128]{1,0:T(8,128)}) %reduce-scatter.2.cloned.1.call-update) | async-done | bytes 32784 | tf_op jit(solution)/shard_map/reduce_scatter | solution.py:30
  902.3 1.7 fusion.15
  904.0 0.0 all-reduce.2.cloned.1.call-update
  904.0 7.6 all_gather.13
  911.6 0.8 convolution_convert_fusion
  912.4 1140.8 %all-reduce.2.cloned.1.call-done = f32[128,256]{1,0:T(8,128)} async-done(((f32[128,256]{1,0:T(8,128)}), f32[128,256]{1,0:T(8,128)}) %all-reduce.2.cloned.1.call-update) | async-done | bytes 131088 | tf_op jit(solution)/shard_map/psum | solution.py:47
  2053.2 1.6 copy.9
  (1 shorter events, 0.0 us)
Async XLA Ops:
  7.2 206.2 %copy-start = (bf16[1024,128]{1,0:T(8,128)(2,1)S(1)}, bf16[1024,128]{1,0:T(8,128)(2,1)}, u32[]{:S(2)}) copy-start(bf16[1024,128]{1,0:T(8,128)(2,1)} %param.9) | copy-start | bytes 786436
  7.2 203.4 %all-gather.2.cloned.1.call-start = ((), (), s32[]{:S(2)}) async-start(), calls=%async_computation.1 | async-start | bytes 2113536 | tf_op jit(solution)/shard_map/all_gather | solution.py:24
  7.9 894.4 %reduce-scatter.2.cloned.1.call-start = ((), (), s32[]{:S(2)}) async-start(), calls=%async_computation.2 | async-start | bytes 4227072 | tf_op jit(solution)/shard_map/reduce_scatter | solution.py:30
  225.2 0.7 copy-start.2
  225.2 8.1 copy-start.1
  225.3 1827.9 %all-reduce.2.cloned.1.call-start = ((), (), s32[]{:S(2)}) async-start(), calls=%async_computation.3 | async-start | bytes 262144 | tf_op jit(solution)/shard_map/psum | solution.py:47
Sparse Core Ops, SparseCore 0:
  9.9 200.6 all-gather.1
  225.4 676.8 reduce-scatter.1
  905.7 1147.4 all-reduce.1
where the time goes:
time: 2060 us
  waiting for transfers between devices  2000 us (97%)
  blocking collectives  23.6 us (1%)
    psum x1, waiting for transfers between devices, local(): grad = lax.psum(partial_grad, 'pts')  1140 us
    reduce_scatter x1, waiting for transfers between devices, local(): lax.psum_scatter(jnp.dot(tile, adjoint, preferred_element_type=jnp.float3...  660 us
    all_gather x1, waiting for transfers between devices, local(): whole_slab = lax.all_gather(slab_points, 'pts', axis=0, tiled=True)  201 us
  transfers between devices with their start and end apart: 3, of which 3 were waited for; matrix products, arithmetic and copies ran while one was open for 0% of the time, Pallas kernels for 0%

commit v1 on v0

v1 whole, which is shorter than its diff:
```python
import jax
import jax.numpy as jnp
from jax import lax
from jax.experimental import pallas as pl
from jax.experimental.pallas import tpu as pltpu
from jax.sharding import PartitionSpec as P

F32 = jnp.float32
BF16 = jnp.bfloat16
PTS = 128
KEYS = 1024
TILE = 256
CORE, X, Z, Y = 0, 1, 3, 5


def swap(value, place, mask):
    return lax.ppermute(value, "pts", [(i, i ^ (mask << place)) for i in range(PTS)])


def swap_lab(value):
    return lax.ppermute(value, "lab", [(0, 1), (1, 0)])


def cross_kernel(weights_ref, rows_ref, *refs):
    packs, wide_ref, sent_ref = refs[:-2], refs[-2], refs[-1]
    rows = rows_ref[:, 0:128]
    wide = rows.astype(F32)
    row_term = jnp.sum(wide * wide * weights_ref[...], axis=1, keepdims=True) * (-1.0 / 64.0)
    total = jnp.zeros((rows.shape[0], 128), F32)
    for pack in packs:
        parts = pack[KEYS : KEYS + 16, :].astype(F32)
        for j in range(KEYS // TILE):
            key_term = parts[j : j + 1] + parts[4 + j : 5 + j] + parts[8 + j : 9 + j]
            tile = pl.ds(j * TILE, TILE)
            inner = lax.dot_general(
                rows, pack[tile, 0:128], (((1,), (1,)), ((), ())), preferred_element_type=F32
            )
            kernel = jnp.exp(inner + row_term + key_term).astype(BF16)
            total += jnp.dot(kernel, pack[tile, 128:256], preferred_element_type=F32)
    wide_ref[...] = total
    sent_ref[...] = total.astype(BF16)


def cross_block(weights, rows, packs):
    count = rows.shape[0]
    return pl.pallas_call(
        cross_kernel,
        out_shape=(
            jax.ShapeDtypeStruct((count, 128), F32),
            jax.ShapeDtypeStruct((count, 128), BF16),
        ),
        in_specs=[pl.BlockSpec(memory_space=pltpu.VMEM)] * (2 + len(packs)),
        out_specs=(pl.BlockSpec(memory_space=pltpu.VMEM),) * 2,
        compiler_params=pltpu.CompilerParams(vmem_limit_bytes=40 * 2**20),
        cost_estimate=pl.CostEstimate(
            flops=4 * count * len(packs) * KEYS * 128,
            bytes_accessed=5 * 2**20,
            transcendentals=count * len(packs) * KEYS,
        ),
        name="cross_block",
    )(weights, rows, *packs)


def local(slab_points, key_points, length_weights, adjoint, label_cov, cotangent):
    first_core = lax.axis_index("pts") % 2 == 0
    first_lab = lax.axis_index("lab") == 0

    keys = key_points.astype(F32)
    scaled = (keys * length_weights * (1.0 / 32.0)).astype(BF16)
    key_term = jnp.sum(keys * keys * length_weights, axis=1) * (-1.0 / 64.0)
    high = lax.reduce_precision(key_term, 8, 7)
    rest = key_term - high
    middle = lax.reduce_precision(rest, 8, 7)
    parts = jnp.stack([high, middle, rest - middle, jnp.zeros_like(high)]).reshape(16, 256)
    pack = jnp.concatenate(
        [jnp.concatenate([scaled, adjoint], axis=1), parts.astype(BF16)], axis=0
    )
    packs = [pack] + [swap(pack, X, m) for m in (1, 2, 3)]
    packs = packs + [swap(p, CORE, 1) for p in packs]

    own = jnp.concatenate([slab_points, cotangent], axis=1)
    over_z = jnp.concatenate([own] + [swap(own, Z, m) for m in (1, 2, 3)], axis=0)
    rows = [over_z] + [swap(over_z, Y, m) for m in (1, 2, 3)]
    cot = jnp.concatenate([r[:, 128:] for r in rows], axis=0)
    cot_far = swap_lab(cot)

    weights = length_weights.reshape(1, 128)
    blocks = {m: cross_block(weights, rows[m], packs) for m in (2, 1, 3, 0)}
    back = {m: swap(blocks[m][1], Y, m).astype(F32) for m in (2, 1, 3)}
    over_y = (blocks[0][0] + back[1]) + (back[2] + back[3])

    sent = jnp.concatenate([blocks[m][1] for m in range(4)], axis=0)
    turned = (((0,), (0,)), ((), ()))
    grad = jnp.concatenate(
        [lax.dot_general(sent, c, turned, preferred_element_type=F32) for c in (cot, cot_far)],
        axis=1,
    )
    upper, lower = grad[:64], grad[64:]
    grad = jnp.where(first_core, upper, lower) + swap(
        jnp.where(first_core, lower, upper), CORE, 1
    )

    joint = [jnp.concatenate([over_y[64 * m : 64 * m + 64], grad], axis=1) for m in range(4)]
    back = [swap(joint[m], Z, m) for m in (1, 2, 3)]
    joint = (joint[0] + back[0]) + (back[1] + back[2])
    cross, grad = joint[:, :128], joint[:, 128:]

    back = [swap(grad, Y, m) for m in (1, 2, 3)]
    part = jnp.dot(cross, label_cov, precision=lax.Precision.HIGHEST, preferred_element_type=F32)
    near, far = part[:, :128], part[:, 128:]
    mixed = jnp.where(first_lab, near, far) + swap_lab(jnp.where(first_lab, far, near))

    grad = (grad + back[0]) + (back[1] + back[2])
    back = [swap(grad, X, m) for m in (1, 2, 3)]
    grad = (grad + back[0]) + (back[1] + back[2])
    grad = jnp.where(
        first_lab, grad, jnp.concatenate([grad[:, 128:], grad[:, :128]], axis=1)
    )
    other = swap(grad, CORE, 1)
    grad = jnp.where(
        first_core,
        jnp.concatenate([grad, other], axis=0),
        jnp.concatenate([other, grad], axis=0),
    )
    return mixed.astype(BF16), grad


def solution(mesh):
    placed = (P("pts", None), P("pts", None), P(), P("pts", "lab"), P("lab", None), P("pts", "lab"))
    return jax.shard_map(
        local,
        mesh=mesh,
        in_specs=placed,
        out_specs=(P("pts", "lab"), P("lab", None)),
        check_vma=False,
    )
```

time: 2060 us -> 130 us (0.06)
  the two profiles are of different devices: /device:TPU:1 before, /device:TPU:32 now
where the time goes in v1:
time: 130 us
  waiting for transfers between devices  62 us (48%)
  starting transfers between devices  42.7 us (33%)
  Pallas kernels  17.3 us (13%)
  local copies, waits for them, and re-layouts  3.74 us (3%)
  other arithmetic  2.54 us (2%)
    ppermute x27, waiting for transfers between devices, swap(): lax.ppermute(value, 'pts', [(i, i ^ mask << place) for i in range(PTS)])  58.7 us
    ppermute x27, starting transfers between devices, swap(): lax.ppermute(value, 'pts', [(i, i ^ mask << place) for i in range(PTS)])  35.7 us
    pallas_call x4, Pallas kernels, cross_block(): pl.pallas_call(cross_kernel, out_shape=(jax.ShapeDtypeStruct((count, 128)...  17.3 us
    ppermute x2, starting transfers between devices, swap_lab(): return lax.ppermute(value, 'lab', [(0, 1), (1, 0)])  6.98 us
    ppermute x2, waiting for transfers between devices, swap_lab(): return lax.ppermute(value, 'lab', [(0, 1), (1, 0)])  3.3 us
  transfers between devices with their start and end apart: 29, of which 19 were waited for; matrix products, arithmetic and copies ran while one was open for 3% of the time, Pallas kernels for 13%

profile of v1, /device:TPU:32, one launch (start us, length us, event | category | flops | bytes accessed | tf_op | source)
XLA Modules:
  0.0 130.0 jit_solution(13227896992679425200)
XLA Ops:
  0.7 1.2 fusion.1
  2.2 1.6 %collective-permute-start.3 = (bf16[1040,256]{1,0:T(8,128)(2,1)S(1)}, bf16[1040,256]{1,0:T(8,128)(2,1)S(1)}, u32[]{:S(2)}, u32[]{:S(2)}) collective-permute-start(bf16[1040,256]{1,0:T(8,128)(2,1)S(1)} %pad_maximum_fusion.refs_0_), channel_id=1, source_target_pairs={{0,4},{2,6},{4,0},{6,2},{8,12},{10,14},{12,8},{14,10},{16,20},{18,... | collective-permute-start | bytes 1597448 | tf_op jit(solution)/shard_map/ppermute | solution.py:17
  3.8 2.7 %collective-permute-start.4 = (bf16[1040,256]{1,0:T(8,128)(2,1)S(1)}, bf16[1040,256]{1,0:T(8,128)(2,1)S(1)}, u32[]{:S(2)}, u32[]{:S(2)}) collective-permute-start(bf16[1040,256]{1,0:T(8,128)(2,1)S(1)} %pad_maximum_fusion.refs_0_), channel_id=1, source_target_pairs={{0,8},{2,10},{4,12},{6,14},{8,0},{10,2},{12,4},{14,6},{16,24},{18,... | collective-permute-start | bytes 1597448 | tf_op jit(solution)/shard_map/ppermute | solution.py:17
  6.5 0.5 collective-permute-start.5
  7.0 1.9 %collective-permute-start = (bf16[64,256]{1,0:T(8,128)(2,1)S(1)}, bf16[64,256]{1,0:T(8,128)(2,1)S(1)}, u32[]{:S(2)}, u32[]{:S(2)}) collective-permute-start(bf16[64,256]{1,0:T(8,128)(2,1)S(1)} %constant_dynamic-update-slice_fusion), channel_id=1, source_target_pairs={{0,16},{2,18},{4,20},{6,22},{8,24},{10,26},{12,28},{14,30},{16,0},... | collective-permute-start | bytes 98312 | tf_op jit(solution)/shard_map/ppermute | solution.py:17
  8.9 1.5 %collective-permute-start.1 = (bf16[64,256]{1,0:T(8,128)(2,1)S(1)}, bf16[64,256]{1,0:T(8,128)(2,1)S(1)}, u32[]{:S(2)}, u32[]{:S(2)}) collective-permute-start(bf16[64,256]{1,0:T(8,128)(2,1)S(1)} %constant_dynamic-update-slice_fusion), channel_id=1, source_target_pairs={{0,32},{2,34},{4,36},{6,38},{8,40},{10,42},{12,44},{14,46},{16,48}... | collective-permute-start | bytes 98312 | tf_op jit(solution)/shard_map/ppermute | solution.py:17
  10.5 0.5 collective-permute-done
  11.0 1.9 %collective-permute-start.2 = (bf16[64,256]{1,0:T(8,128)(2,1)S(1)}, bf16[64,256]{1,0:T(8,128)(2,1)S(1)}, u32[]{:S(2)}, u32[]{:S(2)}) collective-permute-start(bf16[64,256]{1,0:T(8,128)(2,1)S(1)} %constant_dynamic-update-slice_fusion), channel_id=1, source_target_pairs={{0,48},{2,50},{4,52},{6,54},{8,56},{10,58},{12,60},{14,62},{16,32}... | collective-permute-start | bytes 98312 | tf_op jit(solution)/shard_map/ppermute | solution.py:17
  12.9 0.8 collective-permute-done.1
  13.7 3.5 %collective-permute-done.3.refs_1_ = bf16[1040,256]{1,0:T(8,128)(2,1)S(1)} collective-permute-done((bf16[1040,256]{1,0:T(8,128)(2,1)S(1)}, bf16[1040,256]{1,0:T(8,128)(2,1)S(1)}, u32[]{:S(2)}, u32[]{:S(2)}) %collective-permute-start.3) | collective-permute-done | bytes 532512 | tf_op jit(solution)/shard_map/ppermute | solution.py:17
  17.3 12.6 %collective-permute-done.4.refs_2_ = bf16[1040,256]{1,0:T(8,128)(2,1)S(1)} collective-permute-done((bf16[1040,256]{1,0:T(8,128)(2,1)S(1)}, bf16[1040,256]{1,0:T(8,128)(2,1)S(1)}, u32[]{:S(2)}, u32[]{:S(2)}) %collective-permute-start.4) | collective-permute-done | bytes 532512 | tf_op jit(solution)/shard_map/ppermute | solution.py:17
  29.8 2.6 %collective-permute-done.5.refs_3_ = bf16[1040,256]{1,0:T(8,128)(2,1)S(1)} collective-permute-done((bf16[1040,256]{1,0:T(8,128)(2,1)S(1)}, bf16[1040,256]{1,0:T(8,128)(2,1)S(1)}, u32[]{:S(2)}, u32[]{:S(2)}) %collective-permute-start.5) | collective-permute-done | bytes 532512 | tf_op jit(solution)/shard_map/ppermute | solution.py:17
  32.4 3.3 %collective-permute-start.12 = (bf16[256,256]{1,0:T(8,128)(2,1)S(1)}, bf16[256,256]{1,0:T(8,128)(2,1)}, u32[]{:S(2)}, u32[]{:S(2)}) collective-permute-start(bf16[256,256]{1,0:T(8,128)(2,1)S(1)} %pad_maximum_fusion.7.rows_ref), channel_id=1, source_target_pairs={{0,128},{2,130},{4,132},{6,134},{8,136},{10,138},{12,140},{14,142}... | collective-permute-start | bytes 393224 | tf_op jit(solution)/shard_map/ppermute | solution.py:17
  35.7 4.3 %collective-permute-done.12.rows_ref = bf16[256,256]{1,0:T(8,128)(2,1)} collective-permute-done((bf16[256,256]{1,0:T(8,128)(2,1)S(1)}, bf16[256,256]{1,0:T(8,128)(2,1)}, u32[]{:S(2)}, u32[]{:S(2)}) %collective-permute-start.12) | collective-permute-done | bytes 131104 | tf_op jit(solution)/shard_map/ppermute | solution.py:17
  40.0 1.6 %collective-permute-start.10 = (bf16[256,256]{1,0:T(8,128)(2,1)S(1)}, bf16[256,256]{1,0:T(8,128)(2,1)S(1)}, u32[]{:S(2)}, u32[]{:S(2)}) collective-permute-start(bf16[256,256]{1,0:T(8,128)(2,1)S(1)} %pad_maximum_fusion.7.rows_ref), channel_id=1, source_target_pairs={{0,64},{2,66},{4,68},{6,70},{8,72},{10,74},{12,76},{14,78},{16,80}... | collective-permute-start | bytes 393224 | tf_op jit(solution)/shard_map/ppermute | solution.py:17
  41.6 3.6 %collective-permute-done.10.rows_ref = bf16[256,256]{1,0:T(8,128)(2,1)S(1)} collective-permute-done((bf16[256,256]{1,0:T(8,128)(2,1)S(1)}, bf16[256,256]{1,0:T(8,128)(2,1)S(1)}, u32[]{:S(2)}, u32[]{:S(2)}) %collective-permute-start.10) | collective-permute-done | bytes 131104 | tf_op jit(solution)/shard_map/ppermute | solution.py:17
  45.1 0.7 copy-done.1
  45.8 3.0 %collective-permute-start.14 = (bf16[256,256]{1,0:T(8,128)(2,1)S(1)}, bf16[256,256]{1,0:T(8,128)(2,1)}, u32[]{:S(2)}, u32[]{:S(2)}) collective-permute-start(bf16[256,256]{1,0:T(8,128)(2,1)S(1)} %pad_maximum_fusion.7.rows_ref), channel_id=1, source_target_pairs={{0,192},{2,194},{4,196},{6,198},{8,200},{10,202},{12,204},{14,206}... | collective-permute-start | bytes 393224 | tf_op jit(solution)/shard_map/ppermute | solution.py:17
  48.8 0.9 slice.67
  49.7 2.4 %collective-permute-done.14.rows_ref = bf16[256,256]{1,0:T(8,128)(2,1)} collective-permute-done((bf16[256,256]{1,0:T(8,128)(2,1)S(1)}, bf16[256,256]{1,0:T(8,128)(2,1)}, u32[]{:S(2)}, u32[]{:S(2)}) %collective-permute-start.14) | collective-permute-done | bytes 131104 | tf_op jit(solution)/shard_map/ppermute | solution.py:17
  52.1 0.8 slice.68
  53.0 6.4 %collective-permute-start.16 = (bf16[1024,128]{1,0:T(8,128)(2,1)S(1)}, bf16[1024,128]{1,0:T(8,128)(2,1)S(1)}, u32[]{:S(2)}, u32[]{:S(2)}) collective-permute-start(bf16[1024,128]{1,0:T(8,128)(2,1)S(1)} %pad_maximum_fusion.1), channel_id=1, source_target_pairs={{0,1},{1,0},{2,3},{3,2},{4,5},{5,4},{6,7},{7,6},{8,9},{9,8},{10,11... | collective-permute-start | bytes 786440 | tf_op jit(solution)/shard_map/ppermute | solution.py:21
  59.4 4.5 %cross_block.7 = (f32[256,128]{1,0:T(8,128)}, bf16[256,128]{1,0:T(8,128)(2,1)S(1)}) custom-call(f32[1,128]{1,0:T(1,128)S(1)} %bitcast.8, bf16[256,256]{1,0:T(8,128)(2,1)} %collective-permute-done.14.rows_ref, bf16[1040,256]{1,0:T(8,128)(2,1)S(1)} %pad_maximum_fusion.refs_0_, bf16[1040,256]{1,0:T(8,128)(2,1)S(1)} %collective-permute-done.3.refs_1_, ...), custom_call_target="tpu_custom_call" | custom-call | flops 1073741824 | bytes 5242880 | tf_op jit(solution)/shard_map/cross_block/pallas_call | solution.py:46
  63.9 3.0 %collective-permute-start.15 = (bf16[256,128]{1,0:T(8,128)(2,1)S(1)}, bf16[256,128]{1,0:T(8,128)(2,1)S(1)}, u32[]{:S(2)}, u32[]{:S(2)}) collective-permute-start(bf16[256,128]{1,0:T(8,128)(2,1)S(1)} %get-tuple-element.10), channel_id=1, source_target_pairs={{0,192},{2,194},{4,196},{6,198},{8,200},{10,202},{12,204},{14,206}... | collective-permute-start | bytes 196616 | tf_op jit(solution)/shard_map/ppermute | solution.py:17
  66.9 4.5 %cross_block.6 = (f32[256,128]{1,0:T(8,128)}, bf16[256,128]{1,0:T(8,128)(2,1)S(1)}) custom-call(f32[1,128]{1,0:T(1,128)S(1)} %bitcast.9, bf16[256,256]{1,0:T(8,128)(2,1)} %collective-permute-done.12.rows_ref, bf16[1040,256]{1,0:T(8,128)(2,1)S(1)} %pad_maximum_fusion.refs_0_, bf16[1040,256]{1,0:T(8,128)(2,1)S(1)} %collective-permute-done.3.refs_1_, ...), custom_call_target="tpu_custom_call" | custom-call | flops 1073741824 | bytes 5242880 | tf_op jit(solution)/shard_map/cross_block/pallas_call | solution.py:46
  71.4 4.5 %cross_block.5 = (f32[256,128]{1,0:T(8,128)}, bf16[256,128]{1,0:T(8,128)(2,1)S(1)}) custom-call(f32[1,128]{1,0:T(1,128)S(1)} %bitcast.10, bf16[256,256]{1,0:T(8,128)(2,1)S(1)} %copy-done.2, bf16[1040,256]{1,0:T(8,128)(2,1)S(1)} %pad_maximum_fusion.refs_0_, bf16[1040,256]{1,0:T(8,128)(2,1)S(1)} %collective-permute-done.3.refs_1_, ...), custom_call_target="tpu_custom_call" | custom-call | flops 1073741824 | bytes 5242880 | tf_op jit(solution)/shard_map/cross_block/pallas_call | solution.py:46
  75.9 1.1 collective-permute-start.11
  77.0 3.8 %cross_block.4 = (f32[256,128]{1,0:T(8,128)S(1)}, bf16[256,128]{1,0:T(8,128)(2,1)S(1)}) custom-call(f32[1,128]{1,0:T(1,128)S(1)} %bitcast.11, bf16[256,256]{1,0:T(8,128)(2,1)S(1)} %pad_maximum_fusion.7.rows_ref, bf16[1040,256]{1,0:T(8,128)(2,1)S(1)} %pad_maximum_fusion.refs_0_, bf16[1040,256]{1,0:T(8,128)(2,1)S(1)} %collective-permute-done.3.refs_1_, ...), custom_call_target="tpu_custom_call" | custom-call | flops 1073741824 | bytes 5242880 | tf_op jit(solution)/shard_map/cross_block/pallas_call | solution.py:46
  82.0 0.9 collective-permute-done.17
  83.1 1.1 collective-permute-start.18
  84.2 1.5 %collective-permute-start.19 = (f32[64,384]{0,1:T(8,128)S(1)}, f32[64,384]{0,1:T(8,128)S(1)}, u32[]{:S(2)}, u32[]{:S(2)}) collective-permute-start(f32[64,384]{0,1:T(8,128)S(1)} %get-tuple-element.20), channel_id=1, source_target_pairs={{0,32},{2,34},{4,36},{6,38},{8,40},{10,42},{12,44},{14,46},{16,48}... | collective-permute-start | bytes 294920 | tf_op jit(solution)/shard_map/ppermute | solution.py:17
  85.7 1.0 collective-permute-start.20
  86.8 5.2 %collective-permute-done.18 = f32[64,384]{0,1:T(8,128)S(1)} collective-permute-done((f32[64,384]{0,1:T(8,128)S(1)}, f32[64,384]{0,1:T(8,128)S(1)}, u32[]{:S(2)}, u32[]{:S(2)}) %collective-permute-start.18) | collective-permute-done | bytes 98336 | tf_op jit(solution)/shard_map/ppermute | solution.py:17
  92.0 7.4 %collective-permute-done.19 = f32[64,384]{0,1:T(8,128)S(1)} collective-permute-done((f32[64,384]{0,1:T(8,128)S(1)}, f32[64,384]{0,1:T(8,128)S(1)}, u32[]{:S(2)}, u32[]{:S(2)}) %collective-permute-start.19) | collective-permute-done | bytes 98336 | tf_op jit(solution)/shard_map/ppermute | solution.py:17
  99.4 4.6 %collective-permute-done.20 = f32[64,384]{0,1:T(8,128)S(1)} collective-permute-done((f32[64,384]{0,1:T(8,128)S(1)}, f32[64,384]{0,1:T(8,128)S(1)}, u32[]{:S(2)}, u32[]{:S(2)}) %collective-permute-start.20) | collective-permute-done | bytes 98336 | tf_op jit(solution)/shard_map/ppermute | solution.py:17
  104.1 1.3 collective-permute-start.22
  105.3 3.5 %collective-permute-start.23 = (f32[64,256]{0,1:T(8,128)S(1)}, f32[64,256]{0,1:T(8,128)S(1)}, u32[]{:S(2)}, u32[]{:S(2)}) collective-permute-start(f32[64,256]{0,1:T(8,128)S(1)} %slice.77), channel_id=1, source_target_pairs={{0,128},{2,130},{4,132},{6,134},{8,136},{10,138},{12,140},{14,142}... | collective-permute-start | bytes 196616 | tf_op jit(solution)/shard_map/ppermute | solution.py:17
  109.4 1.4 %collective-permute-done.22 = f32[64,256]{0,1:T(8,128)S(1)} collective-permute-done((f32[64,256]{0,1:T(8,128)S(1)}, f32[64,256]{0,1:T(8,128)S(1)}, u32[]{:S(2)}, u32[]{:S(2)}) %collective-permute-start.22) | collective-permute-done | bytes 65568 | tf_op jit(solution)/shard_map/ppermute | solution.py:17
  110.7 3.4 %collective-permute-done.23 = f32[64,256]{0,1:T(8,128)S(1)} collective-permute-done((f32[64,256]{0,1:T(8,128)S(1)}, f32[64,256]{0,1:T(8,128)S(1)}, u32[]{:S(2)}, u32[]{:S(2)}) %collective-permute-start.23) | collective-permute-done | bytes 65568 | tf_op jit(solution)/shard_map/ppermute | solution.py:17
  114.2 1.6 %collective-permute-done.24 = f32[64,256]{0,1:T(8,128)S(1)} collective-permute-done((f32[64,256]{0,1:T(8,128)S(1)}, f32[64,256]{0,1:T(8,128)S(1)}, u32[]{:S(2)}, u32[]{:S(2)}) %collective-permute-start.24) | collective-permute-done | bytes 65568 | tf_op jit(solution)/shard_map/ppermute | solution.py:17
  116.0 1.9 %collective-permute-start.26 = (f32[64,256]{0,1:T(8,128)S(1)}, f32[64,256]{0,1:T(8,128)S(1)}, u32[]{:S(2)}, u32[]{:S(2)}) collective-permute-start(f32[64,256]{0,1:T(8,128)S(1)} %add_add_fusion.1), channel_id=1, source_target_pairs={{0,8},{2,10},{4,12},{6,14},{8,0},{10,2},{12,4},{14,6},{16,24},{18,... | collective-permute-start | bytes 196616 | tf_op jit(solution)/shard_map/ppermute | solution.py:17
  117.9 2.8 %collective-permute-start.27 = (f32[64,256]{0,1:T(8,128)S(1)}, f32[64,256]{0,1:T(8,128)S(1)}, u32[]{:S(2)}, u32[]{:S(2)}) collective-permute-start(f32[64,256]{0,1:T(8,128)S(1)} %add_add_fusion.1), channel_id=1, source_target_pairs={{0,12},{2,14},{4,8},{6,10},{8,4},{10,6},{12,0},{14,2},{16,28},{18,... | collective-permute-start | bytes 196616 | tf_op jit(solution)/shard_map/ppermute | solution.py:17
  120.7 0.6 collective-permute-start.21
  121.7 1.7 %collective-permute-done.26 = f32[64,256]{0,1:T(8,128)S(1)} collective-permute-done((f32[64,256]{0,1:T(8,128)S(1)}, f32[64,256]{0,1:T(8,128)S(1)}, u32[]{:S(2)}, u32[]{:S(2)}) %collective-permute-start.26) | collective-permute-done | bytes 65568 | tf_op jit(solution)/shard_map/ppermute | solution.py:17
  123.4 1.6 %collective-permute-done.27 = f32[64,256]{0,1:T(8,128)S(1)} collective-permute-done((f32[64,256]{0,1:T(8,128)S(1)}, f32[64,256]{0,1:T(8,128)S(1)}, u32[]{:S(2)}, u32[]{:S(2)}) %collective-permute-start.27) | collective-permute-done | bytes 65568 | tf_op jit(solution)/shard_map/ppermute | solution.py:17
  125.2 3.3 %collective-permute-done.21 = f32[64,128]{1,0:T(8,128)S(1)} collective-permute-done((f32[64,128]{1,0:T(8,128)S(1)}, f32[64,128]{1,0:T(8,128)S(1)}, u32[]{:S(2)}, u32[]{:S(2)}) %collective-permute-start.21) | collective-permute-done | bytes 32800 | tf_op jit(solution)/shard_map/ppermute | solution.py:21
  128.5 0.6 add_convert_fusion
  129.2 0.8 copy.12
  (70 shorter events, 3.1 us)
Async XLA Ops:
  0.6 108.5 %copy-start = (f32[128,256]{1,0:T(8,128)S(1)}, f32[128,256]{1,0:T(8,128)}, u32[]{:S(2)}) copy-start(f32[128,256]{1,0:T(8,128)} %param.10) | copy-start | bytes 393220
  0.6 1.4 %copy-start.4 = (bf16[1024,128]{1,0:T(8,128)(2,1)S(1)}, bf16[1024,128]{1,0:T(8,128)(2,1)}, u32[]{:S(2)}) copy-start(bf16[1024,128]{1,0:T(8,128)(2,1)} %param.9) | copy-start | bytes 786436
  2.1 4.9 %copy-start.5 = (bf16[64,128]{1,0:T(8,128)(2,1)S(1)}, bf16[64,128]{1,0:T(8,128)(2,1)}, u32[]{:S(2)}) copy-start(bf16[64,128]{1,0:T(8,128)(2,1)} %param.6) | copy-start | bytes 49156
  2.1 4.9 %copy-start.6 = (bf16[64,128]{1,0:T(8,128)(2,1)S(1)}, bf16[64,128]{1,0:T(8,128)(2,1)}, u32[]{:S(2)}) copy-start(bf16[64,128]{1,0:T(8,128)(2,1)} %param.11) | copy-start | bytes 49156
  2.2 15.1 %collective-permute-start.3 = (bf16[1040,256]{1,0:T(8,128)(2,1)S(1)}, bf16[1040,256]{1,0:T(8,128)(2,1)S(1)}, u32[]{:S(2)}, u32[]{:S(2)}) collective-permute-start(bf16[1040,256]{1,0:T(8,128)(2,1)S(1)} %pad_maximum_fusion.refs_0_), channel_id=1, source_target_pairs={{0,4},{2,6},{4,0},{6,2},{8,12},{10,14},{12,8},{14,10},{16,20},{18,... | collective-permute-start | bytes 1597448 | tf_op jit(solution)/shard_map/ppermute | solution.py:17
  3.8 26.1 %collective-permute-start.4 = (bf16[1040,256]{1,0:T(8,128)(2,1)S(1)}, bf16[1040,256]{1,0:T(8,128)(2,1)S(1)}, u32[]{:S(2)}, u32[]{:S(2)}) collective-permute-start(bf16[1040,256]{1,0:T(8,128)(2,1)S(1)} %pad_maximum_fusion.refs_0_), channel_id=1, source_target_pairs={{0,8},{2,10},{4,12},{6,14},{8,0},{10,2},{12,4},{14,6},{16,24},{18,... | collective-permute-start | bytes 1597448 | tf_op jit(solution)/shard_map/ppermute | solution.py:17
  6.5 25.9 %collective-permute-start.5 = (bf16[1040,256]{1,0:T(8,128)(2,1)S(1)}, bf16[1040,256]{1,0:T(8,128)(2,1)S(1)}, u32[]{:S(2)}, u32[]{:S(2)}) collective-permute-start(bf16[1040,256]{1,0:T(8,128)(2,1)S(1)} %pad_maximum_fusion.refs_0_), channel_id=1, source_target_pairs={{0,12},{2,14},{4,8},{6,10},{8,4},{10,6},{12,0},{14,2},{16,28},{18,... | collective-permute-start | bytes 1597448 | tf_op jit(solution)/shard_map/ppermute | solution.py:17
  7.0 4.0 %collective-permute-start = (bf16[64,256]{1,0:T(8,128)(2,1)S(1)}, bf16[64,256]{1,0:T(8,128)(2,1)S(1)}, u32[]{:S(2)}, u32[]{:S(2)}) collective-permute-start(bf16[64,256]{1,0:T(8,128)(2,1)S(1)} %constant_dynamic-update-slice_fusion), channel_id=1, source_target_pairs={{0,16},{2,18},{4,20},{6,22},{8,24},{10,26},{12,28},{14,30},{16,0},... | collective-permute-start | bytes 98312 | tf_op jit(solution)/shard_map/ppermute | solution.py:17
  8.9 4.8 %collective-permute-start.1 = (bf16[64,256]{1,0:T(8,128)(2,1)S(1)}, bf16[64,256]{1,0:T(8,128)(2,1)S(1)}, u32[]{:S(2)}, u32[]{:S(2)}) collective-permute-start(bf16[64,256]{1,0:T(8,128)(2,1)S(1)} %constant_dynamic-update-slice_fusion), channel_id=1, source_target_pairs={{0,32},{2,34},{4,36},{6,38},{8,40},{10,42},{12,44},{14,46},{16,48}... | collective-permute-start | bytes 98312 | tf_op jit(solution)/shard_map/ppermute | solution.py:17
  11.0 21.4 %collective-permute-start.2 = (bf16[64,256]{1,0:T(8,128)(2,1)S(1)}, bf16[64,256]{1,0:T(8,128)(2,1)S(1)}, u32[]{:S(2)}, u32[]{:S(2)}) collective-permute-start(bf16[64,256]{1,0:T(8,128)(2,1)S(1)} %constant_dynamic-update-slice_fusion), channel_id=1, source_target_pairs={{0,48},{2,50},{4,52},{6,54},{8,56},{10,58},{12,60},{14,62},{16,32}... | collective-permute-start | bytes 98312 | tf_op jit(solution)/shard_map/ppermute | solution.py:17
  13.7 45.6 %collective-permute-start.6 = (bf16[1040,256]{1,0:T(8,128)(2,1)S(1)}, bf16[1040,256]{1,0:T(8,128)(2,1)S(1)}, u32[]{:S(2)}, u32[]{:S(2)}) collective-permute-start(bf16[1040,256]{1,0:T(8,128)(2,1)S(1)} %pad_maximum_fusion.refs_0_), channel_id=1, source_target_pairs={{0,2},{2,0},{4,6},{6,4},{8,10},{10,8},{12,14},{14,12},{16,18},{18,... | collective-permute-start | bytes 1597448 | tf_op jit(solution)/shard_map/ppermute | solution.py:17
  17.2 42.1 %collective-permute-start.7 = (bf16[1040,256]{1,0:T(8,128)(2,1)S(1)}, bf16[1040,256]{1,0:T(8,128)(2,1)S(1)}, u32[]{:S(2)}, u32[]{:S(2)}) collective-permute-start(bf16[1040,256]{1,0:T(8,128)(2,1)S(1)} %collective-permute-done.3.refs_1_), channel_id=1, source_target_pairs={{0,2},{2,0},{4,6},{6,4},{8,10},{10,8},{12,14},{14,12},{16,18},{18,... | collective-permute-start | bytes 1597448 | tf_op jit(solution)/shard_map/ppermute | solution.py:17
  29.8 29.5 %collective-permute-start.8 = (bf16[1040,256]{1,0:T(8,128)(2,1)S(1)}, bf16[1040,256]{1,0:T(8,128)(2,1)}, u32[]{:S(2)}, u32[]{:S(2)}) collective-permute-start(bf16[1040,256]{1,0:T(8,128)(2,1)S(1)} %collective-permute-done.4.refs_2_), channel_id=1, source_target_pairs={{0,2},{2,0},{4,6},{6,4},{8,10},{10,8},{12,14},{14,12},{16,18},{18,... | collective-permute-start | bytes 1597448 | tf_op jit(solution)/shard_map/ppermute | solution.py:17
  32.4 27.0 %collective-permute-start.9 = (bf16[1040,256]{1,0:T(8,128)(2,1)S(1)}, bf16[1040,256]{1,0:T(8,128)(2,1)}, u32[]{:S(2)}, u32[]{:S(2)}) collective-permute-start(bf16[1040,256]{1,0:T(8,128)(2,1)S(1)} %collective-permute-done.5.refs_3_), channel_id=1, source_target_pairs={{0,2},{2,0},{4,6},{6,4},{8,10},{10,8},{12,14},{14,12},{16,18},{18,... | collective-permute-start | bytes 1597448 | tf_op jit(solution)/shard_map/ppermute | solution.py:17
  32.4 7.6 %collective-permute-start.12 = (bf16[256,256]{1,0:T(8,128)(2,1)S(1)}, bf16[256,256]{1,0:T(8,128)(2,1)}, u32[]{:S(2)}, u32[]{:S(2)}) collective-permute-start(bf16[256,256]{1,0:T(8,128)(2,1)S(1)} %pad_maximum_fusion.7.rows_ref), channel_id=1, source_target_pairs={{0,128},{2,130},{4,132},{6,134},{8,136},{10,138},{12,140},{14,142}... | collective-permute-start | bytes 393224 | tf_op jit(solution)/shard_map/ppermute | solution.py:17
  40.0 5.1 %collective-permute-start.10 = (bf16[256,256]{1,0:T(8,128)(2,1)S(1)}, bf16[256,256]{1,0:T(8,128)(2,1)S(1)}, u32[]{:S(2)}, u32[]{:S(2)}) collective-permute-start(bf16[256,256]{1,0:T(8,128)(2,1)S(1)} %pad_maximum_fusion.7.rows_ref), channel_id=1, source_target_pairs={{0,64},{2,66},{4,68},{6,70},{8,72},{10,74},{12,76},{14,78},{16,80}... | collective-permute-start | bytes 393224 | tf_op jit(solution)/shard_map/ppermute | solution.py:17
  45.1 0.7 copy-start.1
  45.8 6.3 %collective-permute-start.14 = (bf16[256,256]{1,0:T(8,128)(2,1)S(1)}, bf16[256,256]{1,0:T(8,128)(2,1)}, u32[]{:S(2)}, u32[]{:S(2)}) collective-permute-start(bf16[256,256]{1,0:T(8,128)(2,1)S(1)} %pad_maximum_fusion.7.rows_ref), channel_id=1, source_target_pairs={{0,192},{2,194},{4,196},{6,198},{8,200},{10,202},{12,204},{14,206}... | collective-permute-start | bytes 393224 | tf_op jit(solution)/shard_map/ppermute | solution.py:17
  48.8 4.1 %slice-start = ((bf16[256,256]{1,0:T(8,128)(2,1)}), bf16[256,128]{1,0:T(8,128)(2,1)S(1)}, s32[]{:S(2)}) async-start(bf16[256,256]{1,0:T(8,128)(2,1)} %copy-done.1), calls=%async_computation | async-start | bytes 131072 | tf_op jit(solution)/shard_map/slice | solution.py:84
  48.8 10.5 %copy-start.3 = (f32[128]{0:T(128)S(1)}, f32[128]{0:T(128)}, u32[]{:S(2)}) copy-start(f32[128]{0:T(128)} %param.8) | copy-start | bytes 1540
  53.0 28.2 %collective-permute-start.16 = (bf16[1024,128]{1,0:T(8,128)(2,1)S(1)}, bf16[1024,128]{1,0:T(8,128)(2,1)S(1)}, u32[]{:S(2)}, u32[]{:S(2)}) collective-permute-start(bf16[1024,128]{1,0:T(8,128)(2,1)S(1)} %pad_maximum_fusion.1), channel_id=1, source_target_pairs={{0,1},{1,0},{2,3},{3,2},{4,5},{5,4},{6,7},{7,6},{8,9},{9,8},{10,11... | collective-permute-start | bytes 786440 | tf_op jit(solution)/shard_map/ppermute | solution.py:21
  63.9 7.5 %copy-start.2 = (bf16[256,256]{1,0:T(8,128)(2,1)S(1)}, bf16[256,256]{1,0:T(8,128)(2,1)}, u32[]{:S(2)}) copy-start(bf16[256,256]{1,0:T(8,128)(2,1)} %copy-done.1) | copy-start | bytes 393220
  63.9 17.7 %collective-permute-start.15 = (bf16[256,128]{1,0:T(8,128)(2,1)S(1)}, bf16[256,128]{1,0:T(8,128)(2,1)S(1)}, u32[]{:S(2)}, u32[]{:S(2)}) collective-permute-start(bf16[256,128]{1,0:T(8,128)(2,1)S(1)} %get-tuple-element.10), channel_id=1, source_target_pairs={{0,192},{2,194},{4,196},{6,198},{8,200},{10,202},{12,204},{14,206}... | collective-permute-start | bytes 196616 | tf_op jit(solution)/shard_map/ppermute | solution.py:17
  71.4 10.2 %collective-permute-start.13 = (bf16[256,128]{1,0:T(8,128)(2,1)S(1)}, bf16[256,128]{1,0:T(8,128)(2,1)S(1)}, u32[]{:S(2)}, u32[]{:S(2)}) collective-permute-start(bf16[256,128]{1,0:T(8,128)(2,1)S(1)} %get-tuple-element.9), channel_id=1, source_target_pairs={{0,128},{2,130},{4,132},{6,134},{8,136},{10,138},{12,140},{14,142}... | collective-permute-start | bytes 196616 | tf_op jit(solution)/shard_map/ppermute | solution.py:17
  75.9 5.8 %collective-permute-start.11 = (bf16[256,128]{1,0:T(8,128)(2,1)S(1)}, bf16[256,128]{1,0:T(8,128)(2,1)S(1)}, u32[]{:S(2)}, u32[]{:S(2)}) collective-permute-start(bf16[256,128]{1,0:T(8,128)(2,1)S(1)} %get-tuple-element.8), channel_id=1, source_target_pairs={{0,64},{2,66},{4,68},{6,70},{8,72},{10,74},{12,76},{14,78},{16,80}... | collective-permute-start | bytes 196616 | tf_op jit(solution)/shard_map/ppermute | solution.py:17
  81.5 1.4 %collective-permute-start.17 = (f32[64,256]{0,1:T(8,128)S(1)}, f32[64,256]{0,1:T(8,128)S(1)}, u32[]{:S(2)}, u32[]{:S(2)}) collective-permute-start(f32[64,256]{0,1:T(8,128)S(1)} %fusion.6), channel_id=1, source_target_pairs={{0,2},{2,0},{4,6},{6,4},{8,10},{10,8},{12,14},{14,12},{16,18},{18,... | collective-permute-start | bytes 196616 | tf_op jit(solution)/shard_map/ppermute | solution.py:17
  83.1 8.9 %collective-permute-start.18 = (f32[64,384]{0,1:T(8,128)S(1)}, f32[64,384]{0,1:T(8,128)S(1)}, u32[]{:S(2)}, u32[]{:S(2)}) collective-permute-start(f32[64,384]{0,1:T(8,128)S(1)} %get-tuple-element.19), channel_id=1, source_target_pairs={{0,16},{2,18},{4,20},{6,22},{8,24},{10,26},{12,28},{14,30},{16,0},... | collective-permute-start | bytes 294920 | tf_op jit(solution)/shard_map/ppermute | solution.py:17
  84.2 15.2 %collective-permute-start.19 = (f32[64,384]{0,1:T(8,128)S(1)}, f32[64,384]{0,1:T(8,128)S(1)}, u32[]{:S(2)}, u32[]{:S(2)}) collective-permute-start(f32[64,384]{0,1:T(8,128)S(1)} %get-tuple-element.20), channel_id=1, source_target_pairs={{0,32},{2,34},{4,36},{6,38},{8,40},{10,42},{12,44},{14,46},{16,48}... | collective-permute-start | bytes 294920 | tf_op jit(solution)/shard_map/ppermute | solution.py:17
  85.7 18.3 %collective-permute-start.20 = (f32[64,384]{0,1:T(8,128)S(1)}, f32[64,384]{0,1:T(8,128)S(1)}, u32[]{:S(2)}, u32[]{:S(2)}) collective-permute-start(f32[64,384]{0,1:T(8,128)S(1)} %get-tuple-element.18), channel_id=1, source_target_pairs={{0,48},{2,50},{4,52},{6,54},{8,56},{10,58},{12,60},{14,62},{16,32}... | collective-permute-start | bytes 294920 | tf_op jit(solution)/shard_map/ppermute | solution.py:17
  104.1 6.7 %collective-permute-start.22 = (f32[64,256]{0,1:T(8,128)S(1)}, f32[64,256]{0,1:T(8,128)S(1)}, u32[]{:S(2)}, u32[]{:S(2)}) collective-permute-start(f32[64,256]{0,1:T(8,128)S(1)} %slice.77), channel_id=1, source_target_pairs={{0,64},{2,66},{4,68},{6,70},{8,72},{10,74},{12,76},{14,78},{16,80}... | collective-permute-start | bytes 196616 | tf_op jit(solution)/shard_map/ppermute | solution.py:17
  105.3 8.9 %collective-permute-start.23 = (f32[64,256]{0,1:T(8,128)S(1)}, f32[64,256]{0,1:T(8,128)S(1)}, u32[]{:S(2)}, u32[]{:S(2)}) collective-permute-start(f32[64,256]{0,1:T(8,128)S(1)} %slice.77), channel_id=1, source_target_pairs={{0,128},{2,130},{4,132},{6,134},{8,136},{10,138},{12,140},{14,142}... | collective-permute-start | bytes 196616 | tf_op jit(solution)/shard_map/ppermute | solution.py:17
  108.9 7.0 %collective-permute-start.24 = (f32[64,256]{0,1:T(8,128)S(1)}, f32[64,256]{0,1:T(8,128)S(1)}, u32[]{:S(2)}, u32[]{:S(2)}) collective-permute-start(f32[64,256]{0,1:T(8,128)S(1)} %slice.77), channel_id=1, source_target_pairs={{0,192},{2,194},{4,196},{6,198},{8,200},{10,202},{12,204},{14,206}... | collective-permute-start | bytes 196616 | tf_op jit(solution)/shard_map/ppermute | solution.py:17
  115.9 5.8 %collective-permute-start.25 = (f32[64,256]{0,1:T(8,128)S(1)}, f32[64,256]{0,1:T(8,128)S(1)}, u32[]{:S(2)}, u32[]{:S(2)}) collective-permute-start(f32[64,256]{0,1:T(8,128)S(1)} %add_add_fusion.1), channel_id=1, source_target_pairs={{0,4},{2,6},{4,0},{6,2},{8,12},{10,14},{12,8},{14,10},{16,20},{18,... | collective-permute-start | bytes 196616 | tf_op jit(solution)/shard_map/ppermute | solution.py:17
  116.0 7.4 %collective-permute-start.26 = (f32[64,256]{0,1:T(8,128)S(1)}, f32[64,256]{0,1:T(8,128)S(1)}, u32[]{:S(2)}, u32[]{:S(2)}) collective-permute-start(f32[64,256]{0,1:T(8,128)S(1)} %add_add_fusion.1), channel_id=1, source_target_pairs={{0,8},{2,10},{4,12},{6,14},{8,0},{10,2},{12,4},{14,6},{16,24},{18,... | collective-permute-start | bytes 196616 | tf_op jit(solution)/shard_map/ppermute | solution.py:17
  117.9 7.1 %collective-permute-start.27 = (f32[64,256]{0,1:T(8,128)S(1)}, f32[64,256]{0,1:T(8,128)S(1)}, u32[]{:S(2)}, u32[]{:S(2)}) collective-permute-start(f32[64,256]{0,1:T(8,128)S(1)} %add_add_fusion.1), channel_id=1, source_target_pairs={{0,12},{2,14},{4,8},{6,10},{8,4},{10,6},{12,0},{14,2},{16,28},{18,... | collective-permute-start | bytes 196616 | tf_op jit(solution)/shard_map/ppermute | solution.py:17
  120.7 7.8 %collective-permute-start.21 = (f32[64,128]{1,0:T(8,128)S(1)}, f32[64,128]{1,0:T(8,128)S(1)}, u32[]{:S(2)}, u32[]{:S(2)}) collective-permute-start(f32[64,128]{1,0:T(8,128)S(1)} %slice_select_fusion), channel_id=1, source_target_pairs={{0,1},{1,0},{2,3},{3,2},{4,5},{5,4},{6,7},{7,6},{8,9},{9,8},{10,11... | collective-permute-start | bytes 98312 | tf_op jit(solution)/shard_map/ppermute | solution.py:21
  125.1 4.0 %collective-permute-start.28 = (f32[64,256]{0,1:T(8,128)S(1)}, f32[64,256]{0,1:T(8,128)S(1)}, u32[]{:S(2)}, u32[]{:S(2)}) collective-permute-start(f32[64,256]{0,1:T(8,128)S(1)} %maximum_select_fusion), channel_id=1, source_target_pairs={{0,2},{2,0},{4,6},{6,4},{8,10},{10,8},{12,14},{14,12},{16,18},{18,... | collective-permute-start | bytes 196616 | tf_op jit(solution)/shard_map/ppermute | solution.py:17

commit v2 on v1

v2 whole, which is shorter than its diff:
```python
import functools

import jax
import jax.numpy as jnp
from jax import lax
from jax.experimental import pallas as pl
from jax.experimental.pallas import tpu as pltpu
from jax.sharding import PartitionSpec as P

F32 = jnp.float32
BF16 = jnp.bfloat16
PTS = 128
HALF = 512
TILE = 256
CORE, X, Z, Y = 0, 1, 3, 5


def swap(value, place, mask):
    return lax.ppermute(value, "pts", [(i, i ^ (mask << place)) for i in range(PTS)])


def swap_ring(value, place, step):
    pairs = []
    for i in range(PTS):
        at = (i >> place) & 3
        pairs.append((i, i + ((((at - step) & 3) - at) << place)))
    return lax.ppermute(value, "pts", pairs)


def swap_lab(value):
    return lax.ppermute(value, "lab", [(0, 1), (1, 0)])


def after(value, *earlier):
    return lax.optimization_barrier((value, *earlier))[0]


def accumulate(total, rows, row_term, pack):
    for base in range(0, pack.shape[0], HALF + 16):
        terms = pack[base + HALF : base + HALF + 16, :].astype(F32)
        for j in range(HALF // TILE):
            key_term = terms[j : j + 1] + terms[4 + j : 5 + j] + terms[8 + j : 9 + j]
            tile = pl.ds(base + j * TILE, TILE)
            inner = lax.dot_general(
                rows, pack[tile, 0:128], (((1,), (1,)), ((), ())), preferred_element_type=F32
            )
            kernel = jnp.exp(inner + row_term + key_term).astype(BF16)
            total += jnp.dot(kernel, pack[tile, 128:256], preferred_element_type=F32)
    return total


def term_of(weights_ref, rows):
    wide = rows.astype(F32)
    return jnp.sum(wide * wide * weights_ref[...], axis=1, keepdims=True) * (-1.0 / 64.0)


def first_kernel(has_total, weights_ref, *refs):
    row_refs, refs = refs[:4], refs[4:]
    start, refs = (refs[0], refs[1:]) if has_total else (None, refs)
    packs, out = refs[:-1], refs[-1]
    for m, row_ref in enumerate(row_refs):
        rows = row_ref[:, 0:128]
        row_term = term_of(weights_ref, rows)
        total = start[256 * m : 256 * m + 256, :] if has_total else jnp.zeros((256, 128), F32)
        for pack in packs:
            total = accumulate(total, rows, row_term, pack)
        out[256 * m : 256 * m + 256, :] = total


def last_kernel(m, weights_ref, row_ref, start, *refs):
    packs, out = refs[:-1], refs[-1]
    rows = row_ref[:, 0:128]
    total = start[256 * m : 256 * m + 256, :]
    row_term = term_of(weights_ref, rows)
    for pack in packs:
        total = accumulate(total, rows, row_term, pack)
    out[...] = total.astype(out.dtype)


def in_vmem(kernel, out, args, keys):
    rows = out.shape[0]
    return pl.pallas_call(
        kernel,
        out_shape=out,
        in_specs=[pl.BlockSpec(memory_space=pltpu.VMEM)] * len(args),
        out_specs=pl.BlockSpec(memory_space=pltpu.VMEM),
        compiler_params=pltpu.CompilerParams(vmem_limit_bytes=16 * 2**20),
        cost_estimate=pl.CostEstimate(
            flops=4 * rows * keys * 128,
            bytes_accessed=2**20,
            transcendentals=rows * keys,
        ),
    )(*args)


def cross_first(weights, rows, total, packs):
    has_total = total is not None
    args = [weights, *rows] + ([total] if has_total else []) + list(packs)
    return in_vmem(
        functools.partial(first_kernel, has_total),
        jax.ShapeDtypeStruct((1024, 128), F32),
        args,
        sum(p.shape[0] for p in packs),
    )


def cross_last(m, weights, rows, total, packs, dtype):
    return in_vmem(
        functools.partial(last_kernel, m),
        jax.ShapeDtypeStruct((256, 128), dtype),
        [weights, rows, total, *packs],
        sum(p.shape[0] for p in packs),
    )


def grad_kernel(*refs):
    sent, rows, far, out = refs[:4], refs[4:8], refs[8], refs[9]
    turned = (((0,), (0,)), ((), ()))
    near_sum = jnp.zeros((128, 128), F32)
    far_sum = jnp.zeros((128, 128), F32)
    for m in range(4):
        left = sent[m][...].astype(BF16)
        near_sum += lax.dot_general(left, rows[m][:, 128:256], turned, preferred_element_type=F32)
        far_sum += lax.dot_general(
            left, far[256 * m : 256 * m + 256, :], turned, preferred_element_type=F32
        )
    out[:, 0:128] = near_sum
    out[:, 128:256] = far_sum


def local(slab_points, key_points, length_weights, adjoint, label_cov, cotangent):
    first_core = lax.axis_index("pts") % 2 == 0
    first_lab = lax.axis_index("lab") == 0
    weights = length_weights.reshape(1, 128)

    keys = key_points.astype(F32)
    scaled = (keys * length_weights * (1.0 / 32.0)).astype(BF16)
    key_term = jnp.sum(keys * keys * length_weights, axis=1) * (-1.0 / 64.0)
    high = lax.reduce_precision(key_term, 8, 7)
    rest = key_term - high
    middle = lax.reduce_precision(rest, 8, 7)
    both = jnp.concatenate([scaled, adjoint], axis=1)
    halves = []
    for h in (slice(0, HALF), slice(HALF, 2 * HALF)):
        blank = jnp.zeros((2, 256), F32)
        parts = [jnp.concatenate([t[h].reshape(2, 256), blank]) for t in (high, middle, rest - middle)]
        parts = jnp.concatenate([*parts, blank, blank]).astype(BF16)
        halves += [both[h], parts]
    pack = jnp.concatenate(halves, axis=0)

    right = swap_ring(pack, X, 1)
    left = swap_ring(pack, X, 3)
    own_far = swap(pack, CORE, 1)

    own = jnp.concatenate([slab_points, cotangent], axis=1)
    over_z = jnp.concatenate([own] + [swap(own, Z, m) for m in (1, 2, 3)], axis=0)
    rows = [over_z] + [swap(over_z, Y, m) for m in (1, 2, 3)]

    right, left = after(right, *rows), after(left, *rows)
    upper = swap_ring(right[:528], X, 1)
    lower = swap_ring(left[528:], X, 3)
    right_far, left_far = swap(right, CORE, 1), swap(left, CORE, 1)
    cot = jnp.concatenate([r[:, 128:] for r in rows], axis=0)
    cot_far = swap_lab(cot)

    total = cross_first(weights, rows, None, [pack, own_far, right, right_far])
    upper, lower = after(upper, total), after(lower, total)
    upper_far, lower_far = swap(upper, CORE, 1), swap(lower, CORE, 1)
    total = cross_first(weights, rows, total, [left, left_far])
    packs = [upper, lower, upper_far, lower_far]
    sent = {
        m: cross_last(m, weights, rows[m], total, packs, F32 if m == 0 else BF16)
        for m in (2, 1, 3, 0)
    }
    back = {m: swap(sent[m], Y, m).astype(F32) for m in (2, 1, 3)}
    over_y = (sent[0] + back[1]) + (back[2] + back[3])

    grad = in_vmem(
        grad_kernel,
        jax.ShapeDtypeStruct((128, 256), F32),
        [sent[m] for m in range(4)] + rows + [cot_far],
        256,
    )
    upper, lower = grad[:64], grad[64:]
    grad = jnp.where(first_core, upper, lower) + swap(
        jnp.where(first_core, lower, upper), CORE, 1
    )

    joint = [jnp.concatenate([over_y[64 * m : 64 * m + 64], grad], axis=1) for m in range(4)]
    back = [swap(joint[m], Z, m) for m in (1, 2, 3)]
    joint = (joint[0] + back[0]) + (back[1] + back[2])
    cross, grad = joint[:, :128], joint[:, 128:]

    back = [swap(grad, Y, m) for m in (1, 2, 3)]
    part = jnp.dot(cross, label_cov, precision=lax.Precision.HIGHEST, preferred_element_type=F32)
    near, far = part[:, :128], part[:, 128:]
    mixed = jnp.where(first_lab, near, far) + swap_lab(jnp.where(first_lab, far, near))

    grad = (grad + back[0]) + (back[1] + back[2])
    back = [swap(grad, X, m) for m in (1, 2, 3)]
    grad = (grad + back[0]) + (back[1] + back[2])
    grad = jnp.where(
        first_lab, grad, jnp.concatenate([grad[:, 128:], grad[:, :128]], axis=1)
    )
    other = swap(grad, CORE, 1)
    grad = jnp.where(
        first_core,
        jnp.concatenate([grad, other], axis=0),
        jnp.concatenate([other, grad], axis=0),
    )
    return mixed.astype(BF16), grad


def solution(mesh):
    placed = (P("pts", None), P("pts", None), P(), P("pts", "lab"), P("lab", None), P("pts", "lab"))
    return jax.shard_map(
        local,
        mesh=mesh,
        in_specs=placed,
        out_specs=(P("pts", "lab"), P("lab", None)),
        check_vma=False,
    )
```

time: 130 us -> 90.3 us (0.69)
  the two profiles are of different devices: /device:TPU:32 before, /device:TPU:2 now
where the time goes in v2:
time: 90.3 us; the launch traced here: 90 us
  starting transfers between devices  43.3 us (48%)
  waiting for transfers between devices  27.7 us (31%)
  Pallas kernels  12.2 us (14%)
  local copies, waits for them, and re-layouts  2.87 us (3%)
  other arithmetic  2.75 us (3%)
  between operations  1.03 us (1%)
    ppermute x25, starting transfers between devices, swap(): lax.ppermute(value, 'pts', [(i, i ^ mask << place) for i in range(PTS)])  27.9 us
    ppermute x25, waiting for transfers between devices, swap(): lax.ppermute(value, 'pts', [(i, i ^ mask << place) for i in range(PTS)])  22.7 us
    pallas_call x7, Pallas kernels, in_vmem(): pl.pallas_call(kernel, out_shape=out, in_specs=[pl.BlockSpec(memory_space...  12.2 us
    ppermute x2, starting transfers between devices, swap_lab(): return lax.ppermute(value, 'lab', [(0, 1), (1, 0)])  9.72 us
    ppermute x4, starting transfers between devices, swap_ring(): return lax.ppermute(value, 'pts', pairs)  5.69 us
    ppermute x2, waiting for transfers between devices, swap_lab(): return lax.ppermute(value, 'lab', [(0, 1), (1, 0)])  3.76 us
    unnamed x15, local copies, waits for them, and re-layouts  2.47 us
  transfers between devices with their start and end apart: 31, of which 12 were waited for; matrix products, arithmetic and copies ran while one was open for 1% of the time, Pallas kernels for 14%

profile of v2, /device:TPU:2, one launch (start us, length us, event | category | flops | bytes accessed | tf_op | source)
XLA Modules:
  0.0 90.0 jit_solution(8826100969873092921)
XLA Ops:
  0.7 1.2 %fusion.3 = (f32[1024]{0:T(1024)S(1)}, bf16[1024,128]{1,0:T(8,128)(2,1)S(1)}) fusion(bf16[1024,128]{1,0:T(8,128)(2,1)} %param.7, f32[128]{0:T(128)} %param.8), kind=kLoop, calls=%fused_computation.5 | loop fusion | flops 916480 | bytes 528896 | tf_op jit(solution)/shard_map/reduce_sum | solution.py:138
  2.1 0.3 concatenate.44.refs_4_
  2.3 2.3 %collective-permute-start.7 = (bf16[1056,256]{1,0:T(8,128)(2,1)S(1)}, bf16[1056,256]{1,0:T(8,128)(2,1)S(1)}, u32[]{:S(2)}, u32[]{:S(2)}) collective-permute-start(bf16[1056,256]{1,0:T(8,128)(2,1)S(1)} %concatenate.44.refs_4_), channel_id=1, source_target_pairs={{0,12},{2,14},{4,0},{6,2},{8,4},{10,6},{12,8},{14,10},{16,28},{18,... | collective-permute-start | bytes 1622024 | tf_op jit(solution)/shard_map/ppermute | solution.py:27
  4.7 3.0 %collective-permute-start.2 = (bf16[64,256]{1,0:T(8,128)(2,1)S(1)}, bf16[64,256]{1,0:T(8,128)(2,1)S(1)}, u32[]{:S(2)}, u32[]{:S(2)}) collective-permute-start(bf16[64,256]{1,0:T(8,128)(2,1)S(1)} %constant_dynamic-update-slice_fusion), channel_id=1, source_target_pairs={{0,48},{2,50},{4,52},{6,54},{8,56},{10,58},{12,60},{14,62},{16,32}... | collective-permute-start | bytes 98312 | tf_op jit(solution)/shard_map/ppermute | solution.py:19
  7.7 1.5 %collective-permute-start = (bf16[64,256]{1,0:T(8,128)(2,1)S(1)}, bf16[64,256]{1,0:T(8,128)(2,1)S(1)}, u32[]{:S(2)}, u32[]{:S(2)}) collective-permute-start(bf16[64,256]{1,0:T(8,128)(2,1)S(1)} %constant_dynamic-update-slice_fusion), channel_id=1, source_target_pairs={{0,16},{2,18},{4,20},{6,22},{8,24},{10,26},{12,28},{14,30},{16,0},... | collective-permute-start | bytes 98312 | tf_op jit(solution)/shard_map/ppermute | solution.py:19
  9.2 0.7 collective-permute-start.9
  9.8 0.7 collective-permute-done.2
  10.5 2.0 %collective-permute-done.1 = bf16[64,256]{1,0:T(8,128)(2,1)S(1)} collective-permute-done((bf16[64,256]{1,0:T(8,128)(2,1)S(1)}, bf16[64,256]{1,0:T(8,128)(2,1)S(1)}, u32[]{:S(2)}, u32[]{:S(2)}) %collective-permute-start.1) | collective-permute-done | bytes 32800 | tf_op jit(solution)/shard_map/ppermute | solution.py:19
  12.5 1.7 %collective-permute-start.3 = (bf16[256,256]{1,0:T(8,128)(2,1)S(1)}, bf16[256,256]{1,0:T(8,128)(2,1)S(1)}, u32[]{:S(2)}, u32[]{:S(2)}) collective-permute-start(bf16[256,256]{1,0:T(8,128)(2,1)S(1)} %pad_maximum_fusion.2.refs_0_.row_ref.refs_4_), channel_id=1, source_target_pairs={{0,64},{2,66},{4,68},{6,70},{8,72},{10,74},{12,76},{14,78},{16,80}... | collective-permute-start | bytes 393224 | tf_op jit(solution)/shard_map/ppermute | solution.py:19
  14.2 2.9 %collective-permute-start.4 = (bf16[256,256]{1,0:T(8,128)(2,1)S(1)}, bf16[256,256]{1,0:T(8,128)(2,1)S(1)}, u32[]{:S(2)}, u32[]{:S(2)}) collective-permute-start(bf16[256,256]{1,0:T(8,128)(2,1)S(1)} %pad_maximum_fusion.2.refs_0_.row_ref.refs_4_), channel_id=1, source_target_pairs={{0,128},{2,130},{4,132},{6,134},{8,136},{10,138},{12,140},{14,142}... | collective-permute-start | bytes 393224 | tf_op jit(solution)/shard_map/ppermute | solution.py:19
  17.3 1.6 %collective-permute-done.3.refs_1_.row_ref.refs_5_ = bf16[256,256]{1,0:T(8,128)(2,1)S(1)} collective-permute-done((bf16[256,256]{1,0:T(8,128)(2,1)S(1)}, bf16[256,256]{1,0:T(8,128)(2,1)S(1)}, u32[]{:S(2)}, u32[]{:S(2)}) %collective-permute-start.3) | collective-permute-done | bytes 131104 | tf_op jit(solution)/shard_map/ppermute | solution.py:19
  18.9 3.3 %collective-permute-done.4.refs_2_.row_ref.refs_6_ = bf16[256,256]{1,0:T(8,128)(2,1)S(1)} collective-permute-done((bf16[256,256]{1,0:T(8,128)(2,1)S(1)}, bf16[256,256]{1,0:T(8,128)(2,1)S(1)}, u32[]{:S(2)}, u32[]{:S(2)}) %collective-permute-start.4) | collective-permute-done | bytes 131104 | tf_op jit(solution)/shard_map/ppermute | solution.py:19
  22.1 1.5 %collective-permute-done.5.refs_3_.row_ref.refs_7_ = bf16[256,256]{1,0:T(8,128)(2,1)S(1)} collective-permute-done((bf16[256,256]{1,0:T(8,128)(2,1)S(1)}, bf16[256,256]{1,0:T(8,128)(2,1)S(1)}, u32[]{:S(2)}, u32[]{:S(2)}) %collective-permute-start.5) | collective-permute-done | bytes 131104 | tf_op jit(solution)/shard_map/ppermute | solution.py:19
  23.7 0.5 collective-permute-start.10
  24.2 2.4 %collective-permute-start.11 = (bf16[528,256]{1,0:T(8,128)(2,1)S(1)}, bf16[528,256]{1,0:T(8,128)(2,1)S(1)}, u32[]{:S(2)}, u32[]{:S(2)}) collective-permute-start(bf16[528,256]{1,0:T(8,128)(2,1)S(1)} %slice.98), channel_id=1, source_target_pairs={{0,12},{2,14},{4,0},{6,2},{8,4},{10,6},{12,8},{14,10},{16,28},{18,... | collective-permute-start | bytes 811016 | tf_op jit(solution)/shard_map/ppermute | solution.py:27
  27.0 0.6 copy-done.1
  27.6 5.4 %shard_map.77.refs_4_ = f32[1024,128]{1,0:T(8,128)S(1)} custom-call(f32[1,128]{1,0:T(1,128)S(1)} %bitcast.2, bf16[256,256]{1,0:T(8,128)(2,1)S(1)} %pad_maximum_fusion.2.refs_0_.row_ref.refs_4_, bf16[256,256]{1,0:T(8,128)(2,1)S(1)} %collective-permute-done.3.refs_1_.row_ref.refs_5_, bf16[256,256]{1,0:T(8,128)(2,1)S(1)} %collective-permute-done.4.refs_2_.row_ref.refs_6_, ...), custom_call_target="tpu_custom_call" | custom-call | flops 2214592512 | bytes 1048576 | tf_op jit(solution)/shard_map/pallas_call | solution.py:82
  33.0 0.8 copy-done.2
  33.8 1.3 %collective-permute-done.12.refs_1_ = bf16[528,256]{1,0:T(8,128)(2,1)S(1)} collective-permute-done((bf16[528,256]{1,0:T(8,128)(2,1)S(1)}, bf16[528,256]{1,0:T(8,128)(2,1)S(1)}, u32[]{:S(2)}, u32[]{:S(2)}) %collective-permute-start.12) | collective-permute-done | bytes 270368 | tf_op jit(solution)/shard_map/ppermute | solution.py:27
  35.1 0.5 collective-permute-start.14
  35.6 5.5 %collective-permute-start.18 = (bf16[1024,128]{1,0:T(8,128)(2,1)S(1)}, bf16[1024,128]{1,0:T(8,128)(2,1)S(1)}, u32[]{:S(2)}, u32[]{:S(2)}) collective-permute-start(bf16[1024,128]{1,0:T(8,128)(2,1)S(1)} %pad_maximum_fusion.1), channel_id=1, source_target_pairs={{0,1},{1,0},{2,3},{3,2},{4,5},{5,4},{6,7},{7,6},{8,9},{9,8},{10,11... | collective-permute-start | bytes 786440 | tf_op jit(solution)/shard_map/ppermute | solution.py:31
  41.1 1.0 %copy-done.3 = f32[1024,128]{1,0:T(8,128)S(1)} copy-done((f32[1024,128]{1,0:T(8,128)S(1)}, f32[1024,128]{1,0:T(8,128)}, u32[]{:S(2)}) %copy-start.3) | copy-done | bytes 524312
  42.2 2.6 %shard_map.78.start = f32[1024,128]{1,0:T(8,128)S(1)} custom-call(f32[1,128]{1,0:T(1,128)S(1)} %bitcast.3, bf16[256,256]{1,0:T(8,128)(2,1)S(1)} %pad_maximum_fusion.2.refs_0_.row_ref.refs_4_, bf16[256,256]{1,0:T(8,128)(2,1)S(1)} %collective-permute-done.3.refs_1_.row_ref.refs_5_, bf16[256,256]{1,0:T(8,128)(2,1)S(1)} %collective-permute-done.4.refs_2_.row_ref.refs_6_, ...), custom_call_target="tpu_custom_call" | custom-call | flops 1107296256 | bytes 1048576 | tf_op jit(solution)/shard_map/pallas_call | solution.py:82
  44.8 1.0 %shard_map.82.refs_3_ = bf16[256,128]{1,0:T(8,128)(2,1)S(1)} custom-call(f32[1,128]{1,0:T(1,128)S(1)} %bitcast.4, bf16[256,256]{1,0:T(8,128)(2,1)S(1)} %collective-permute-done.5.refs_3_.row_ref.refs_7_, f32[1024,128]{1,0:T(8,128)S(1)} %shard_map.78.start, bf16[528,256]{1,0:T(8,128)(2,1)S(1)} %collective-permute-done.11.refs_0_, ...), custom_call_target="tpu_custom_call" | custom-call | flops 276824064 | bytes 1048576 | tf_op jit(solution)/shard_map/pallas_call | solution.py:82
  45.8 3.1 %collective-permute-start.17 = (bf16[256,128]{1,0:T(8,128)(2,1)S(1)}, bf16[256,128]{1,0:T(8,128)(2,1)S(1)}, u32[]{:S(2)}, u32[]{:S(2)}) collective-permute-start(bf16[256,128]{1,0:T(8,128)(2,1)S(1)} %shard_map.82.refs_3_), channel_id=1, source_target_pairs={{0,192},{2,194},{4,196},{6,198},{8,200},{10,202},{12,204},{14,206}... | collective-permute-start | bytes 196616 | tf_op jit(solution)/shard_map/ppermute | solution.py:19
  48.9 0.9 %shard_map.81.refs_2_ = bf16[256,128]{1,0:T(8,128)(2,1)S(1)} custom-call(f32[1,128]{1,0:T(1,128)S(1)} %bitcast.5, bf16[256,256]{1,0:T(8,128)(2,1)S(1)} %collective-permute-done.4.refs_2_.row_ref.refs_6_, f32[1024,128]{1,0:T(8,128)S(1)} %shard_map.78.start, bf16[528,256]{1,0:T(8,128)(2,1)S(1)} %collective-permute-done.11.refs_0_, ...), custom_call_target="tpu_custom_call" | custom-call | flops 276824064 | bytes 1048576 | tf_op jit(solution)/shard_map/pallas_call | solution.py:82
  49.8 0.9 %collective-permute-start.16 = (bf16[256,128]{1,0:T(8,128)(2,1)S(1)}, bf16[256,128]{1,0:T(8,128)(2,1)S(1)}, u32[]{:S(2)}, u32[]{:S(2)}) collective-permute-start(bf16[256,128]{1,0:T(8,128)(2,1)S(1)} %shard_map.81.refs_2_), channel_id=1, source_target_pairs={{0,128},{2,130},{4,132},{6,134},{8,136},{10,138},{12,140},{14,142}... | collective-permute-start | bytes 196616 | tf_op jit(solution)/shard_map/ppermute | solution.py:19
  50.8 1.0 %shard_map.80.refs_1_ = bf16[256,128]{1,0:T(8,128)(2,1)S(1)} custom-call(f32[1,128]{1,0:T(1,128)S(1)} %bitcast.6, bf16[256,256]{1,0:T(8,128)(2,1)S(1)} %collective-permute-done.3.refs_1_.row_ref.refs_5_, f32[1024,128]{1,0:T(8,128)S(1)} %shard_map.78.start, bf16[528,256]{1,0:T(8,128)(2,1)S(1)} %collective-permute-done.11.refs_0_, ...), custom_call_target="tpu_custom_call" | custom-call | flops 276824064 | bytes 1048576 | tf_op jit(solution)/shard_map/pallas_call | solution.py:82
  51.7 0.5 collective-permute-start.15
  52.2 0.9 %shard_map.79.refs_0_ = f32[256,128]{1,0:T(8,128)S(1)} custom-call(f32[1,128]{1,0:T(1,128)S(1)} %bitcast.7, bf16[256,256]{1,0:T(8,128)(2,1)S(1)} %pad_maximum_fusion.2.refs_0_.row_ref.refs_4_, f32[1024,128]{1,0:T(8,128)S(1)} %shard_map.78.start, bf16[528,256]{1,0:T(8,128)(2,1)S(1)} %collective-permute-done.11.refs_0_, ...), custom_call_target="tpu_custom_call" | custom-call | flops 276824064 | bytes 1048576 | tf_op jit(solution)/shard_map/pallas_call | solution.py:82
  53.2 0.4 shard_map.83
  53.7 2.9 %collective-permute-done.16 = bf16[256,128]{1,0:T(8,128)(2,1)S(1)} collective-permute-done((bf16[256,128]{1,0:T(8,128)(2,1)S(1)}, bf16[256,128]{1,0:T(8,128)(2,1)S(1)}, u32[]{:S(2)}, u32[]{:S(2)}) %collective-permute-start.16) | collective-permute-done | bytes 65568 | tf_op jit(solution)/shard_map/ppermute | solution.py:19
  56.7 0.4 collective-permute-start.20
  57.1 2.2 %collective-permute-start.21 = (f32[64,384]{1,0:T(8,128)S(1)}, f32[64,384]{1,0:T(8,128)S(1)}, u32[]{:S(2)}, u32[]{:S(2)}) collective-permute-start(f32[64,384]{1,0:T(8,128)S(1)} %get-tuple-element.22), channel_id=1, source_target_pairs={{0,32},{2,34},{4,36},{6,38},{8,40},{10,42},{12,44},{14,46},{16,48}... | collective-permute-start | bytes 294920 | tf_op jit(solution)/shard_map/ppermute | solution.py:19
  59.3 1.9 %collective-permute-start.22 = (f32[64,384]{1,0:T(8,128)S(1)}, f32[64,384]{1,0:T(8,128)S(1)}, u32[]{:S(2)}, u32[]{:S(2)}) collective-permute-start(f32[64,384]{1,0:T(8,128)S(1)} %get-tuple-element.20), channel_id=1, source_target_pairs={{0,48},{2,50},{4,52},{6,54},{8,56},{10,58},{12,60},{14,62},{16,32}... | collective-permute-start | bytes 294920 | tf_op jit(solution)/shard_map/ppermute | solution.py:19
  61.2 0.5 collective-permute-done.20
  61.6 5.6 %collective-permute-done.21 = f32[64,384]{1,0:T(8,128)S(1)} collective-permute-done((f32[64,384]{1,0:T(8,128)S(1)}, f32[64,384]{1,0:T(8,128)S(1)}, u32[]{:S(2)}, u32[]{:S(2)}) %collective-permute-start.21) | collective-permute-done | bytes 98336 | tf_op jit(solution)/shard_map/ppermute | solution.py:19
  67.3 3.0 %collective-permute-start.25 = (f32[64,256]{1,0:T(8,128)S(1)}, f32[64,256]{1,0:T(8,128)S(1)}, u32[]{:S(2)}, u32[]{:S(2)}) collective-permute-start(f32[64,256]{1,0:T(8,128)S(1)} %slice.137), channel_id=1, source_target_pairs={{0,128},{2,130},{4,132},{6,134},{8,136},{10,138},{12,140},{14,142}... | collective-permute-start | bytes 196616 | tf_op jit(solution)/shard_map/ppermute | solution.py:19
  70.3 0.5 collective-permute-start.26
  71.1 2.3 %collective-permute-done.25 = f32[64,256]{1,0:T(8,128)S(1)} collective-permute-done((f32[64,256]{1,0:T(8,128)S(1)}, f32[64,256]{1,0:T(8,128)S(1)}, u32[]{:S(2)}, u32[]{:S(2)}) %collective-permute-start.25) | collective-permute-done | bytes 65568 | tf_op jit(solution)/shard_map/ppermute | solution.py:19
  73.4 2.4 %collective-permute-done.26 = f32[64,256]{1,0:T(8,128)S(1)} collective-permute-done((f32[64,256]{1,0:T(8,128)S(1)}, f32[64,256]{1,0:T(8,128)S(1)}, u32[]{:S(2)}, u32[]{:S(2)}) %collective-permute-start.26) | collective-permute-done | bytes 65568 | tf_op jit(solution)/shard_map/ppermute | solution.py:19
  75.8 0.5 collective-permute-start.28
  76.2 2.6 %collective-permute-start.29 = (f32[64,256]{1,0:T(8,128)S(1)}, f32[64,256]{1,0:T(8,128)S(1)}, u32[]{:S(2)}, u32[]{:S(2)}) collective-permute-start(f32[64,256]{1,0:T(8,128)S(1)} %add_add_fusion.2), channel_id=1, source_target_pairs={{0,12},{2,14},{4,8},{6,10},{8,4},{10,6},{12,0},{14,2},{16,28},{18,... | collective-permute-start | bytes 196616 | tf_op jit(solution)/shard_map/ppermute | solution.py:19
  78.9 1.7 %collective-permute-start.27 = (f32[64,256]{1,0:T(8,128)S(1)}, f32[64,256]{1,0:T(8,128)S(1)}, u32[]{:S(2)}, u32[]{:S(2)}) collective-permute-start(f32[64,256]{1,0:T(8,128)S(1)} %add_add_fusion.2), channel_id=1, source_target_pairs={{0,4},{2,6},{4,0},{6,2},{8,12},{10,14},{12,8},{14,10},{16,20},{18,... | collective-permute-start | bytes 196616 | tf_op jit(solution)/shard_map/ppermute | solution.py:19
  80.6 4.2 %collective-permute-start.23 = (f32[64,128]{1,0:T(8,128)S(1)}, f32[64,128]{1,0:T(8,128)S(1)}, u32[]{:S(2)}, u32[]{:S(2)}) collective-permute-start(f32[64,128]{1,0:T(8,128)S(1)} %slice_select_fusion.1), channel_id=1, source_target_pairs={{0,1},{1,0},{2,3},{3,2},{4,5},{5,4},{6,7},{7,6},{8,9},{9,8},{10,11... | collective-permute-start | bytes 98312 | tf_op jit(solution)/shard_map/ppermute | solution.py:31
  85.0 3.8 %collective-permute-done.23 = f32[64,128]{1,0:T(8,128)S(1)} collective-permute-done((f32[64,128]{1,0:T(8,128)S(1)}, f32[64,128]{1,0:T(8,128)S(1)}, u32[]{:S(2)}, u32[]{:S(2)}) %collective-permute-start.23) | collective-permute-done | bytes 32800 | tf_op jit(solution)/shard_map/ppermute | solution.py:31
  88.8 0.6 add_convert_fusion
  89.4 0.7 maximum_select_fusion
  (70 shorter events, 1.5 us)
Async XLA Ops:
  0.6 70.3 %copy-start = (f32[128,256]{1,0:T(8,128)S(1)}, f32[128,256]{1,0:T(8,128)}, u32[]{:S(2)}) copy-start(f32[128,256]{1,0:T(8,128)} %param.10) | copy-start | bytes 393220
  0.6 1.3 %copy-start.4 = (bf16[1024,128]{1,0:T(8,128)(2,1)S(1)}, bf16[1024,128]{1,0:T(8,128)(2,1)}, u32[]{:S(2)}) copy-start(bf16[1024,128]{1,0:T(8,128)(2,1)} %param.9) | copy-start | bytes 786436
  2.0 2.6 %copy-start.5 = (bf16[64,128]{1,0:T(8,128)(2,1)S(1)}, bf16[64,128]{1,0:T(8,128)(2,1)}, u32[]{:S(2)}) copy-start(bf16[64,128]{1,0:T(8,128)(2,1)} %param.6) | copy-start | bytes 49156
  2.3 2.4 %copy-start.6 = (bf16[64,128]{1,0:T(8,128)(2,1)S(1)}, bf16[64,128]{1,0:T(8,128)(2,1)}, u32[]{:S(2)}) copy-start(bf16[64,128]{1,0:T(8,128)(2,1)} %param.11) | copy-start | bytes 49156
  2.3 21.3 %collective-permute-start.7 = (bf16[1056,256]{1,0:T(8,128)(2,1)S(1)}, bf16[1056,256]{1,0:T(8,128)(2,1)S(1)}, u32[]{:S(2)}, u32[]{:S(2)}) collective-permute-start(bf16[1056,256]{1,0:T(8,128)(2,1)S(1)} %concatenate.44.refs_4_), channel_id=1, source_target_pairs={{0,12},{2,14},{4,0},{6,2},{8,4},{10,6},{12,8},{14,10},{16,28},{18,... | collective-permute-start | bytes 1622024 | tf_op jit(solution)/shard_map/ppermute | solution.py:27
  4.7 5.8 %collective-permute-start.2 = (bf16[64,256]{1,0:T(8,128)(2,1)S(1)}, bf16[64,256]{1,0:T(8,128)(2,1)S(1)}, u32[]{:S(2)}, u32[]{:S(2)}) collective-permute-start(bf16[64,256]{1,0:T(8,128)(2,1)S(1)} %constant_dynamic-update-slice_fusion), channel_id=1, source_target_pairs={{0,48},{2,50},{4,52},{6,54},{8,56},{10,58},{12,60},{14,62},{16,32}... | collective-permute-start | bytes 98312 | tf_op jit(solution)/shard_map/ppermute | solution.py:19
  7.7 4.8 %collective-permute-start.1 = (bf16[64,256]{1,0:T(8,128)(2,1)S(1)}, bf16[64,256]{1,0:T(8,128)(2,1)S(1)}, u32[]{:S(2)}, u32[]{:S(2)}) collective-permute-start(bf16[64,256]{1,0:T(8,128)(2,1)S(1)} %constant_dynamic-update-slice_fusion), channel_id=1, source_target_pairs={{0,32},{2,34},{4,36},{6,38},{8,40},{10,42},{12,44},{14,46},{16,48}... | collective-permute-start | bytes 98312 | tf_op jit(solution)/shard_map/ppermute | solution.py:19
  7.7 4.8 %collective-permute-start = (bf16[64,256]{1,0:T(8,128)(2,1)S(1)}, bf16[64,256]{1,0:T(8,128)(2,1)S(1)}, u32[]{:S(2)}, u32[]{:S(2)}) collective-permute-start(bf16[64,256]{1,0:T(8,128)(2,1)S(1)} %constant_dynamic-update-slice_fusion), channel_id=1, source_target_pairs={{0,16},{2,18},{4,20},{6,22},{8,24},{10,26},{12,28},{14,30},{16,0},... | collective-permute-start | bytes 98312 | tf_op jit(solution)/shard_map/ppermute | solution.py:19
  9.2 14.5 %collective-permute-start.9 = (bf16[1056,256]{1,0:T(8,128)(2,1)S(1)}, bf16[1056,256]{1,0:T(8,128)(2,1)S(1)}, u32[]{:S(2)}, u32[]{:S(2)}) collective-permute-start(bf16[1056,256]{1,0:T(8,128)(2,1)S(1)} %concatenate.44.refs_4_), channel_id=1, source_target_pairs={{0,4},{2,6},{4,8},{6,10},{8,12},{10,14},{12,0},{14,2},{16,20},{18,... | collective-permute-start | bytes 1622024 | tf_op jit(solution)/shard_map/ppermute | solution.py:27
  12.5 6.3 %collective-permute-start.3 = (bf16[256,256]{1,0:T(8,128)(2,1)S(1)}, bf16[256,256]{1,0:T(8,128)(2,1)S(1)}, u32[]{:S(2)}, u32[]{:S(2)}) collective-permute-start(bf16[256,256]{1,0:T(8,128)(2,1)S(1)} %pad_maximum_fusion.2.refs_0_.row_ref.refs_4_), channel_id=1, source_target_pairs={{0,64},{2,66},{4,68},{6,70},{8,72},{10,74},{12,76},{14,78},{16,80}... | collective-permute-start | bytes 393224 | tf_op jit(solution)/shard_map/ppermute | solution.py:19
  14.2 8.0 %collective-permute-start.4 = (bf16[256,256]{1,0:T(8,128)(2,1)S(1)}, bf16[256,256]{1,0:T(8,128)(2,1)S(1)}, u32[]{:S(2)}, u32[]{:S(2)}) collective-permute-start(bf16[256,256]{1,0:T(8,128)(2,1)S(1)} %pad_maximum_fusion.2.refs_0_.row_ref.refs_4_), channel_id=1, source_target_pairs={{0,128},{2,130},{4,132},{6,134},{8,136},{10,138},{12,140},{14,142}... | collective-permute-start | bytes 393224 | tf_op jit(solution)/shard_map/ppermute | solution.py:19
  17.1 6.6 %collective-permute-start.5 = (bf16[256,256]{1,0:T(8,128)(2,1)S(1)}, bf16[256,256]{1,0:T(8,128)(2,1)S(1)}, u32[]{:S(2)}, u32[]{:S(2)}) collective-permute-start(bf16[256,256]{1,0:T(8,128)(2,1)S(1)} %pad_maximum_fusion.2.refs_0_.row_ref.refs_4_), channel_id=1, source_target_pairs={{0,192},{2,194},{4,196},{6,198},{8,200},{10,202},{12,204},{14,206}... | collective-permute-start | bytes 393224 | tf_op jit(solution)/shard_map/ppermute | solution.py:19
  18.9 8.1 %collective-permute-start.6 = (bf16[1056,256]{1,0:T(8,128)(2,1)S(1)}, bf16[1056,256]{1,0:T(8,128)(2,1)S(1)}, u32[]{:S(2)}, u32[]{:S(2)}) collective-permute-start(bf16[1056,256]{1,0:T(8,128)(2,1)S(1)} %concatenate.44.refs_4_), channel_id=1, source_target_pairs={{0,2},{2,0},{4,6},{6,4},{8,10},{10,8},{12,14},{14,12},{16,18},{18,... | collective-permute-start | bytes 1622024 | tf_op jit(solution)/shard_map/ppermute | solution.py:19
  23.6 3.3 %collective-permute-start.8 = (bf16[1056,256]{1,0:T(8,128)(2,1)S(1)}, bf16[1056,256]{1,0:T(8,128)(2,1)S(1)}, u32[]{:S(2)}, u32[]{:S(2)}) collective-permute-start(bf16[1056,256]{1,0:T(8,128)(2,1)S(1)} %collective-permute-done.7.refs_6_), channel_id=1, source_target_pairs={{0,2},{2,0},{4,6},{6,4},{8,10},{10,8},{12,14},{14,12},{16,18},{18,... | collective-permute-start | bytes 1622024 | tf_op jit(solution)/shard_map/ppermute | solution.py:19
  23.7 17.5 %collective-permute-start.10 = (bf16[1056,256]{1,0:T(8,128)(2,1)S(1)}, bf16[1056,256]{1,0:T(8,128)(2,1)S(1)}, u32[]{:S(2)}, u32[]{:S(2)}) collective-permute-start(bf16[1056,256]{1,0:T(8,128)(2,1)S(1)} %collective-permute-done.9.refs_5_), channel_id=1, source_target_pairs={{0,2},{2,0},{4,6},{6,4},{8,10},{10,8},{12,14},{14,12},{16,18},{18,... | collective-permute-start | bytes 1622024 | tf_op jit(solution)/shard_map/ppermute | solution.py:19
  24.2 9.6 %collective-permute-start.11 = (bf16[528,256]{1,0:T(8,128)(2,1)S(1)}, bf16[528,256]{1,0:T(8,128)(2,1)S(1)}, u32[]{:S(2)}, u32[]{:S(2)}) collective-permute-start(bf16[528,256]{1,0:T(8,128)(2,1)S(1)} %slice.98), channel_id=1, source_target_pairs={{0,12},{2,14},{4,0},{6,2},{8,4},{10,6},{12,8},{14,10},{16,28},{18,... | collective-permute-start | bytes 811016 | tf_op jit(solution)/shard_map/ppermute | solution.py:27
  26.6 8.5 %collective-permute-start.12 = (bf16[528,256]{1,0:T(8,128)(2,1)S(1)}, bf16[528,256]{1,0:T(8,128)(2,1)S(1)}, u32[]{:S(2)}, u32[]{:S(2)}) collective-permute-start(bf16[528,256]{1,0:T(8,128)(2,1)S(1)} %slice.99), channel_id=1, source_target_pairs={{0,4},{2,6},{4,8},{6,10},{8,12},{10,14},{12,0},{14,2},{16,20},{18,... | collective-permute-start | bytes 811016 | tf_op jit(solution)/shard_map/ppermute | solution.py:27
  27.0 0.7 copy-start.1
  33.0 0.8 copy-start.2
  35.1 9.7 %collective-permute-start.13 = (bf16[528,256]{1,0:T(8,128)(2,1)S(1)}, bf16[528,256]{1,0:T(8,128)(2,1)S(1)}, u32[]{:S(2)}, u32[]{:S(2)}) collective-permute-start(bf16[528,256]{1,0:T(8,128)(2,1)S(1)} %collective-permute-done.11.refs_0_), channel_id=1, source_target_pairs={{0,2},{2,0},{4,6},{6,4},{8,10},{10,8},{12,14},{14,12},{16,18},{18,... | collective-permute-start | bytes 811016 | tf_op jit(solution)/shard_map/ppermute | solution.py:19
  35.1 9.7 %collective-permute-start.14 = (bf16[528,256]{1,0:T(8,128)(2,1)S(1)}, bf16[528,256]{1,0:T(8,128)(2,1)S(1)}, u32[]{:S(2)}, u32[]{:S(2)}) collective-permute-start(bf16[528,256]{1,0:T(8,128)(2,1)S(1)} %collective-permute-done.12.refs_1_), channel_id=1, source_target_pairs={{0,2},{2,0},{4,6},{6,4},{8,10},{10,8},{12,14},{14,12},{16,18},{18,... | collective-permute-start | bytes 811016 | tf_op jit(solution)/shard_map/ppermute | solution.py:19
  35.6 17.6 %collective-permute-start.18 = (bf16[1024,128]{1,0:T(8,128)(2,1)S(1)}, bf16[1024,128]{1,0:T(8,128)(2,1)S(1)}, u32[]{:S(2)}, u32[]{:S(2)}) collective-permute-start(bf16[1024,128]{1,0:T(8,128)(2,1)S(1)} %pad_maximum_fusion.1), channel_id=1, source_target_pairs={{0,1},{1,0},{2,3},{3,2},{4,5},{5,4},{6,7},{7,6},{8,9},{9,8},{10,11... | collective-permute-start | bytes 786440 | tf_op jit(solution)/shard_map/ppermute | solution.py:31
  41.1 1.0 %copy-start.3 = (f32[1024,128]{1,0:T(8,128)S(1)}, f32[1024,128]{1,0:T(8,128)}, u32[]{:S(2)}) copy-start(f32[1024,128]{1,0:T(8,128)} %copy-done.2) | copy-start | bytes 1572868
  45.8 7.9 %collective-permute-start.17 = (bf16[256,128]{1,0:T(8,128)(2,1)S(1)}, bf16[256,128]{1,0:T(8,128)(2,1)S(1)}, u32[]{:S(2)}, u32[]{:S(2)}) collective-permute-start(bf16[256,128]{1,0:T(8,128)(2,1)S(1)} %shard_map.82.refs_3_), channel_id=1, source_target_pairs={{0,192},{2,194},{4,196},{6,198},{8,200},{10,202},{12,204},{14,206}... | collective-permute-start | bytes 196616 | tf_op jit(solution)/shard_map/ppermute | solution.py:19
  49.8 6.8 %collective-permute-start.16 = (bf16[256,128]{1,0:T(8,128)(2,1)S(1)}, bf16[256,128]{1,0:T(8,128)(2,1)S(1)}, u32[]{:S(2)}, u32[]{:S(2)}) collective-permute-start(bf16[256,128]{1,0:T(8,128)(2,1)S(1)} %shard_map.81.refs_2_), channel_id=1, source_target_pairs={{0,128},{2,130},{4,132},{6,134},{8,136},{10,138},{12,140},{14,142}... | collective-permute-start | bytes 196616 | tf_op jit(solution)/shard_map/ppermute | solution.py:19
  51.7 4.9 %collective-permute-start.15 = (bf16[256,128]{1,0:T(8,128)(2,1)S(1)}, bf16[256,128]{1,0:T(8,128)(2,1)S(1)}, u32[]{:S(2)}, u32[]{:S(2)}) collective-permute-start(bf16[256,128]{1,0:T(8,128)(2,1)S(1)} %shard_map.80.refs_1_), channel_id=1, source_target_pairs={{0,64},{2,66},{4,68},{6,70},{8,72},{10,74},{12,76},{14,78},{16,80}... | collective-permute-start | bytes 196616 | tf_op jit(solution)/shard_map/ppermute | solution.py:19
  53.6 3.0 %collective-permute-start.19 = (f32[64,256]{1,0:T(8,128)S(1)}, f32[64,256]{1,0:T(8,128)S(1)}, u32[]{:S(2)}, u32[]{:S(2)}) collective-permute-start(f32[64,256]{1,0:T(8,128)S(1)} %slice_select_fusion), channel_id=1, source_target_pairs={{0,2},{2,0},{4,6},{6,4},{8,10},{10,8},{12,14},{14,12},{16,18},{18,... | collective-permute-start | bytes 196616 | tf_op jit(solution)/shard_map/ppermute | solution.py:19
  56.7 4.9 %collective-permute-start.20 = (f32[64,384]{1,0:T(8,128)S(1)}, f32[64,384]{1,0:T(8,128)S(1)}, u32[]{:S(2)}, u32[]{:S(2)}) collective-permute-start(f32[64,384]{1,0:T(8,128)S(1)} %get-tuple-element.21), channel_id=1, source_target_pairs={{0,16},{2,18},{4,20},{6,22},{8,24},{10,26},{12,28},{14,30},{16,0},... | collective-permute-start | bytes 294920 | tf_op jit(solution)/shard_map/ppermute | solution.py:19
  57.1 10.2 %collective-permute-start.21 = (f32[64,384]{1,0:T(8,128)S(1)}, f32[64,384]{1,0:T(8,128)S(1)}, u32[]{:S(2)}, u32[]{:S(2)}) collective-permute-start(f32[64,384]{1,0:T(8,128)S(1)} %get-tuple-element.22), channel_id=1, source_target_pairs={{0,32},{2,34},{4,36},{6,38},{8,40},{10,42},{12,44},{14,46},{16,48}... | collective-permute-start | bytes 294920 | tf_op jit(solution)/shard_map/ppermute | solution.py:19
  59.3 8.0 %collective-permute-start.22 = (f32[64,384]{1,0:T(8,128)S(1)}, f32[64,384]{1,0:T(8,128)S(1)}, u32[]{:S(2)}, u32[]{:S(2)}) collective-permute-start(f32[64,384]{1,0:T(8,128)S(1)} %get-tuple-element.20), channel_id=1, source_target_pairs={{0,48},{2,50},{4,52},{6,54},{8,56},{10,58},{12,60},{14,62},{16,32}... | collective-permute-start | bytes 294920 | tf_op jit(solution)/shard_map/ppermute | solution.py:19
  67.3 6.1 %collective-permute-start.25 = (f32[64,256]{1,0:T(8,128)S(1)}, f32[64,256]{1,0:T(8,128)S(1)}, u32[]{:S(2)}, u32[]{:S(2)}) collective-permute-start(f32[64,256]{1,0:T(8,128)S(1)} %slice.137), channel_id=1, source_target_pairs={{0,128},{2,130},{4,132},{6,134},{8,136},{10,138},{12,140},{14,142}... | collective-permute-start | bytes 196616 | tf_op jit(solution)/shard_map/ppermute | solution.py:19
  70.3 5.5 %collective-permute-start.26 = (f32[64,256]{1,0:T(8,128)S(1)}, f32[64,256]{1,0:T(8,128)S(1)}, u32[]{:S(2)}, u32[]{:S(2)}) collective-permute-start(f32[64,256]{1,0:T(8,128)S(1)} %slice.137), channel_id=1, source_target_pairs={{0,192},{2,194},{4,196},{6,198},{8,200},{10,202},{12,204},{14,206}... | collective-permute-start | bytes 196616 | tf_op jit(solution)/shard_map/ppermute | solution.py:19
  70.7 5.0 %collective-permute-start.24 = (f32[64,256]{1,0:T(8,128)S(1)}, f32[64,256]{1,0:T(8,128)S(1)}, u32[]{:S(2)}, u32[]{:S(2)}) collective-permute-start(f32[64,256]{1,0:T(8,128)S(1)} %slice.137), channel_id=1, source_target_pairs={{0,64},{2,66},{4,68},{6,70},{8,72},{10,74},{12,76},{14,78},{16,80}... | collective-permute-start | bytes 196616 | tf_op jit(solution)/shard_map/ppermute | solution.py:19
  75.8 9.0 %collective-permute-start.28 = (f32[64,256]{1,0:T(8,128)S(1)}, f32[64,256]{1,0:T(8,128)S(1)}, u32[]{:S(2)}, u32[]{:S(2)}) collective-permute-start(f32[64,256]{1,0:T(8,128)S(1)} %add_add_fusion.2), channel_id=1, source_target_pairs={{0,8},{2,10},{4,12},{6,14},{8,0},{10,2},{12,4},{14,6},{16,24},{18,... | collective-permute-start | bytes 196616 | tf_op jit(solution)/shard_map/ppermute | solution.py:19
  76.2 8.6 %collective-permute-start.29 = (f32[64,256]{1,0:T(8,128)S(1)}, f32[64,256]{1,0:T(8,128)S(1)}, u32[]{:S(2)}, u32[]{:S(2)}) collective-permute-start(f32[64,256]{1,0:T(8,128)S(1)} %add_add_fusion.2), channel_id=1, source_target_pairs={{0,12},{2,14},{4,8},{6,10},{8,4},{10,6},{12,0},{14,2},{16,28},{18,... | collective-permute-start | bytes 196616 | tf_op jit(solution)/shard_map/ppermute | solution.py:19
  78.9 6.0 %collective-permute-start.27 = (f32[64,256]{1,0:T(8,128)S(1)}, f32[64,256]{1,0:T(8,128)S(1)}, u32[]{:S(2)}, u32[]{:S(2)}) collective-permute-start(f32[64,256]{1,0:T(8,128)S(1)} %add_add_fusion.2), channel_id=1, source_target_pairs={{0,4},{2,6},{4,0},{6,2},{8,12},{10,14},{12,8},{14,10},{16,20},{18,... | collective-permute-start | bytes 196616 | tf_op jit(solution)/shard_map/ppermute | solution.py:19
  80.6 8.2 %collective-permute-start.23 = (f32[64,128]{1,0:T(8,128)S(1)}, f32[64,128]{1,0:T(8,128)S(1)}, u32[]{:S(2)}, u32[]{:S(2)}) collective-permute-start(f32[64,128]{1,0:T(8,128)S(1)} %slice_select_fusion.1), channel_id=1, source_target_pairs={{0,1},{1,0},{2,3},{3,2},{4,5},{5,4},{6,7},{7,6},{8,9},{9,8},{10,11... | collective-permute-start | bytes 98312 | tf_op jit(solution)/shard_map/ppermute | solution.py:31
  84.9 4.5 %collective-permute-start.30 = (f32[64,256]{1,0:T(8,128)S(1)}, f32[64,256]{1,0:T(8,128)S(1)}, u32[]{:S(2)}, u32[]{:S(2)}) collective-permute-start(f32[64,256]{1,0:T(8,128)S(1)} %maximum_select_fusion.1), channel_id=1, source_target_pairs={{0,2},{2,0},{4,6},{6,4},{8,10},{10,8},{12,14},{14,12},{16,18},{18,... | collective-permute-start | bytes 196616 | tf_op jit(solution)/shard_map/ppermute | solution.py:19

commit v3 on v2

v3 whole, which is shorter than its diff:
```python
import functools

import jax
import jax.numpy as jnp
from jax import lax
from jax.experimental import pallas as pl
from jax.experimental.pallas import tpu as pltpu
from jax.sharding import PartitionSpec as P

F32 = jnp.float32
BF16 = jnp.bfloat16
PTS = 128
HALF = 512
TILE = 256
CORE, X, Z, Y = 0, 1, 3, 5


def swap(value, place, mask):
    return lax.ppermute(value, "pts", [(i, i ^ (mask << place)) for i in range(PTS)])


def swap_ring(value, place, step):
    pairs = []
    for i in range(PTS):
        at = (i >> place) & 3
        pairs.append((i, i + ((((at - step) & 3) - at) << place)))
    return lax.ppermute(value, "pts", pairs)


def swap_lab(value):
    return lax.ppermute(value, "lab", [(0, 1), (1, 0)])


def accumulate(total, rows, row_term, pack):
    for base in range(0, pack.shape[0], HALF + 16):
        terms = pack[base + HALF : base + HALF + 16, :].astype(F32)
        for j in range(HALF // TILE):
            key_term = terms[j : j + 1] + terms[4 + j : 5 + j] + terms[8 + j : 9 + j]
            tile = pl.ds(base + j * TILE, TILE)
            inner = lax.dot_general(
                rows, pack[tile, 0:128], (((1,), (1,)), ((), ())), preferred_element_type=F32
            )
            kernel = jnp.exp(inner + row_term + key_term).astype(BF16)
            total += jnp.dot(kernel, pack[tile, 128:256], preferred_element_type=F32)
    return total


def prepare_kernel(weights_ref, *refs):
    part_refs, (rows_ref, term_ref, cot_ref, zero_ref) = refs[:4], refs[4:]
    weights = weights_ref[...].reshape(1, 128) * (-1.0 / 64.0)
    for d, ref in enumerate(part_refs):
        for m in range(4):
            place = pl.ds(256 * m + 64 * d, 64)
            part = ref[64 * m : 64 * m + 64, :]
            wide = part.astype(F32)
            rows_ref[place, :] = part
            term = jnp.sum(wide * wide * weights, axis=1, keepdims=True)
            term_ref[place, :] = jnp.broadcast_to(term, (64, 128))
        cot_ref[64 * d : 64 * d + 64, :] = ref[256:320, :]
    zero_ref[...] = jnp.zeros_like(zero_ref)


def first_kernel(has_total, *refs):
    rows_ref, term_ref, refs = refs[0], refs[1], refs[2:]
    start, refs = (refs[0], refs[1:]) if has_total else (None, refs)
    packs, out, zero_ref = refs[:-2], refs[-2], refs[-1]
    for m in range(4):
        place = slice(256 * m, 256 * m + 256)
        total = start[place, :] if has_total else jnp.zeros((256, 128), F32)
        for pack in packs:
            total = accumulate(total, rows_ref[place, :], term_ref[place, 0:1], pack)
        out[place, :] = total
    zero_ref[...] = jnp.zeros_like(zero_ref)


def last_kernel(m, *refs):
    rows_ref, term_ref, start, packs, out = refs[0], refs[1], refs[2], refs[3:-1], refs[-1]
    place = slice(256 * m, 256 * m + 256)
    total = start[place, :]
    for pack in packs:
        total = accumulate(total, rows_ref[place, :], term_ref[place, 0:1], pack)
    out[...] = total.astype(out.dtype)


def in_vmem(kernel, out, args, small=None, scratch=()):
    spaces = [pltpu.VMEM] * len(args)
    if small is not None:
        spaces[small] = pltpu.SMEM
    return pl.pallas_call(
        kernel,
        out_shape=out,
        in_specs=[pl.BlockSpec(memory_space=space) for space in spaces],
        scratch_shapes=scratch,
        out_specs=jax.tree.map(lambda _: pl.BlockSpec(memory_space=pltpu.VMEM), out),
        compiler_params=pltpu.CompilerParams(vmem_limit_bytes=8 * 2**20),
        cost_estimate=pl.CostEstimate(
            flops=1000,
            bytes_accessed=2 * 2**20,
            transcendentals=0,
        ),
    )(*args)


ZEROS = jax.ShapeDtypeStruct((16, 256), BF16)


def prepare(weights, rows):
    return in_vmem(
        prepare_kernel,
        (
            jax.ShapeDtypeStruct((1024, 128), BF16),
            jax.ShapeDtypeStruct((1024, 128), F32),
            jax.ShapeDtypeStruct((256, 128), BF16),
            ZEROS,
        ),
        [weights, *rows],
    )


def cross_first(rows, term, total, packs):
    has_total = total is not None
    return in_vmem(
        functools.partial(first_kernel, has_total),
        (jax.ShapeDtypeStruct((1024, 128), F32), ZEROS),
        [rows, term] + ([total] if has_total else []) + list(packs),
    )


def cross_last(m, rows, term, total, packs, dtype):
    return in_vmem(
        functools.partial(last_kernel, m),
        jax.ShapeDtypeStruct((256, 128), dtype),
        [rows, term, total, *packs],
    )


def gate_kernel(value_ref, _, out_ref):
    out_ref[...] = value_ref[...]


def grad_kernel(place_ref, own, *refs):
    back, near, far, cov_ref = refs[:3], refs[3], refs[4], refs[5]
    mixed_ref, mixed_far_ref, grad_ref, grad_far_ref, held = refs[6:]
    own_columns = pl.ds(pl.multiple_of(place_ref[0] * 128, 128), 128)
    far_columns = pl.ds(pl.multiple_of(128 - place_ref[0] * 128, 128), 128)
    turned = (((0,), (0,)), ((), ()))
    one, two, three = (b[...].astype(F32) for b in back)
    cross = (own[...] + one) + (two + three)
    exact = dict(precision=lax.Precision.HIGHEST, preferred_element_type=F32)
    mixed_far_ref[...] = jnp.dot(cross, cov_ref[:, far_columns], **exact).astype(BF16)
    mixed_ref[...] = jnp.dot(cross, cov_ref[:, own_columns], **exact)
    high = cross.astype(BF16)
    rest = (cross - high.astype(F32)).astype(BF16)
    for columns, cot in ((own_columns, near[...]), (far_columns, far[...])):
        held[:, columns] = lax.dot_general(
            high, cot, turned, preferred_element_type=F32
        ) + lax.dot_general(rest, cot, turned, preferred_element_type=F32)
    core = place_ref[1]
    grad_ref[...] = held[pl.ds(pl.multiple_of(core * 64, 64), 64), :]
    grad_far_ref[...] = held[pl.ds(pl.multiple_of(64 - core * 64, 64), 64), :]


def local(slab_points, key_points, length_weights, adjoint, label_cov, cotangent):
    core, lab = lax.axis_index("pts") & 1, lax.axis_index("lab")

    keys = key_points.astype(F32)
    scaled = (keys * length_weights * (1.0 / 32.0)).astype(BF16)
    key_term = jnp.sum(keys * keys * length_weights, axis=1) * (-1.0 / 64.0)
    high = lax.reduce_precision(key_term, 8, 7)
    rest = key_term - high
    middle = lax.reduce_precision(rest, 8, 7)
    both = jnp.concatenate([scaled, adjoint], axis=1)
    halves = []
    for h in (slice(0, HALF), slice(HALF, 2 * HALF)):
        blank = jnp.zeros((2, 256), F32)
        parts = [jnp.concatenate([t[h].reshape(2, 256), blank]) for t in (high, middle, rest - middle)]
        parts = jnp.concatenate([*parts, blank, blank]).astype(BF16)
        halves += [both[h], parts]
    pack = jnp.concatenate(halves, axis=0)

    right = swap_ring(pack, X, 1)
    left = swap_ring(pack, X, 3)
    own_far = swap(pack, CORE, 1)

    own = in_vmem(gate_kernel, jax.ShapeDtypeStruct((64, 128), BF16), [slab_points, own_far])
    part = jnp.concatenate([own] + [swap(own, Z, m) for m in (1, 2, 3)] + [cotangent], axis=0)
    rows, term, cot, zeros = prepare(
        length_weights, [part] + [swap(part, Y, m) for m in (1, 2, 3)]
    )

    right, left = right + zeros[0:1], left + zeros[0:1]
    upper = swap_ring(right[:528], X, 1)
    lower = swap_ring(left[528:], X, 3)
    right_far, left_far = swap(right, CORE, 1), swap(left, CORE, 1)
    cot_far = swap_lab(cot)

    total, zeros = cross_first(rows, term, None, [pack, own_far, right, right_far])
    upper, lower = upper + zeros[0:1], lower + zeros[0:1]
    upper_far, lower_far = swap(upper, CORE, 1), swap(lower, CORE, 1)
    total, _ = cross_first(rows, term, total, [left, left_far])
    packs = [upper, lower, upper_far, lower_far]
    sent = {
        m: cross_last(m, rows, term, total, packs, F32 if m == 0 else BF16)
        for m in (2, 1, 3, 0)
    }
    back = [swap(sent[m], Z, m) for m in (1, 2, 3)]

    mixed, mixed_far, grad, grad_far = in_vmem(
        grad_kernel,
        (
            jax.ShapeDtypeStruct((256, 128), F32),
            jax.ShapeDtypeStruct((256, 128), BF16),
            jax.ShapeDtypeStruct((64, 256), F32),
            jax.ShapeDtypeStruct((64, 256), F32),
        ),
        [jnp.stack([lab, core]), sent[0], *back, cot, cot_far, label_cov],
        small=0,
        scratch=[pltpu.VMEM((128, 256), F32)],
    )
    mixed = mixed + swap_lab(mixed_far).astype(F32)
    grad = grad + swap(grad_far, CORE, 1)
    back = [swap(grad, X, m) for m in (1, 2, 3)]
    grad = ((grad + back[0]) + (back[1] + back[2])).astype(BF16)

    back = [
        swap(
            jnp.concatenate([mixed[64 * m : 64 * m + 64].astype(BF16), grad], axis=1), Y, m
        ).astype(F32)
        for m in (1, 2, 3)
    ]
    mixed = (mixed[:64] + back[0][:, :128]) + (back[1][:, :128] + back[2][:, :128])
    back = [b[:, 128:] for b in back]
    grad = ((grad.astype(F32) + back[0]) + (back[1] + back[2])).astype(BF16)

    back = [swap(grad, Z, m).astype(F32) for m in (1, 2, 3)]
    grad = (grad.astype(F32) + back[0]) + (back[1] + back[2])
    other = swap(grad, CORE, 1)
    grad = jnp.where(
        core == 0,
        jnp.concatenate([grad, other], axis=0),
        jnp.concatenate([other, grad], axis=0),
    )
    return mixed.astype(BF16), grad


def solution(mesh):
    placed = (P("pts", None), P("pts", None), P(), P("pts", "lab"), P("lab", None), P("pts", "lab"))
    return jax.shard_map(
        local,
        mesh=mesh,
        in_specs=placed,
        out_specs=(P("pts", "lab"), P("lab", None)),
        check_vma=False,
    )
```

time: 90.3 us -> 88.2 us (0.977)
  the two profiles are of different devices: /device:TPU:2 before, /device:TPU:1 now
where the time goes in v3:
time: 88.2 us; the launch traced here: 88 us
  starting transfers between devices  46.7 us (53%)
  waiting for transfers between devices  23.7 us (27%)
  Pallas kernels  13.3 us (15%)
  other arithmetic  2.88 us (3%)
  between operations  0.94 us (1%)
    ppermute x25, starting transfers between devices, swap(): lax.ppermute(value, 'pts', [(i, i ^ mask << place) for i in range(PTS)])  37.1 us
    ppermute x25, waiting for transfers between devices, swap(): lax.ppermute(value, 'pts', [(i, i ^ mask << place) for i in range(PTS)])  16.9 us
    pallas_call x9, Pallas kernels, in_vmem(): pl.pallas_call(kernel, out_shape=out, in_specs=[pl.BlockSpec(memory_space...  13.3 us
    ppermute x2, starting transfers between devices, swap_lab(): return lax.ppermute(value, 'lab', [(0, 1), (1, 0)])  5.07 us
    ppermute x4, starting transfers between devices, swap_ring(): return lax.ppermute(value, 'pts', pairs)  4.59 us
    ppermute x2, waiting for transfers between devices, swap_lab(): return lax.ppermute(value, 'lab', [(0, 1), (1, 0)])  3.7 us
    ppermute x4, waiting for transfers between devices, swap_ring(): return lax.ppermute(value, 'pts', pairs)  3.07 us
  transfers between devices with their start and end apart: 31, of which 13 were waited for; matrix products, arithmetic and copies ran while one was open for 1% of the time, Pallas kernels for 14%

profile of v3, /device:TPU:1, one launch (start us, length us, event | category | flops | bytes accessed | tf_op | source)
XLA Modules:
  0.0 88.0 jit_solution(4806364787667381882)
XLA Ops:
  0.6 1.2 %fusion.3 = (f32[1024]{0:T(1024)S(1)}, bf16[1024,128]{1,0:T(8,128)(2,1)S(1)}) fusion(bf16[1024,128]{1,0:T(8,128)(2,1)} %param.7, f32[128]{0:T(128)} %weights_ref.1), kind=kLoop, calls=%fused_computation.5 | loop fusion | flops 916480 | bytes 528896 | tf_op jit(solution)/shard_map/reduce_sum | solution.py:168
  2.0 0.3 concatenate.30.refs_2_
  2.3 3.3 %collective-permute-start = (bf16[1056,256]{1,0:T(8,128)(2,1)S(1)}, bf16[1056,256]{1,0:T(8,128)(2,1)S(1)}, u32[]{:S(2)}, u32[]{:S(2)}) collective-permute-start(bf16[1056,256]{1,0:T(8,128)(2,1)S(1)} %concatenate.30.refs_2_), channel_id=1, source_target_pairs={{0,2},{2,0},{4,6},{6,4},{8,10},{10,8},{12,14},{14,12},{16,18},{18,... | collective-permute-start | bytes 1622024 | tf_op jit(solution)/shard_map/ppermute | solution.py:19
  5.6 0.8 collective-permute-start.7
  6.4 0.7 collective-permute-start.9
  7.2 0.9 %collective-permute-start.1 = (bf16[64,128]{1,0:T(8,128)(2,1)S(1)}, bf16[64,128]{1,0:T(8,128)(2,1)S(1)}, u32[]{:S(2)}, u32[]{:S(2)}) collective-permute-start(bf16[64,128]{1,0:T(8,128)(2,1)S(1)} %shard_map.77), channel_id=1, source_target_pairs={{0,16},{2,18},{4,20},{6,22},{8,24},{10,26},{12,28},{14,30},{16,0},... | collective-permute-start | bytes 49160 | tf_op jit(solution)/shard_map/ppermute | solution.py:19
  8.1 3.0 %collective-permute-start.2 = (bf16[64,128]{1,0:T(8,128)(2,1)S(1)}, bf16[64,128]{1,0:T(8,128)(2,1)S(1)}, u32[]{:S(2)}, u32[]{:S(2)}) collective-permute-start(bf16[64,128]{1,0:T(8,128)(2,1)S(1)} %shard_map.77), channel_id=1, source_target_pairs={{0,32},{2,34},{4,36},{6,38},{8,40},{10,42},{12,44},{14,46},{16,48}... | collective-permute-start | bytes 49160 | tf_op jit(solution)/shard_map/ppermute | solution.py:19
  11.1 1.5 %collective-permute-done.2 = bf16[64,128]{1,0:T(8,128)(2,1)S(1)} collective-permute-done((bf16[64,128]{1,0:T(8,128)(2,1)S(1)}, bf16[64,128]{1,0:T(8,128)(2,1)S(1)}, u32[]{:S(2)}, u32[]{:S(2)}) %collective-permute-start.2) | collective-permute-done | bytes 16416 | tf_op jit(solution)/shard_map/ppermute | solution.py:19
  12.6 2.9 %collective-permute-done.3 = bf16[64,128]{1,0:T(8,128)(2,1)S(1)} collective-permute-done((bf16[64,128]{1,0:T(8,128)(2,1)S(1)}, bf16[64,128]{1,0:T(8,128)(2,1)S(1)}, u32[]{:S(2)}, u32[]{:S(2)}) %collective-permute-start.3) | collective-permute-done | bytes 16416 | tf_op jit(solution)/shard_map/ppermute | solution.py:19
  15.5 1.4 %collective-permute-start.4 = (bf16[320,128]{1,0:T(8,128)(2,1)S(1)}, bf16[320,128]{1,0:T(8,128)(2,1)S(1)}, u32[]{:S(2)}, u32[]{:S(2)}) collective-permute-start(bf16[320,128]{1,0:T(8,128)(2,1)S(1)} %constant_dynamic-update-slice_fusion.refs_0_), channel_id=1, source_target_pairs={{0,64},{2,66},{4,68},{6,70},{8,72},{10,74},{12,76},{14,78},{16,80}... | collective-permute-start | bytes 245768 | tf_op jit(solution)/shard_map/ppermute | solution.py:19
  16.9 2.6 %collective-permute-start.5 = (bf16[320,128]{1,0:T(8,128)(2,1)S(1)}, bf16[320,128]{1,0:T(8,128)(2,1)S(1)}, u32[]{:S(2)}, u32[]{:S(2)}) collective-permute-start(bf16[320,128]{1,0:T(8,128)(2,1)S(1)} %constant_dynamic-update-slice_fusion.refs_0_), channel_id=1, source_target_pairs={{0,128},{2,130},{4,132},{6,134},{8,136},{10,138},{12,140},{14,142}... | collective-permute-start | bytes 245768 | tf_op jit(solution)/shard_map/ppermute | solution.py:19
  19.5 2.7 %collective-permute-done.5.refs_2_ = bf16[320,128]{1,0:T(8,128)(2,1)S(1)} collective-permute-done((bf16[320,128]{1,0:T(8,128)(2,1)S(1)}, bf16[320,128]{1,0:T(8,128)(2,1)S(1)}, u32[]{:S(2)}, u32[]{:S(2)}) %collective-permute-start.5) | collective-permute-done | bytes 81952 | tf_op jit(solution)/shard_map/ppermute | solution.py:19
  22.2 2.8 %collective-permute-done.6.refs_3_ = bf16[320,128]{1,0:T(8,128)(2,1)S(1)} collective-permute-done((bf16[320,128]{1,0:T(8,128)(2,1)S(1)}, bf16[320,128]{1,0:T(8,128)(2,1)S(1)}, u32[]{:S(2)}, u32[]{:S(2)}) %collective-permute-start.6) | collective-permute-done | bytes 81952 | tf_op jit(solution)/shard_map/ppermute | solution.py:19
  25.1 0.2 shard_map.78
  25.4 2.8 %collective-permute-start.8 = (bf16[1056,256]{1,0:T(8,128)(2,1)S(1)}, bf16[1056,256]{1,0:T(8,128)(2,1)S(1)}, u32[]{:S(2)}, u32[]{:S(2)}) collective-permute-start(bf16[1056,256]{1,0:T(8,128)(2,1)S(1)} %get-tuple-element.48.refs_4_), channel_id=1, source_target_pairs={{0,2},{2,0},{4,6},{6,4},{8,10},{10,8},{12,14},{14,12},{16,18},{18,... | collective-permute-start | bytes 1622024 | tf_op jit(solution)/shard_map/ppermute | solution.py:19
  28.3 3.0 %collective-permute-start.11 = (bf16[528,256]{1,0:T(8,128)(2,1)S(1)}, bf16[528,256]{1,0:T(8,128)(2,1)S(1)}, u32[]{:S(2)}, u32[]{:S(2)}) collective-permute-start(bf16[528,256]{1,0:T(8,128)(2,1)S(1)} %slice.113), channel_id=1, source_target_pairs={{0,12},{2,14},{4,0},{6,2},{8,4},{10,6},{12,8},{14,10},{16,28},{18,... | collective-permute-start | bytes 811016 | tf_op jit(solution)/shard_map/ppermute | solution.py:27
  31.4 0.6 collective-permute-start.10
  32.0 5.3 %shard_map.79 = (f32[1024,128]{1,0:T(8,128)S(1)}, bf16[16,256]{1,0:T(8,128)(2,1)S(1)}) custom-call(bf16[1024,128]{1,0:T(8,128)(2,1)S(1)} %get-tuple-element.13.refs_0_, f32[1024,128]{1,0:T(8,128)S(1)} %get-tuple-element.14.refs_1_, bf16[1056,256]{1,0:T(8,128)(2,1)S(1)} %concatenate.30.refs_2_, bf16[1056,256]{1,0:T(8,128)(2,1)S(1)} %collective-permute-done._.refs_3_, ...), custom_call_target="tpu_custom_call" | custom-call | flops 1000 | bytes 2097152 | tf_op jit(solution)/shard_map/pallas_call | solution.py:89
  37.3 3.1 %collective-permute-done.12 = bf16[528,256]{1,0:T(8,128)(2,1)S(1)} collective-permute-done((bf16[528,256]{1,0:T(8,128)(2,1)S(1)}, bf16[528,256]{1,0:T(8,128)(2,1)S(1)}, u32[]{:S(2)}, u32[]{:S(2)}) %collective-permute-start.12) | collective-permute-done | bytes 270368 | tf_op jit(solution)/shard_map/ppermute | solution.py:27
  40.4 1.2 %collective-permute-start.13 = (bf16[528,256]{1,0:T(8,128)(2,1)S(1)}, bf16[528,256]{1,0:T(8,128)(2,1)S(1)}, u32[]{:S(2)}, u32[]{:S(2)}) collective-permute-start(bf16[528,256]{1,0:T(8,128)(2,1)S(1)} %get-tuple-element.46.refs_3_), channel_id=1, source_target_pairs={{0,2},{2,0},{4,6},{6,4},{8,10},{10,8},{12,14},{14,12},{16,18},{18,... | collective-permute-start | bytes 811016 | tf_op jit(solution)/shard_map/ppermute | solution.py:19
  41.7 4.2 %collective-permute-start.18 = (bf16[256,128]{1,0:T(8,128)(2,1)S(1)}, bf16[256,128]{1,0:T(8,128)(2,1)S(1)}, u32[]{:S(2)}, u32[]{:S(2)}) collective-permute-start(bf16[256,128]{1,0:T(8,128)(2,1)S(1)} %get-tuple-element.19.refs_3_), channel_id=1, source_target_pairs={{0,1},{1,0},{2,3},{3,2},{4,5},{5,4},{6,7},{7,6},{8,9},{9,8},{10,11... | collective-permute-start | bytes 196616 | tf_op jit(solution)/shard_map/ppermute | solution.py:31
  45.9 2.9 %shard_map.80 = (f32[1024,128]{1,0:T(8,128)S(1)}, bf16[16,256]{1,0:T(8,128)(2,1)}) custom-call(bf16[1024,128]{1,0:T(8,128)(2,1)S(1)} %get-tuple-element.13.refs_0_, f32[1024,128]{1,0:T(8,128)S(1)} %get-tuple-element.14.refs_1_, f32[1024,128]{1,0:T(8,128)S(1)} %get-tuple-element.16.refs_2_, bf16[1056,256]{1,0:T(8,128)(2,1)S(1)} %get-tuple-element.47.refs_3_, ...), custom_call_target="tpu_custom_call" | custom-call | flops 1000 | bytes 2097152 | tf_op jit(solution)/shard_map/pallas_call | solution.py:89
  48.9 1.0 %shard_map.84 = bf16[256,128]{1,0:T(8,128)(2,1)S(1)} custom-call(bf16[1024,128]{1,0:T(8,128)(2,1)S(1)} %get-tuple-element.13.refs_0_, f32[1024,128]{1,0:T(8,128)S(1)} %get-tuple-element.14.refs_1_, f32[1024,128]{1,0:T(8,128)S(1)} %get-tuple-element.17.refs_2_, bf16[528,256]{1,0:T(8,128)(2,1)S(1)} %get-tuple-element.46.refs_3_, ...), custom_call_target="tpu_custom_call" | custom-call | flops 1000 | bytes 2097152 | tf_op jit(solution)/shard_map/pallas_call | solution.py:89
  49.9 1.7 %collective-permute-start.17 = (bf16[256,128]{1,0:T(8,128)(2,1)S(1)}, bf16[256,128]{1,0:T(8,128)(2,1)S(1)}, u32[]{:S(2)}, u32[]{:S(2)}) collective-permute-start(bf16[256,128]{1,0:T(8,128)(2,1)S(1)} %shard_map.84), channel_id=1, source_target_pairs={{0,48},{2,50},{4,52},{6,54},{8,56},{10,58},{12,60},{14,62},{16,32}... | collective-permute-start | bytes 196616 | tf_op jit(solution)/shard_map/ppermute | solution.py:19
  51.6 1.0 %shard_map.83 = bf16[256,128]{1,0:T(8,128)(2,1)S(1)} custom-call(bf16[1024,128]{1,0:T(8,128)(2,1)S(1)} %get-tuple-element.13.refs_0_, f32[1024,128]{1,0:T(8,128)S(1)} %get-tuple-element.14.refs_1_, f32[1024,128]{1,0:T(8,128)S(1)} %get-tuple-element.17.refs_2_, bf16[528,256]{1,0:T(8,128)(2,1)S(1)} %get-tuple-element.46.refs_3_, ...), custom_call_target="tpu_custom_call" | custom-call | flops 1000 | bytes 2097152 | tf_op jit(solution)/shard_map/pallas_call | solution.py:89
  52.5 0.3 collective-permute-start.16
  52.9 1.0 %shard_map.82 = bf16[256,128]{1,0:T(8,128)(2,1)S(1)} custom-call(bf16[1024,128]{1,0:T(8,128)(2,1)S(1)} %get-tuple-element.13.refs_0_, f32[1024,128]{1,0:T(8,128)S(1)} %get-tuple-element.14.refs_1_, f32[1024,128]{1,0:T(8,128)S(1)} %get-tuple-element.17.refs_2_, bf16[528,256]{1,0:T(8,128)(2,1)S(1)} %get-tuple-element.46.refs_3_, ...), custom_call_target="tpu_custom_call" | custom-call | flops 1000 | bytes 2097152 | tf_op jit(solution)/shard_map/pallas_call | solution.py:89
  53.8 2.0 %collective-permute-start.15 = (bf16[256,128]{1,0:T(8,128)(2,1)S(1)}, bf16[256,128]{1,0:T(8,128)(2,1)S(1)}, u32[]{:S(2)}, u32[]{:S(2)}) collective-permute-start(bf16[256,128]{1,0:T(8,128)(2,1)S(1)} %shard_map.82), channel_id=1, source_target_pairs={{0,16},{2,18},{4,20},{6,22},{8,24},{10,26},{12,28},{14,30},{16,0},... | collective-permute-start | bytes 196616 | tf_op jit(solution)/shard_map/ppermute | solution.py:19
  55.9 1.0 %shard_map.81.own = f32[256,128]{1,0:T(8,128)S(1)} custom-call(bf16[1024,128]{1,0:T(8,128)(2,1)S(1)} %get-tuple-element.13.refs_0_, f32[1024,128]{1,0:T(8,128)S(1)} %get-tuple-element.14.refs_1_, f32[1024,128]{1,0:T(8,128)S(1)} %get-tuple-element.17.refs_2_, bf16[528,256]{1,0:T(8,128)(2,1)S(1)} %get-tuple-element.46.refs_3_, ...), custom_call_target="tpu_custom_call" | custom-call | flops 1000 | bytes 2097152 | tf_op jit(solution)/shard_map/pallas_call | solution.py:89
  56.9 2.1 %collective-permute-done.16.refs_1_ = bf16[256,128]{1,0:T(8,128)(2,1)S(1)} collective-permute-done((bf16[256,128]{1,0:T(8,128)(2,1)S(1)}, bf16[256,128]{1,0:T(8,128)(2,1)S(1)}, u32[]{:S(2)}, u32[]{:S(2)}) %collective-permute-start.16) | collective-permute-done | bytes 65568 | tf_op jit(solution)/shard_map/ppermute | solution.py:19
  59.0 1.0 %shard_map.85 = (f32[256,128]{1,0:T(8,128)S(1)}, bf16[256,128]{1,0:T(8,128)(2,1)S(1)}, f32[64,256]{1,0:T(8,128)S(1)}, f32[64,256]{1,0:T(8,128)S(1)}) custom-call(s32[2]{0:T(128)S(1)} %pad_add_fusion.place_ref, f32[256,128]{1,0:T(8,128)S(1)} %shard_map.81.own, bf16[256,128]{1,0:T(8,128)(2,1)S(1)} %collective-permute-done.15.refs_0_, ...), custom_call_target="tpu_custom_call" | custom-call | flops 1000 | bytes 2097152 | tf_op jit(solution)/shard_map/pallas_call | solution.py:89
  60.0 1.3 %collective-permute-start.20 = (f32[64,256]{1,0:T(8,128)S(1)}, f32[64,256]{1,0:T(8,128)S(1)}, u32[]{:S(2)}, u32[]{:S(2)}) collective-permute-start(f32[64,256]{1,0:T(8,128)S(1)} %get-tuple-element.23), channel_id=1, source_target_pairs={{0,2},{2,0},{4,6},{6,4},{8,10},{10,8},{12,14},{14,12},{16,18},{18,... | collective-permute-start | bytes 196616 | tf_op jit(solution)/shard_map/ppermute | solution.py:19
  61.3 0.9 collective-permute-start.19
  62.3 1.1 %collective-permute-start.22 = (f32[64,256]{1,0:T(8,128)S(1)}, f32[64,256]{1,0:T(8,128)S(1)}, u32[]{:S(2)}, u32[]{:S(2)}) collective-permute-start(f32[64,256]{1,0:T(8,128)S(1)} %add.83), channel_id=1, source_target_pairs={{0,8},{2,10},{4,12},{6,14},{8,0},{10,2},{12,4},{14,6},{16,24},{18,... | collective-permute-start | bytes 196616 | tf_op jit(solution)/shard_map/ppermute | solution.py:19
  63.4 2.8 %collective-permute-start.23 = (f32[64,256]{1,0:T(8,128)S(1)}, f32[64,256]{1,0:T(8,128)S(1)}, u32[]{:S(2)}, u32[]{:S(2)}) collective-permute-start(f32[64,256]{1,0:T(8,128)S(1)} %add.83), channel_id=1, source_target_pairs={{0,12},{2,14},{4,8},{6,10},{8,4},{10,6},{12,0},{14,2},{16,28},{18,... | collective-permute-start | bytes 196616 | tf_op jit(solution)/shard_map/ppermute | solution.py:19
  66.2 3.7 %collective-permute-done.19 = bf16[256,128]{1,0:T(8,128)(2,1)S(1)} collective-permute-done((bf16[256,128]{1,0:T(8,128)(2,1)S(1)}, bf16[256,128]{1,0:T(8,128)(2,1)S(1)}, u32[]{:S(2)}, u32[]{:S(2)}) %collective-permute-start.19) | collective-permute-done | bytes 65568 | tf_op jit(solution)/shard_map/ppermute | solution.py:31
  70.1 1.3 %collective-permute-start.25 = (bf16[64,384]{1,0:T(8,128)(2,1)S(1)}, bf16[64,384]{1,0:T(8,128)(2,1)S(1)}, u32[]{:S(2)}, u32[]{:S(2)}) collective-permute-start(bf16[64,384]{1,0:T(8,128)(2,1)S(1)} %get-tuple-element.34), channel_id=1, source_target_pairs={{0,128},{2,130},{4,132},{6,134},{8,136},{10,138},{12,140},{14,142}... | collective-permute-start | bytes 147464 | tf_op jit(solution)/shard_map/ppermute | solution.py:19
  71.4 2.5 %collective-permute-start.26 = (bf16[64,384]{1,0:T(8,128)(2,1)S(1)}, bf16[64,384]{1,0:T(8,128)(2,1)S(1)}, u32[]{:S(2)}, u32[]{:S(2)}) collective-permute-start(bf16[64,384]{1,0:T(8,128)(2,1)S(1)} %get-tuple-element.35), channel_id=1, source_target_pairs={{0,192},{2,194},{4,196},{6,198},{8,200},{10,202},{12,204},{14,206}... | collective-permute-start | bytes 147464 | tf_op jit(solution)/shard_map/ppermute | solution.py:19
  74.0 0.7 collective-permute-done.25
  74.6 1.5 %collective-permute-done.26 = bf16[64,384]{1,0:T(8,128)(2,1)S(1)} collective-permute-done((bf16[64,384]{1,0:T(8,128)(2,1)S(1)}, bf16[64,384]{1,0:T(8,128)(2,1)S(1)}, u32[]{:S(2)}, u32[]{:S(2)}) %collective-permute-start.26) | collective-permute-done | bytes 49184 | tf_op jit(solution)/shard_map/ppermute | solution.py:19
  76.2 1.7 %collective-permute-start.27 = (bf16[64,256]{1,0:T(8,128)(2,1)S(1)}, bf16[64,256]{1,0:T(8,128)(2,1)S(1)}, u32[]{:S(2)}, u32[]{:S(2)}) collective-permute-start(bf16[64,256]{1,0:T(8,128)(2,1)S(1)} %fusion.6), channel_id=1, source_target_pairs={{0,16},{2,18},{4,20},{6,22},{8,24},{10,26},{12,28},{14,30},{16,0},... | collective-permute-start | bytes 98312 | tf_op jit(solution)/shard_map/ppermute | solution.py:19
  77.9 2.2 %collective-permute-start.29 = (bf16[64,256]{1,0:T(8,128)(2,1)S(1)}, bf16[64,256]{1,0:T(8,128)(2,1)S(1)}, u32[]{:S(2)}, u32[]{:S(2)}) collective-permute-start(bf16[64,256]{1,0:T(8,128)(2,1)S(1)} %fusion.6), channel_id=1, source_target_pairs={{0,48},{2,50},{4,52},{6,54},{8,56},{10,58},{12,60},{14,62},{16,32}... | collective-permute-start | bytes 98312 | tf_op jit(solution)/shard_map/ppermute | solution.py:19
  80.1 1.6 %collective-permute-done.28 = bf16[64,256]{1,0:T(8,128)(2,1)S(1)} collective-permute-done((bf16[64,256]{1,0:T(8,128)(2,1)S(1)}, bf16[64,256]{1,0:T(8,128)(2,1)S(1)}, u32[]{:S(2)}, u32[]{:S(2)}) %collective-permute-start.28) | collective-permute-done | bytes 32800 | tf_op jit(solution)/shard_map/ppermute | solution.py:19
  81.7 0.7 collective-permute-done.29
  82.5 4.0 %collective-permute-start.30 = (f32[64,256]{1,0:T(8,128)S(1)}, f32[64,256]{1,0:T(8,128)S(1)}, u32[]{:S(2)}, u32[]{:S(2)}) collective-permute-start(f32[64,256]{1,0:T(8,128)S(1)} %add_add_fusion), channel_id=1, source_target_pairs={{0,2},{2,0},{4,6},{6,4},{8,10},{10,8},{12,14},{14,12},{16,18},{18,... | collective-permute-start | bytes 196616 | tf_op jit(solution)/shard_map/ppermute | solution.py:19
  86.5 0.6 fusion.8
  87.1 0.3 collective-permute-done.30
  87.4 0.7 maximum_select_fusion
  (67 shorter events, 1.1 us)
Async XLA Ops:
  0.6 1.3 %copy-start.3 = (bf16[1024,128]{1,0:T(8,128)(2,1)S(1)}, bf16[1024,128]{1,0:T(8,128)(2,1)}, u32[]{:S(2)}) copy-start(bf16[1024,128]{1,0:T(8,128)(2,1)} %param.9) | copy-start | bytes 786436
  2.0 5.2 %copy-start.1 = (bf16[64,128]{1,0:T(8,128)(2,1)S(1)}, bf16[64,128]{1,0:T(8,128)(2,1)}, u32[]{:S(2)}) copy-start(bf16[64,128]{1,0:T(8,128)(2,1)} %value_ref.1) | copy-start | bytes 49156
  2.3 4.9 %collective-permute-start = (bf16[1056,256]{1,0:T(8,128)(2,1)S(1)}, bf16[1056,256]{1,0:T(8,128)(2,1)S(1)}, u32[]{:S(2)}, u32[]{:S(2)}) collective-permute-start(bf16[1056,256]{1,0:T(8,128)(2,1)S(1)} %concatenate.30.refs_2_), channel_id=1, source_target_pairs={{0,2},{2,0},{4,6},{6,4},{8,10},{10,8},{12,14},{14,12},{16,18},{18,... | collective-permute-start | bytes 1622024 | tf_op jit(solution)/shard_map/ppermute | solution.py:19
  5.6 19.7 %collective-permute-start.7 = (bf16[1056,256]{1,0:T(8,128)(2,1)S(1)}, bf16[1056,256]{1,0:T(8,128)(2,1)S(1)}, u32[]{:S(2)}, u32[]{:S(2)}) collective-permute-start(bf16[1056,256]{1,0:T(8,128)(2,1)S(1)} %concatenate.30.refs_2_), channel_id=1, source_target_pairs={{0,12},{2,14},{4,0},{6,2},{8,4},{10,6},{12,8},{14,10},{16,28},{18,... | collective-permute-start | bytes 1622024 | tf_op jit(solution)/shard_map/ppermute | solution.py:27
  6.4 18.9 %collective-permute-start.9 = (bf16[1056,256]{1,0:T(8,128)(2,1)S(1)}, bf16[1056,256]{1,0:T(8,128)(2,1)S(1)}, u32[]{:S(2)}, u32[]{:S(2)}) collective-permute-start(bf16[1056,256]{1,0:T(8,128)(2,1)S(1)} %concatenate.30.refs_2_), channel_id=1, source_target_pairs={{0,4},{2,6},{4,8},{6,10},{8,12},{10,14},{12,0},{14,2},{16,20},{18,... | collective-permute-start | bytes 1622024 | tf_op jit(solution)/shard_map/ppermute | solution.py:27
  7.2 3.9 %collective-permute-start.1 = (bf16[64,128]{1,0:T(8,128)(2,1)S(1)}, bf16[64,128]{1,0:T(8,128)(2,1)S(1)}, u32[]{:S(2)}, u32[]{:S(2)}) collective-permute-start(bf16[64,128]{1,0:T(8,128)(2,1)S(1)} %shard_map.77), channel_id=1, source_target_pairs={{0,16},{2,18},{4,20},{6,22},{8,24},{10,26},{12,28},{14,30},{16,0},... | collective-permute-start | bytes 49160 | tf_op jit(solution)/shard_map/ppermute | solution.py:19
  8.1 4.5 %collective-permute-start.2 = (bf16[64,128]{1,0:T(8,128)(2,1)S(1)}, bf16[64,128]{1,0:T(8,128)(2,1)S(1)}, u32[]{:S(2)}, u32[]{:S(2)}) collective-permute-start(bf16[64,128]{1,0:T(8,128)(2,1)S(1)} %shard_map.77), channel_id=1, source_target_pairs={{0,32},{2,34},{4,36},{6,38},{8,40},{10,42},{12,44},{14,46},{16,48}... | collective-permute-start | bytes 49160 | tf_op jit(solution)/shard_map/ppermute | solution.py:19
  11.1 4.4 %collective-permute-start.3 = (bf16[64,128]{1,0:T(8,128)(2,1)S(1)}, bf16[64,128]{1,0:T(8,128)(2,1)S(1)}, u32[]{:S(2)}, u32[]{:S(2)}) collective-permute-start(bf16[64,128]{1,0:T(8,128)(2,1)S(1)} %shard_map.77), channel_id=1, source_target_pairs={{0,48},{2,50},{4,52},{6,54},{8,56},{10,58},{12,60},{14,62},{16,32}... | collective-permute-start | bytes 49160 | tf_op jit(solution)/shard_map/ppermute | solution.py:19
  12.6 2.9 %copy-start.4 = (bf16[64,128]{1,0:T(8,128)(2,1)S(1)}, bf16[64,128]{1,0:T(8,128)(2,1)}, u32[]{:S(2)}) copy-start(bf16[64,128]{1,0:T(8,128)(2,1)} %param.11) | copy-start | bytes 49156
  15.5 9.5 %copy-start.2 = (f32[128]{0:T(128)S(1)}, f32[128]{0:T(128)}, u32[]{:S(2)}) copy-start(f32[128]{0:T(128)} %weights_ref.1) | copy-start | bytes 1540
  15.5 4.0 %collective-permute-start.4 = (bf16[320,128]{1,0:T(8,128)(2,1)S(1)}, bf16[320,128]{1,0:T(8,128)(2,1)S(1)}, u32[]{:S(2)}, u32[]{:S(2)}) collective-permute-start(bf16[320,128]{1,0:T(8,128)(2,1)S(1)} %constant_dynamic-update-slice_fusion.refs_0_), channel_id=1, source_target_pairs={{0,64},{2,66},{4,68},{6,70},{8,72},{10,74},{12,76},{14,78},{16,80}... | collective-permute-start | bytes 245768 | tf_op jit(solution)/shard_map/ppermute | solution.py:19
  16.9 5.3 %collective-permute-start.5 = (bf16[320,128]{1,0:T(8,128)(2,1)S(1)}, bf16[320,128]{1,0:T(8,128)(2,1)S(1)}, u32[]{:S(2)}, u32[]{:S(2)}) collective-permute-start(bf16[320,128]{1,0:T(8,128)(2,1)S(1)} %constant_dynamic-update-slice_fusion.refs_0_), channel_id=1, source_target_pairs={{0,128},{2,130},{4,132},{6,134},{8,136},{10,138},{12,140},{14,142}... | collective-permute-start | bytes 245768 | tf_op jit(solution)/shard_map/ppermute | solution.py:19
  19.5 5.5 %collective-permute-start.6 = (bf16[320,128]{1,0:T(8,128)(2,1)S(1)}, bf16[320,128]{1,0:T(8,128)(2,1)S(1)}, u32[]{:S(2)}, u32[]{:S(2)}) collective-permute-start(bf16[320,128]{1,0:T(8,128)(2,1)S(1)} %constant_dynamic-update-slice_fusion.refs_0_), channel_id=1, source_target_pairs={{0,192},{2,194},{4,196},{6,198},{8,200},{10,202},{12,204},{14,206}... | collective-permute-start | bytes 245768 | tf_op jit(solution)/shard_map/ppermute | solution.py:19
  25.4 6.6 %collective-permute-start.8 = (bf16[1056,256]{1,0:T(8,128)(2,1)S(1)}, bf16[1056,256]{1,0:T(8,128)(2,1)S(1)}, u32[]{:S(2)}, u32[]{:S(2)}) collective-permute-start(bf16[1056,256]{1,0:T(8,128)(2,1)S(1)} %get-tuple-element.48.refs_4_), channel_id=1, source_target_pairs={{0,2},{2,0},{4,6},{6,4},{8,10},{10,8},{12,14},{14,12},{16,18},{18,... | collective-permute-start | bytes 1622024 | tf_op jit(solution)/shard_map/ppermute | solution.py:19
  28.3 9.0 %collective-permute-start.11 = (bf16[528,256]{1,0:T(8,128)(2,1)S(1)}, bf16[528,256]{1,0:T(8,128)(2,1)S(1)}, u32[]{:S(2)}, u32[]{:S(2)}) collective-permute-start(bf16[528,256]{1,0:T(8,128)(2,1)S(1)} %slice.113), channel_id=1, source_target_pairs={{0,12},{2,14},{4,0},{6,2},{8,4},{10,6},{12,8},{14,10},{16,28},{18,... | collective-permute-start | bytes 811016 | tf_op jit(solution)/shard_map/ppermute | solution.py:27
  31.3 9.1 %collective-permute-start.12 = (bf16[528,256]{1,0:T(8,128)(2,1)S(1)}, bf16[528,256]{1,0:T(8,128)(2,1)S(1)}, u32[]{:S(2)}, u32[]{:S(2)}) collective-permute-start(bf16[528,256]{1,0:T(8,128)(2,1)S(1)} %slice.114), channel_id=1, source_target_pairs={{0,4},{2,6},{4,8},{6,10},{8,12},{10,14},{12,0},{14,2},{16,20},{18,... | collective-permute-start | bytes 811016 | tf_op jit(solution)/shard_map/ppermute | solution.py:27
  31.4 14.5 %collective-permute-start.10 = (bf16[1056,256]{1,0:T(8,128)(2,1)S(1)}, bf16[1056,256]{1,0:T(8,128)(2,1)S(1)}, u32[]{:S(2)}, u32[]{:S(2)}) collective-permute-start(bf16[1056,256]{1,0:T(8,128)(2,1)S(1)} %get-tuple-element.47.refs_3_), channel_id=1, source_target_pairs={{0,2},{2,0},{4,6},{6,4},{8,10},{10,8},{12,14},{14,12},{16,18},{18,... | collective-permute-start | bytes 1622024 | tf_op jit(solution)/shard_map/ppermute | solution.py:19
  40.4 8.5 %collective-permute-start.13 = (bf16[528,256]{1,0:T(8,128)(2,1)S(1)}, bf16[528,256]{1,0:T(8,128)(2,1)S(1)}, u32[]{:S(2)}, u32[]{:S(2)}) collective-permute-start(bf16[528,256]{1,0:T(8,128)(2,1)S(1)} %get-tuple-element.46.refs_3_), channel_id=1, source_target_pairs={{0,2},{2,0},{4,6},{6,4},{8,10},{10,8},{12,14},{14,12},{16,18},{18,... | collective-permute-start | bytes 811016 | tf_op jit(solution)/shard_map/ppermute | solution.py:19
  41.6 7.3 %collective-permute-start.14 = (bf16[528,256]{1,0:T(8,128)(2,1)S(1)}, bf16[528,256]{1,0:T(8,128)(2,1)S(1)}, u32[]{:S(2)}, u32[]{:S(2)}) collective-permute-start(bf16[528,256]{1,0:T(8,128)(2,1)S(1)} %get-tuple-element.45.refs_4_), channel_id=1, source_target_pairs={{0,2},{2,0},{4,6},{6,4},{8,10},{10,8},{12,14},{14,12},{16,18},{18,... | collective-permute-start | bytes 811016 | tf_op jit(solution)/shard_map/ppermute | solution.py:19
  41.7 15.1 %collective-permute-start.18 = (bf16[256,128]{1,0:T(8,128)(2,1)S(1)}, bf16[256,128]{1,0:T(8,128)(2,1)S(1)}, u32[]{:S(2)}, u32[]{:S(2)}) collective-permute-start(bf16[256,128]{1,0:T(8,128)(2,1)S(1)} %get-tuple-element.19.refs_3_), channel_id=1, source_target_pairs={{0,1},{1,0},{2,3},{3,2},{4,5},{5,4},{6,7},{7,6},{8,9},{9,8},{10,11... | collective-permute-start | bytes 196616 | tf_op jit(solution)/shard_map/ppermute | solution.py:31
  49.9 7.0 %collective-permute-start.17 = (bf16[256,128]{1,0:T(8,128)(2,1)S(1)}, bf16[256,128]{1,0:T(8,128)(2,1)S(1)}, u32[]{:S(2)}, u32[]{:S(2)}) collective-permute-start(bf16[256,128]{1,0:T(8,128)(2,1)S(1)} %shard_map.84), channel_id=1, source_target_pairs={{0,48},{2,50},{4,52},{6,54},{8,56},{10,58},{12,60},{14,62},{16,32}... | collective-permute-start | bytes 196616 | tf_op jit(solution)/shard_map/ppermute | solution.py:19
  52.5 6.4 %collective-permute-start.16 = (bf16[256,128]{1,0:T(8,128)(2,1)S(1)}, bf16[256,128]{1,0:T(8,128)(2,1)S(1)}, u32[]{:S(2)}, u32[]{:S(2)}) collective-permute-start(bf16[256,128]{1,0:T(8,128)(2,1)S(1)} %shard_map.83), channel_id=1, source_target_pairs={{0,32},{2,34},{4,36},{6,38},{8,40},{10,42},{12,44},{14,46},{16,48}... | collective-permute-start | bytes 196616 | tf_op jit(solution)/shard_map/ppermute | solution.py:19
  53.8 5.1 %collective-permute-start.15 = (bf16[256,128]{1,0:T(8,128)(2,1)S(1)}, bf16[256,128]{1,0:T(8,128)(2,1)S(1)}, u32[]{:S(2)}, u32[]{:S(2)}) collective-permute-start(bf16[256,128]{1,0:T(8,128)(2,1)S(1)} %shard_map.82), channel_id=1, source_target_pairs={{0,16},{2,18},{4,20},{6,22},{8,24},{10,26},{12,28},{14,30},{16,0},... | collective-permute-start | bytes 196616 | tf_op jit(solution)/shard_map/ppermute | solution.py:19
  55.9 3.1 %copy-start = (f32[128,256]{1,0:T(8,128)S(1)}, f32[128,256]{1,0:T(8,128)}, u32[]{:S(2)}) copy-start(f32[128,256]{1,0:T(8,128)} %refs_5_.1) | copy-start | bytes 393220
  60.0 2.2 %collective-permute-start.20 = (f32[64,256]{1,0:T(8,128)S(1)}, f32[64,256]{1,0:T(8,128)S(1)}, u32[]{:S(2)}, u32[]{:S(2)}) collective-permute-start(f32[64,256]{1,0:T(8,128)S(1)} %get-tuple-element.23), channel_id=1, source_target_pairs={{0,2},{2,0},{4,6},{6,4},{8,10},{10,8},{12,14},{14,12},{16,18},{18,... | collective-permute-start | bytes 196616 | tf_op jit(solution)/shard_map/ppermute | solution.py:19
  61.3 8.6 %collective-permute-start.19 = (bf16[256,128]{1,0:T(8,128)(2,1)S(1)}, bf16[256,128]{1,0:T(8,128)(2,1)S(1)}, u32[]{:S(2)}, u32[]{:S(2)}) collective-permute-start(bf16[256,128]{1,0:T(8,128)(2,1)S(1)} %get-tuple-element.21), channel_id=1, source_target_pairs={{0,1},{1,0},{2,3},{3,2},{4,5},{5,4},{6,7},{7,6},{8,9},{9,8},{10,11... | collective-permute-start | bytes 196616 | tf_op jit(solution)/shard_map/ppermute | solution.py:31
  62.2 7.7 %collective-permute-start.21 = (f32[64,256]{1,0:T(8,128)S(1)}, f32[64,256]{1,0:T(8,128)S(1)}, u32[]{:S(2)}, u32[]{:S(2)}) collective-permute-start(f32[64,256]{1,0:T(8,128)S(1)} %add.83), channel_id=1, source_target_pairs={{0,4},{2,6},{4,0},{6,2},{8,12},{10,14},{12,8},{14,10},{16,20},{18,... | collective-permute-start | bytes 196616 | tf_op jit(solution)/shard_map/ppermute | solution.py:19
  62.3 7.6 %collective-permute-start.22 = (f32[64,256]{1,0:T(8,128)S(1)}, f32[64,256]{1,0:T(8,128)S(1)}, u32[]{:S(2)}, u32[]{:S(2)}) collective-permute-start(f32[64,256]{1,0:T(8,128)S(1)} %add.83), channel_id=1, source_target_pairs={{0,8},{2,10},{4,12},{6,14},{8,0},{10,2},{12,4},{14,6},{16,24},{18,... | collective-permute-start | bytes 196616 | tf_op jit(solution)/shard_map/ppermute | solution.py:19
  63.4 6.5 %collective-permute-start.23 = (f32[64,256]{1,0:T(8,128)S(1)}, f32[64,256]{1,0:T(8,128)S(1)}, u32[]{:S(2)}, u32[]{:S(2)}) collective-permute-start(f32[64,256]{1,0:T(8,128)S(1)} %add.83), channel_id=1, source_target_pairs={{0,12},{2,14},{4,8},{6,10},{8,4},{10,6},{12,0},{14,2},{16,28},{18,... | collective-permute-start | bytes 196616 | tf_op jit(solution)/shard_map/ppermute | solution.py:19
  70.0 3.9 %collective-permute-start.24 = (bf16[64,384]{1,0:T(8,128)(2,1)S(1)}, bf16[64,384]{1,0:T(8,128)(2,1)S(1)}, u32[]{:S(2)}, u32[]{:S(2)}) collective-permute-start(bf16[64,384]{1,0:T(8,128)(2,1)S(1)} %get-tuple-element.33), channel_id=1, source_target_pairs={{0,64},{2,66},{4,68},{6,70},{8,72},{10,74},{12,76},{14,78},{16,80}... | collective-permute-start | bytes 147464 | tf_op jit(solution)/shard_map/ppermute | solution.py:19
  70.1 4.5 %collective-permute-start.25 = (bf16[64,384]{1,0:T(8,128)(2,1)S(1)}, bf16[64,384]{1,0:T(8,128)(2,1)S(1)}, u32[]{:S(2)}, u32[]{:S(2)}) collective-permute-start(bf16[64,384]{1,0:T(8,128)(2,1)S(1)} %get-tuple-element.34), channel_id=1, source_target_pairs={{0,128},{2,130},{4,132},{6,134},{8,136},{10,138},{12,140},{14,142}... | collective-permute-start | bytes 147464 | tf_op jit(solution)/shard_map/ppermute | solution.py:19
  71.4 4.7 %collective-permute-start.26 = (bf16[64,384]{1,0:T(8,128)(2,1)S(1)}, bf16[64,384]{1,0:T(8,128)(2,1)S(1)}, u32[]{:S(2)}, u32[]{:S(2)}) collective-permute-start(bf16[64,384]{1,0:T(8,128)(2,1)S(1)} %get-tuple-element.35), channel_id=1, source_target_pairs={{0,192},{2,194},{4,196},{6,198},{8,200},{10,202},{12,204},{14,206}... | collective-permute-start | bytes 147464 | tf_op jit(solution)/shard_map/ppermute | solution.py:19
  76.2 3.9 %collective-permute-start.27 = (bf16[64,256]{1,0:T(8,128)(2,1)S(1)}, bf16[64,256]{1,0:T(8,128)(2,1)S(1)}, u32[]{:S(2)}, u32[]{:S(2)}) collective-permute-start(bf16[64,256]{1,0:T(8,128)(2,1)S(1)} %fusion.6), channel_id=1, source_target_pairs={{0,16},{2,18},{4,20},{6,22},{8,24},{10,26},{12,28},{14,30},{16,0},... | collective-permute-start | bytes 98312 | tf_op jit(solution)/shard_map/ppermute | solution.py:19
  77.9 3.8 %collective-permute-start.28 = (bf16[64,256]{1,0:T(8,128)(2,1)S(1)}, bf16[64,256]{1,0:T(8,128)(2,1)S(1)}, u32[]{:S(2)}, u32[]{:S(2)}) collective-permute-start(bf16[64,256]{1,0:T(8,128)(2,1)S(1)} %fusion.6), channel_id=1, source_target_pairs={{0,32},{2,34},{4,36},{6,38},{8,40},{10,42},{12,44},{14,46},{16,48}... | collective-permute-start | bytes 98312 | tf_op jit(solution)/shard_map/ppermute | solution.py:19
  77.9 4.6 %collective-permute-start.29 = (bf16[64,256]{1,0:T(8,128)(2,1)S(1)}, bf16[64,256]{1,0:T(8,128)(2,1)S(1)}, u32[]{:S(2)}, u32[]{:S(2)}) collective-permute-start(bf16[64,256]{1,0:T(8,128)(2,1)S(1)} %fusion.6), channel_id=1, source_target_pairs={{0,48},{2,50},{4,52},{6,54},{8,56},{10,58},{12,60},{14,62},{16,32}... | collective-permute-start | bytes 98312 | tf_op jit(solution)/shard_map/ppermute | solution.py:19
  82.5 4.9 %collective-permute-start.30 = (f32[64,256]{1,0:T(8,128)S(1)}, f32[64,256]{1,0:T(8,128)S(1)}, u32[]{:S(2)}, u32[]{:S(2)}) collective-permute-start(f32[64,256]{1,0:T(8,128)S(1)} %add_add_fusion), channel_id=1, source_target_pairs={{0,2},{2,0},{4,6},{6,4},{8,10},{10,8},{12,14},{14,12},{16,18},{18,... | collective-permute-start | bytes 196616 | tf_op jit(solution)/shard_map/ppermute | solution.py:19

commit v4 on v3

--- a/solution.py
+++ b/solution.py
@@ -60,36 +60,31 @@
     zero_ref[...] = jnp.zeros_like(zero_ref)
 
 
-def first_kernel(has_total, *refs):
-    rows_ref, term_ref, refs = refs[0], refs[1], refs[2:]
-    start, refs = (refs[0], refs[1:]) if has_total else (None, refs)
+def first_kernel(rows_ref, term_ref, *refs):
     packs, out, zero_ref = refs[:-2], refs[-2], refs[-1]
-    for m in range(4):
-        place = slice(256 * m, 256 * m + 256)
-        total = start[place, :] if has_total else jnp.zeros((256, 128), F32)
+    for place in (slice(0, 512), slice(512, 1024)):
+        total = jnp.zeros((512, 128), F32)
         for pack in packs:
             total = accumulate(total, rows_ref[place, :], term_ref[place, 0:1], pack)
         out[place, :] = total
     zero_ref[...] = jnp.zeros_like(zero_ref)
 
 
-def last_kernel(m, *refs):
-    rows_ref, term_ref, start, packs, out = refs[0], refs[1], refs[2], refs[3:-1], refs[-1]
-    place = slice(256 * m, 256 * m + 256)
+def last_kernel(first, rows_ref, term_ref, start, *refs):
+    packs, outs = refs[-8:-2], refs[-2:]
+    place = slice(256 * first, 256 * first + 512)
     total = start[place, :]
     for pack in packs:
         total = accumulate(total, rows_ref[place, :], term_ref[place, 0:1], pack)
-    out[...] = total.astype(out.dtype)
-
-
-def in_vmem(kernel, out, args, small=None, scratch=()):
-    spaces = [pltpu.VMEM] * len(args)
-    if small is not None:
-        spaces[small] = pltpu.SMEM
+    for m, out in enumerate(outs):
+        out[...] = total[256 * m : 256 * m + 256].astype(out.dtype)
+
+
+def in_vmem(kernel, out, args, scratch=()):
     return pl.pallas_call(
         kernel,
         out_shape=out,
-        in_specs=[pl.BlockSpec(memory_space=space) for space in spaces],
+        in_specs=[pl.BlockSpec(memory_space=pltpu.VMEM)] * len(args),
         scratch_shapes=scratch,
         out_specs=jax.tree.map(lambda _: pl.BlockSpec(memory_space=pltpu.VMEM), out),
         compiler_params=pltpu.CompilerParams(vmem_limit_bytes=8 * 2**20),
@@ -117,32 +112,35 @@
     )
 
 
-def cross_first(rows, term, total, packs):
-    has_total = total is not None
+def cross_first(rows, term, packs):
     return in_vmem(
-        functools.partial(first_kernel, has_total),
-        (jax.ShapeDtypeStruct((1024, 128), F32), ZEROS),
-        [rows, term] + ([total] if has_total else []) + list(packs),
-    )
-
-
-def cross_last(m, rows, term, total, packs, dtype):
-    return in_vmem(
-        functools.partial(last_kernel, m),
-        jax.ShapeDtypeStruct((256, 128), dtype),
-        [rows, term, total, *packs],
-    )
+        first_kernel, (jax.ShapeDtypeStruct((1024, 128), F32), ZEROS), [rows, term, *packs]
+    )
+
+
+def cross_last(first, rows, term, total, packs, earlier=()):
+    outs = [jax.ShapeDtypeStruct((256, 128), BF16 if m else F32) for m in (first, first + 1)]
+    args = [rows, term, total, *earlier, *packs]
+    return in_vmem(functools.partial(last_kernel, first), outs, args)
 
 
 def gate_kernel(value_ref, _, out_ref):
     out_ref[...] = value_ref[...]
 
 
-def grad_kernel(place_ref, own, *refs):
+def halves_kernel(right_ref, left_ref, *refs):
+    upper_ref, lower_ref, zero_ref = refs[-3:]
+    zero_ref[...] = jnp.zeros_like(zero_ref)
+    upper_ref[...] = right_ref[0:528, :]
+    lower_ref[...] = left_ref[528:1056, :]
+
+
+def grad_kernel(own, *refs):
     back, near, far, cov_ref = refs[:3], refs[3], refs[4], refs[5]
     mixed_ref, mixed_far_ref, grad_ref, grad_far_ref, held = refs[6:]
-    own_columns = pl.ds(pl.multiple_of(place_ref[0] * 128, 128), 128)
-    far_columns = pl.ds(pl.multiple_of(128 - place_ref[0] * 128, 128), 128)
+    lab, core = lax.axis_index("lab"), lax.axis_index("pts") & 1
+    own_columns = pl.ds(pl.multiple_of(lab * 128, 128), 128)
+    far_columns = pl.ds(pl.multiple_of(128 - lab * 128, 128), 128)
     turned = (((0,), (0,)), ((), ()))
     one, two, three = (b[...].astype(F32) for b in back)
     cross = (own[...] + one) + (two + three)
@@ -155,13 +153,17 @@
         held[:, columns] = lax.dot_general(
             high, cot, turned, preferred_element_type=F32
         ) + lax.dot_general(rest, cot, turned, preferred_element_type=F32)
-    core = place_ref[1]
     grad_ref[...] = held[pl.ds(pl.multiple_of(core * 64, 64), 64), :]
     grad_far_ref[...] = held[pl.ds(pl.multiple_of(64 - core * 64, 64), 64), :]
 
 
+def join_kernel(own_ref, other_ref, out_ref):
+    core = lax.axis_index("pts") & 1
+    out_ref[pl.ds(pl.multiple_of(core * 64, 64), 64), :] = own_ref[...]
+    out_ref[pl.ds(pl.multiple_of(64 - core * 64, 64), 64), :] = other_ref[...]
+
+
 def local(slab_points, key_points, length_weights, adjoint, label_cov, cotangent):
-    core, lab = lax.axis_index("pts") & 1, lax.axis_index("lab")
 
     keys = key_points.astype(F32)
     scaled = (keys * length_weights * (1.0 / 32.0)).astype(BF16)
@@ -178,31 +180,25 @@
         halves += [both[h], parts]
     pack = jnp.concatenate(halves, axis=0)
 
-    right = swap_ring(pack, X, 1)
-    left = swap_ring(pack, X, 3)
+    right, left = swap_ring(pack, X, 1), swap_ring(pack, X, 3)
     own_far = swap(pack, CORE, 1)
 
     own = in_vmem(gate_kernel, jax.ShapeDtypeStruct((64, 128), BF16), [slab_points, own_far])
     part = jnp.concatenate([own] + [swap(own, Z, m) for m in (1, 2, 3)] + [cotangent], axis=0)
-    rows, term, cot, zeros = prepare(
-        length_weights, [part] + [swap(part, Y, m) for m in (1, 2, 3)]
-    )
-
-    right, left = right + zeros[0:1], left + zeros[0:1]
-    upper = swap_ring(right[:528], X, 1)
-    lower = swap_ring(left[528:], X, 3)
-    right_far, left_far = swap(right, CORE, 1), swap(left, CORE, 1)
+    parts = [part] + [swap(part, Y, m) for m in (1, 2, 3)]
+    rows, term, cot, _ = prepare(length_weights, parts)
+
+    half = jax.ShapeDtypeStruct((528, 256), BF16)
+    upper, lower, zeros = in_vmem(halves_kernel, (half, half, ZEROS), [right, left, parts[1]])
+    upper, lower = swap_ring(upper, X, 1), swap_ring(lower, X, 3)
+    right_far, left_far = swap(right + zeros[0:1], CORE, 1), swap(left + zeros[0:1], CORE, 1)
+
+    total, zeros = cross_first(rows, term, [pack, own_far, right, left])
+    upper, lower = upper + zeros[0:1], lower + zeros[0:1]
     cot_far = swap_lab(cot)
-
-    total, zeros = cross_first(rows, term, None, [pack, own_far, right, right_far])
-    upper, lower = upper + zeros[0:1], lower + zeros[0:1]
-    upper_far, lower_far = swap(upper, CORE, 1), swap(lower, CORE, 1)
-    total, _ = cross_first(rows, term, total, [left, left_far])
-    packs = [upper, lower, upper_far, lower_far]
-    sent = {
-        m: cross_last(m, rows, term, total, packs, F32 if m == 0 else BF16)
-        for m in (2, 1, 3, 0)
-    }
+    packs = [right_far, left_far, upper, lower, swap(upper, CORE, 1), swap(lower, CORE, 1)]
+    sent = cross_last(2, rows, term, total, packs)
+    sent = cross_last(0, rows, term, total, packs, sent[:1]) + sent
     back = [swap(sent[m], Z, m) for m in (1, 2, 3)]
 
     mixed, mixed_far, grad, grad_far = in_vmem(
@@ -213,14 +209,16 @@
             jax.ShapeDtypeStruct((64, 256), F32),
             jax.ShapeDtypeStruct((64, 256), F32),
         ),
-        [jnp.stack([lab, core]), sent[0], *back, cot, cot_far, label_cov],
-        small=0,
+        [sent[0], *back, cot, cot_far, label_cov],
         scratch=[pltpu.VMEM((128, 256), F32)],
     )
     mixed = mixed + swap_lab(mixed_far).astype(F32)
     grad = grad + swap(grad_far, CORE, 1)
     back = [swap(grad, X, m) for m in (1, 2, 3)]
     grad = ((grad + back[0]) + (back[1] + back[2])).astype(BF16)
+
+    back = [swap(grad, Z, m).astype(F32) for m in (1, 2, 3)]
+    grad = ((grad.astype(F32) + back[0]) + (back[1] + back[2])).astype(BF16)
 
     back = [
         swap(
@@ -230,15 +228,9 @@
     ]
     mixed = (mixed[:64] + back[0][:, :128]) + (back[1][:, :128] + back[2][:, :128])
     back = [b[:, 128:] for b in back]
-    grad = ((grad.astype(F32) + back[0]) + (back[1] + back[2])).astype(BF16)
-
-    back = [swap(grad, Z, m).astype(F32) for m in (1, 2, 3)]
     grad = (grad.astype(F32) + back[0]) + (back[1] + back[2])
-    other = swap(grad, CORE, 1)
-    grad = jnp.where(
-        core == 0,
-        jnp.concatenate([grad, other], axis=0),
-        jnp.concatenate([other, grad], axis=0),
+    grad = in_vmem(
+        join_kernel, jax.ShapeDtypeStruct((128, 256), F32), [grad, swap(grad, CORE, 1)]
     )
     return mixed.astype(BF16), grad
 

time: 88.2 us -> 81 us (0.918)
  waiting for transfers between devices: 23.7 us -> 20.9 us
  starting transfers between devices: 46.7 us -> 44.8 us
  Pallas kernels: 13.3 us -> 11.6 us
    ppermute x25, starting transfers between devices: 37.1 us -> 33.7 us  [swap(): lax.ppermute(value, 'pts', [(i, i ^ mask << place) for i in range(PTS)])]
    ppermute x25, waiting for transfers between devices: 16.9 us -> 14.4 us  [swap(): lax.ppermute(value, 'pts', [(i, i ^ mask << place) for i in range(PTS)])]
    ppermute x2, starting transfers between devices: 5.07 us -> 6.83 us  [swap_lab(): return lax.ppermute(value, 'lab', [(0, 1), (1, 0)])]
    pallas_call x9 -> x8, Pallas kernels: 13.3 us -> 11.6 us  [in_vmem(): pl.pallas_call(kernel, out_shape=out, in_specs=[pl.BlockSpec(memory_space...]
    ppermute x4, waiting for transfers between devices: 3.07 us -> 1.57 us  [swap_ring(): return lax.ppermute(value, 'pts', pairs)]
    ppermute x2, waiting for transfers between devices: 3.7 us -> 4.98 us  [swap_lab(): return lax.ppermute(value, 'lab', [(0, 1), (1, 0)])]
  transfers between devices with their start and end apart: 31 -> 31, of which waited for: 13 -> 12; matrix products, arithmetic and copies ran while one was open for 1% -> 1% of each run, Pallas kernels for 14% -> 13%
where the time goes in v4:
time: 81 us; the launch traced here: 80.8 us
  starting transfers between devices  44.8 us (55%)
  waiting for transfers between devices  20.9 us (26%)
  Pallas kernels  11.6 us (14%)
  other arithmetic  2.14 us (3%)
  between operations  0.92 us (1%)
    ppermute x25, starting transfers between devices, swap(): lax.ppermute(value, 'pts', [(i, i ^ mask << place) for i in range(PTS)])  33.7 us
    ppermute x25, waiting for transfers between devices, swap(): lax.ppermute(value, 'pts', [(i, i ^ mask << place) for i in range(PTS)])  14.4 us
    pallas_call x8, Pallas kernels, in_vmem(): pl.pallas_call(kernel, out_shape=out, in_specs=[pl.BlockSpec(memory_space...  11.6 us
    ppermute x2, starting transfers between devices, swap_lab(): return lax.ppermute(value, 'lab', [(0, 1), (1, 0)])  6.83 us
    ppermute x2, waiting for transfers between devices, swap_lab(): return lax.ppermute(value, 'lab', [(0, 1), (1, 0)])  4.98 us
    ppermute x4, starting transfers between devices, swap_ring(): return lax.ppermute(value, 'pts', pairs)  4.22 us
  transfers between devices with their start and end apart: 31, of which 12 were waited for; matrix products, arithmetic and copies ran while one was open for 1% of the time, Pallas kernels for 13%

profile of v4, /device:TPU:1, one launch (start us, length us, event | category | flops | bytes accessed | tf_op | source)
XLA Modules:
  0.0 80.8 jit_solution(1959640234839127343)
XLA Ops:
  0.6 1.2 %fusion.3 = (f32[1024]{0:T(1024)S(1)}, bf16[1024,128]{1,0:T(8,128)(2,1)S(1)}) fusion(bf16[1024,128]{1,0:T(8,128)(2,1)} %param.7, f32[128]{0:T(128)} %weights_ref.1), kind=kLoop, calls=%fused_computation.5 | loop fusion | flops 916480 | bytes 528896 | tf_op jit(solution)/shard_map/reduce_sum | solution.py:170
  2.0 0.3 concatenate.24.refs_0_
  2.3 3.3 %collective-permute-start = (bf16[1056,256]{1,0:T(8,128)(2,1)S(1)}, bf16[1056,256]{1,0:T(8,128)(2,1)S(1)}, u32[]{:S(2)}, u32[]{:S(2)}) collective-permute-start(bf16[1056,256]{1,0:T(8,128)(2,1)S(1)} %concatenate.24.refs_0_), channel_id=1, source_target_pairs={{0,2},{2,0},{4,6},{6,4},{8,10},{10,8},{12,14},{14,12},{16,18},{18,... | collective-permute-start | bytes 1622024 | tf_op jit(solution)/shard_map/ppermute | solution.py:19
  5.6 0.8 collective-permute-start.7
  6.4 0.7 collective-permute-start.8
  7.1 0.1 collective-permute-done._.refs_1_
  7.2 0.9 %collective-permute-start.1 = (bf16[64,128]{1,0:T(8,128)(2,1)S(1)}, bf16[64,128]{1,0:T(8,128)(2,1)S(1)}, u32[]{:S(2)}, u32[]{:S(2)}) collective-permute-start(bf16[64,128]{1,0:T(8,128)(2,1)S(1)} %shard_map.77), channel_id=1, source_target_pairs={{0,16},{2,18},{4,20},{6,22},{8,24},{10,26},{12,28},{14,30},{16,0},... | collective-permute-start | bytes 49160 | tf_op jit(solution)/shard_map/ppermute | solution.py:19
  8.1 3.0 %collective-permute-start.2 = (bf16[64,128]{1,0:T(8,128)(2,1)S(1)}, bf16[64,128]{1,0:T(8,128)(2,1)S(1)}, u32[]{:S(2)}, u32[]{:S(2)}) collective-permute-start(bf16[64,128]{1,0:T(8,128)(2,1)S(1)} %shard_map.77), channel_id=1, source_target_pairs={{0,32},{2,34},{4,36},{6,38},{8,40},{10,42},{12,44},{14,46},{16,48}... | collective-permute-start | bytes 49160 | tf_op jit(solution)/shard_map/ppermute | solution.py:19
  11.1 1.5 %collective-permute-done.2 = bf16[64,128]{1,0:T(8,128)(2,1)S(1)} collective-permute-done((bf16[64,128]{1,0:T(8,128)(2,1)S(1)}, bf16[64,128]{1,0:T(8,128)(2,1)S(1)}, u32[]{:S(2)}, u32[]{:S(2)}) %collective-permute-start.2) | collective-permute-done | bytes 16416 | tf_op jit(solution)/shard_map/ppermute | solution.py:19
  12.6 2.9 %collective-permute-done.3 = bf16[64,128]{1,0:T(8,128)(2,1)S(1)} collective-permute-done((bf16[64,128]{1,0:T(8,128)(2,1)S(1)}, bf16[64,128]{1,0:T(8,128)(2,1)S(1)}, u32[]{:S(2)}, u32[]{:S(2)}) %collective-permute-start.3) | collective-permute-done | bytes 16416 | tf_op jit(solution)/shard_map/ppermute | solution.py:19
  15.5 1.4 %collective-permute-start.4 = (bf16[320,128]{1,0:T(8,128)(2,1)S(1)}, bf16[320,128]{1,0:T(8,128)(2,1)S(1)}, u32[]{:S(2)}, u32[]{:S(2)}) collective-permute-start(bf16[320,128]{1,0:T(8,128)(2,1)S(1)} %constant_dynamic-update-slice_fusion.refs_0_), channel_id=1, source_target_pairs={{0,64},{2,66},{4,68},{6,70},{8,72},{10,74},{12,76},{14,78},{16,80}... | collective-permute-start | bytes 245768 | tf_op jit(solution)/shard_map/ppermute | solution.py:19
  16.9 2.6 %collective-permute-start.5 = (bf16[320,128]{1,0:T(8,128)(2,1)S(1)}, bf16[320,128]{1,0:T(8,128)(2,1)S(1)}, u32[]{:S(2)}, u32[]{:S(2)}) collective-permute-start(bf16[320,128]{1,0:T(8,128)(2,1)S(1)} %constant_dynamic-update-slice_fusion.refs_0_), channel_id=1, source_target_pairs={{0,128},{2,130},{4,132},{6,134},{8,136},{10,138},{12,140},{14,142}... | collective-permute-start | bytes 245768 | tf_op jit(solution)/shard_map/ppermute | solution.py:19
  19.5 1.6 %collective-permute-done.8.refs_3_.left_ref = bf16[1056,256]{1,0:T(8,128)(2,1)S(1)} collective-permute-done((bf16[1056,256]{1,0:T(8,128)(2,1)S(1)}, bf16[1056,256]{1,0:T(8,128)(2,1)S(1)}, u32[]{:S(2)}, u32[]{:S(2)}) %collective-permute-start.8) | collective-permute-done | bytes 540704 | tf_op jit(solution)/shard_map/ppermute | solution.py:27
  21.2 2.7 %collective-permute-start.11 = (bf16[528,256]{1,0:T(8,128)(2,1)S(1)}, bf16[528,256]{1,0:T(8,128)(2,1)S(1)}, u32[]{:S(2)}, u32[]{:S(2)}) collective-permute-start(bf16[528,256]{1,0:T(8,128)(2,1)S(1)} %get-tuple-element.22), channel_id=1, source_target_pairs={{0,12},{2,14},{4,0},{6,2},{8,4},{10,6},{12,8},{14,10},{16,28},{18,... | collective-permute-start | bytes 811016 | tf_op jit(solution)/shard_map/ppermute | solution.py:27
  24.0 2.3 %collective-permute-start.9 = (bf16[1056,256]{1,0:T(8,128)(2,1)S(1)}, bf16[1056,256]{1,0:T(8,128)(2,1)S(1)}, u32[]{:S(2)}, u32[]{:S(2)}) collective-permute-start(bf16[1056,256]{1,0:T(8,128)(2,1)S(1)} %get-tuple-element.58), channel_id=1, source_target_pairs={{0,2},{2,0},{4,6},{6,4},{8,10},{10,8},{12,14},{14,12},{16,18},{18,... | collective-permute-start | bytes 1622024 | tf_op jit(solution)/shard_map/ppermute | solution.py:19
  26.3 0.3 collective-permute-start.10
  26.6 0.7 shard_map.78
  27.4 4.8 %shard_map.79 = (f32[1024,128]{1,0:T(8,128)S(1)}, bf16[16,256]{1,0:T(8,128)(2,1)S(1)}) custom-call(bf16[1024,128]{1,0:T(8,128)(2,1)S(1)} %get-tuple-element.18.rows_ref, f32[1024,128]{1,0:T(8,128)S(1)} %get-tuple-element.19.term_ref, bf16[1056,256]{1,0:T(8,128)(2,1)S(1)} %concatenate.24.refs_0_, bf16[1056,256]{1,0:T(8,128)(2,1)S(1)} %collective-permute-done._.refs_1_, ...), custom_call_target="tpu_custom_call" | custom-call | flops 1000 | bytes 2097152 | tf_op jit(solution)/shard_map/pallas_call | solution.py:84
  32.3 1.3 %collective-permute-start.13 = (bf16[528,256]{1,0:T(8,128)(2,1)S(1)}, bf16[528,256]{1,0:T(8,128)(2,1)S(1)}, u32[]{:S(2)}, u32[]{:S(2)}) collective-permute-start(bf16[528,256]{1,0:T(8,128)(2,1)S(1)} %get-tuple-element.56.refs_2_.refs_3_), channel_id=1, source_target_pairs={{0,2},{2,0},{4,6},{6,4},{8,10},{10,8},{12,14},{14,12},{16,18},{18,... | collective-permute-start | bytes 811016 | tf_op jit(solution)/shard_map/ppermute | solution.py:19
  33.5 0.1 collective-permute-start.14
  33.6 5.6 %collective-permute-start.18 = (bf16[256,128]{1,0:T(8,128)(2,1)S(1)}, bf16[256,128]{1,0:T(8,128)(2,1)S(1)}, u32[]{:S(2)}, u32[]{:S(2)}) collective-permute-start(bf16[256,128]{1,0:T(8,128)(2,1)S(1)} %get-tuple-element.29.refs_3_), channel_id=1, source_target_pairs={{0,1},{1,0},{2,3},{3,2},{4,5},{5,4},{6,7},{7,6},{8,9},{9,8},{10,11... | collective-permute-start | bytes 196616 | tf_op jit(solution)/shard_map/ppermute | solution.py:31
  39.3 2.5 %shard_map.81 = (bf16[256,128]{1,0:T(8,128)(2,1)S(1)}, bf16[256,128]{1,0:T(8,128)(2,1)S(1)}) custom-call(bf16[1024,128]{1,0:T(8,128)(2,1)S(1)} %get-tuple-element.18.rows_ref, f32[1024,128]{1,0:T(8,128)S(1)} %get-tuple-element.19.term_ref, f32[1024,128]{1,0:T(8,128)S(1)} %get-tuple-element.20.start, ...), custom_call_target="tpu_custom_call" | custom-call | flops 1000 | bytes 2097152 | tf_op jit(solution)/shard_map/pallas_call | solution.py:84
  41.8 1.5 %collective-permute-start.16 = (bf16[256,128]{1,0:T(8,128)(2,1)S(1)}, bf16[256,128]{1,0:T(8,128)(2,1)S(1)}, u32[]{:S(2)}, u32[]{:S(2)}) collective-permute-start(bf16[256,128]{1,0:T(8,128)(2,1)S(1)} %get-tuple-element.25.refs_0_), channel_id=1, source_target_pairs={{0,32},{2,34},{4,36},{6,38},{8,40},{10,42},{12,44},{14,46},{16,48}... | collective-permute-start | bytes 196616 | tf_op jit(solution)/shard_map/ppermute | solution.py:19
  43.3 2.5 %shard_map.82 = (f32[256,128]{1,0:T(8,128)S(1)}, bf16[256,128]{1,0:T(8,128)(2,1)S(1)}) custom-call(bf16[1024,128]{1,0:T(8,128)(2,1)S(1)} %get-tuple-element.18.rows_ref, f32[1024,128]{1,0:T(8,128)S(1)} %get-tuple-element.19.term_ref, f32[1024,128]{1,0:T(8,128)S(1)} %get-tuple-element.20.start, bf16[256,128]{1,0:T(8,128)(2,1)S(1)} %get-tuple-element.25.refs_0_, ...), custom_call_target="tpu_custom_call" | custom-call | flops 1000 | bytes 2097152 | tf_op jit(solution)/shard_map/pallas_call | solution.py:84
  45.7 0.8 %collective-permute-start.15 = (bf16[256,128]{1,0:T(8,128)(2,1)S(1)}, bf16[256,128]{1,0:T(8,128)(2,1)S(1)}, u32[]{:S(2)}, u32[]{:S(2)}) collective-permute-start(bf16[256,128]{1,0:T(8,128)(2,1)S(1)} %get-tuple-element.27), channel_id=1, source_target_pairs={{0,16},{2,18},{4,20},{6,22},{8,24},{10,26},{12,28},{14,30},{16,0},... | collective-permute-start | bytes 196616 | tf_op jit(solution)/shard_map/ppermute | solution.py:19
  46.6 1.6 %collective-permute-start.17 = (bf16[256,128]{1,0:T(8,128)(2,1)S(1)}, bf16[256,128]{1,0:T(8,128)(2,1)S(1)}, u32[]{:S(2)}, u32[]{:S(2)}) collective-permute-start(bf16[256,128]{1,0:T(8,128)(2,1)S(1)} %get-tuple-element.28), channel_id=1, source_target_pairs={{0,48},{2,50},{4,52},{6,54},{8,56},{10,58},{12,60},{14,62},{16,32}... | collective-permute-start | bytes 196616 | tf_op jit(solution)/shard_map/ppermute | solution.py:19
  48.2 0.8 collective-permute-done.15.refs_0_
  48.9 3.0 %collective-permute-done.17.refs_2_ = bf16[256,128]{1,0:T(8,128)(2,1)S(1)} collective-permute-done((bf16[256,128]{1,0:T(8,128)(2,1)S(1)}, bf16[256,128]{1,0:T(8,128)(2,1)S(1)}, u32[]{:S(2)}, u32[]{:S(2)}) %collective-permute-start.17) | collective-permute-done | bytes 65568 | tf_op jit(solution)/shard_map/ppermute | solution.py:19
  51.9 0.5 shard_map.83
  52.4 1.9 %collective-permute-start.20 = (f32[64,256]{1,0:T(8,128)S(1)}, f32[64,256]{1,0:T(8,128)S(1)}, u32[]{:S(2)}, u32[]{:S(2)}) collective-permute-start(f32[64,256]{1,0:T(8,128)S(1)} %get-tuple-element.33), channel_id=1, source_target_pairs={{0,2},{2,0},{4,6},{6,4},{8,10},{10,8},{12,14},{14,12},{16,18},{18,... | collective-permute-start | bytes 196616 | tf_op jit(solution)/shard_map/ppermute | solution.py:19
  54.3 1.2 %collective-permute-start.19 = (bf16[256,128]{1,0:T(8,128)(2,1)S(1)}, bf16[256,128]{1,0:T(8,128)(2,1)S(1)}, u32[]{:S(2)}, u32[]{:S(2)}) collective-permute-start(bf16[256,128]{1,0:T(8,128)(2,1)S(1)} %get-tuple-element.31), channel_id=1, source_target_pairs={{0,1},{1,0},{2,3},{3,2},{4,5},{5,4},{6,7},{7,6},{8,9},{9,8},{10,11... | collective-permute-start | bytes 196616 | tf_op jit(solution)/shard_map/ppermute | solution.py:31
  55.5 0.7 collective-permute-start.22
  56.2 1.5 %collective-permute-start.23 = (f32[64,256]{1,0:T(8,128)S(1)}, f32[64,256]{1,0:T(8,128)S(1)}, u32[]{:S(2)}, u32[]{:S(2)}) collective-permute-start(f32[64,256]{1,0:T(8,128)S(1)} %add.83), channel_id=1, source_target_pairs={{0,12},{2,14},{4,8},{6,10},{8,4},{10,6},{12,0},{14,2},{16,28},{18,... | collective-permute-start | bytes 196616 | tf_op jit(solution)/shard_map/ppermute | solution.py:19
  57.7 0.5 collective-permute-start.21
  58.2 5.0 %collective-permute-done.19 = bf16[256,128]{1,0:T(8,128)(2,1)S(1)} collective-permute-done((bf16[256,128]{1,0:T(8,128)(2,1)S(1)}, bf16[256,128]{1,0:T(8,128)(2,1)S(1)}, u32[]{:S(2)}, u32[]{:S(2)}) %collective-permute-start.19) | collective-permute-done | bytes 65568 | tf_op jit(solution)/shard_map/ppermute | solution.py:31
  63.3 0.9 %collective-permute-start.26 = (bf16[64,256]{1,0:T(8,128)(2,1)S(1)}, bf16[64,256]{1,0:T(8,128)(2,1)S(1)}, u32[]{:S(2)}, u32[]{:S(2)}) collective-permute-start(bf16[64,256]{1,0:T(8,128)(2,1)S(1)} %add_convert_fusion.1), channel_id=1, source_target_pairs={{0,48},{2,50},{4,52},{6,54},{8,56},{10,58},{12,60},{14,62},{16,32}... | collective-permute-start | bytes 98312 | tf_op jit(solution)/shard_map/ppermute | solution.py:19
  64.2 2.8 %collective-permute-start.24 = (bf16[64,256]{1,0:T(8,128)(2,1)S(1)}, bf16[64,256]{1,0:T(8,128)(2,1)S(1)}, u32[]{:S(2)}, u32[]{:S(2)}) collective-permute-start(bf16[64,256]{1,0:T(8,128)(2,1)S(1)} %add_convert_fusion.1), channel_id=1, source_target_pairs={{0,16},{2,18},{4,20},{6,22},{8,24},{10,26},{12,28},{14,30},{16,0},... | collective-permute-start | bytes 98312 | tf_op jit(solution)/shard_map/ppermute | solution.py:19
  66.9 1.1 %collective-permute-done.26 = bf16[64,256]{1,0:T(8,128)(2,1)S(1)} collective-permute-done((bf16[64,256]{1,0:T(8,128)(2,1)S(1)}, bf16[64,256]{1,0:T(8,128)(2,1)S(1)}, u32[]{:S(2)}, u32[]{:S(2)}) %collective-permute-start.26) | collective-permute-done | bytes 32800 | tf_op jit(solution)/shard_map/ppermute | solution.py:19
  68.1 1.0 %collective-permute-done.25 = bf16[64,256]{1,0:T(8,128)(2,1)S(1)} collective-permute-done((bf16[64,256]{1,0:T(8,128)(2,1)S(1)}, bf16[64,256]{1,0:T(8,128)(2,1)S(1)}, u32[]{:S(2)}, u32[]{:S(2)}) %collective-permute-start.25) | collective-permute-done | bytes 32800 | tf_op jit(solution)/shard_map/ppermute | solution.py:19
  69.1 2.8 %collective-permute-start.29 = (bf16[64,384]{1,0:T(8,128)(2,1)S(1)}, bf16[64,384]{1,0:T(8,128)(2,1)S(1)}, u32[]{:S(2)}, u32[]{:S(2)}) collective-permute-start(bf16[64,384]{1,0:T(8,128)(2,1)S(1)} %get-tuple-element.45), channel_id=1, source_target_pairs={{0,192},{2,194},{4,196},{6,198},{8,200},{10,202},{12,204},{14,206}... | collective-permute-start | bytes 147464 | tf_op jit(solution)/shard_map/ppermute | solution.py:19
  71.9 0.3 collective-permute-start.28
  72.3 0.3 collective-permute-start.27
  72.6 0.8 collective-permute-done.29
  73.4 3.0 %collective-permute-done.28 = bf16[64,384]{1,0:T(8,128)(2,1)S(1)} collective-permute-done((bf16[64,384]{1,0:T(8,128)(2,1)S(1)}, bf16[64,384]{1,0:T(8,128)(2,1)S(1)}, u32[]{:S(2)}, u32[]{:S(2)}) %collective-permute-start.28) | collective-permute-done | bytes 49184 | tf_op jit(solution)/shard_map/ppermute | solution.py:19
  76.4 2.8 %collective-permute-start.30 = (f32[64,256]{1,0:T(8,128)S(1)}, f32[64,256]{1,0:T(8,128)S(1)}, u32[]{:S(2)}, u32[]{:S(2)}) collective-permute-start(f32[64,256]{1,0:T(8,128)S(1)} %fusion.5.own_ref), channel_id=1, source_target_pairs={{0,2},{2,0},{4,6},{6,4},{8,10},{10,8},{12,14},{14,12},{16,18},{18,... | collective-permute-start | bytes 196616 | tf_op jit(solution)/shard_map/ppermute | solution.py:19
  79.2 0.6 fusion.7
  79.8 0.3 collective-permute-done.30.other_ref
  80.1 0.7 shard_map.84
  (62 shorter events, 0.6 us)
Async XLA Ops:
  0.6 1.3 %copy-start.3 = (bf16[1024,128]{1,0:T(8,128)(2,1)S(1)}, bf16[1024,128]{1,0:T(8,128)(2,1)}, u32[]{:S(2)}) copy-start(bf16[1024,128]{1,0:T(8,128)(2,1)} %param.9) | copy-start | bytes 786436
  2.0 5.2 %copy-start.1 = (bf16[64,128]{1,0:T(8,128)(2,1)S(1)}, bf16[64,128]{1,0:T(8,128)(2,1)}, u32[]{:S(2)}) copy-start(bf16[64,128]{1,0:T(8,128)(2,1)} %value_ref.1) | copy-start | bytes 49156
  2.3 4.9 %collective-permute-start = (bf16[1056,256]{1,0:T(8,128)(2,1)S(1)}, bf16[1056,256]{1,0:T(8,128)(2,1)S(1)}, u32[]{:S(2)}, u32[]{:S(2)}) collective-permute-start(bf16[1056,256]{1,0:T(8,128)(2,1)S(1)} %concatenate.24.refs_0_), channel_id=1, source_target_pairs={{0,2},{2,0},{4,6},{6,4},{8,10},{10,8},{12,14},{14,12},{16,18},{18,... | collective-permute-start | bytes 1622024 | tf_op jit(solution)/shard_map/ppermute | solution.py:19
  5.6 13.9 %collective-permute-start.7 = (bf16[1056,256]{1,0:T(8,128)(2,1)S(1)}, bf16[1056,256]{1,0:T(8,128)(2,1)S(1)}, u32[]{:S(2)}, u32[]{:S(2)}) collective-permute-start(bf16[1056,256]{1,0:T(8,128)(2,1)S(1)} %concatenate.24.refs_0_), channel_id=1, source_target_pairs={{0,12},{2,14},{4,0},{6,2},{8,4},{10,6},{12,8},{14,10},{16,28},{18,... | collective-permute-start | bytes 1622024 | tf_op jit(solution)/shard_map/ppermute | solution.py:27
  6.4 14.7 %collective-permute-start.8 = (bf16[1056,256]{1,0:T(8,128)(2,1)S(1)}, bf16[1056,256]{1,0:T(8,128)(2,1)S(1)}, u32[]{:S(2)}, u32[]{:S(2)}) collective-permute-start(bf16[1056,256]{1,0:T(8,128)(2,1)S(1)} %concatenate.24.refs_0_), channel_id=1, source_target_pairs={{0,4},{2,6},{4,8},{6,10},{8,12},{10,14},{12,0},{14,2},{16,20},{18,... | collective-permute-start | bytes 1622024 | tf_op jit(solution)/shard_map/ppermute | solution.py:27
  7.2 3.9 %collective-permute-start.1 = (bf16[64,128]{1,0:T(8,128)(2,1)S(1)}, bf16[64,128]{1,0:T(8,128)(2,1)S(1)}, u32[]{:S(2)}, u32[]{:S(2)}) collective-permute-start(bf16[64,128]{1,0:T(8,128)(2,1)S(1)} %shard_map.77), channel_id=1, source_target_pairs={{0,16},{2,18},{4,20},{6,22},{8,24},{10,26},{12,28},{14,30},{16,0},... | collective-permute-start | bytes 49160 | tf_op jit(solution)/shard_map/ppermute | solution.py:19
  8.1 4.5 %collective-permute-start.2 = (bf16[64,128]{1,0:T(8,128)(2,1)S(1)}, bf16[64,128]{1,0:T(8,128)(2,1)S(1)}, u32[]{:S(2)}, u32[]{:S(2)}) collective-permute-start(bf16[64,128]{1,0:T(8,128)(2,1)S(1)} %shard_map.77), channel_id=1, source_target_pairs={{0,32},{2,34},{4,36},{6,38},{8,40},{10,42},{12,44},{14,46},{16,48}... | collective-permute-start | bytes 49160 | tf_op jit(solution)/shard_map/ppermute | solution.py:19
  11.1 4.4 %collective-permute-start.3 = (bf16[64,128]{1,0:T(8,128)(2,1)S(1)}, bf16[64,128]{1,0:T(8,128)(2,1)S(1)}, u32[]{:S(2)}, u32[]{:S(2)}) collective-permute-start(bf16[64,128]{1,0:T(8,128)(2,1)S(1)} %shard_map.77), channel_id=1, source_target_pairs={{0,48},{2,50},{4,52},{6,54},{8,56},{10,58},{12,60},{14,62},{16,32}... | collective-permute-start | bytes 49160 | tf_op jit(solution)/shard_map/ppermute | solution.py:19
  12.6 2.9 %copy-start.4 = (bf16[64,128]{1,0:T(8,128)(2,1)S(1)}, bf16[64,128]{1,0:T(8,128)(2,1)}, u32[]{:S(2)}) copy-start(bf16[64,128]{1,0:T(8,128)(2,1)} %param.11) | copy-start | bytes 49156
  15.5 5.6 %collective-permute-start.4 = (bf16[320,128]{1,0:T(8,128)(2,1)S(1)}, bf16[320,128]{1,0:T(8,128)(2,1)S(1)}, u32[]{:S(2)}, u32[]{:S(2)}) collective-permute-start(bf16[320,128]{1,0:T(8,128)(2,1)S(1)} %constant_dynamic-update-slice_fusion.refs_0_), channel_id=1, source_target_pairs={{0,64},{2,66},{4,68},{6,70},{8,72},{10,74},{12,76},{14,78},{16,80}... | collective-permute-start | bytes 245768 | tf_op jit(solution)/shard_map/ppermute | solution.py:19
  16.9 9.4 %collective-permute-start.5 = (bf16[320,128]{1,0:T(8,128)(2,1)S(1)}, bf16[320,128]{1,0:T(8,128)(2,1)S(1)}, u32[]{:S(2)}, u32[]{:S(2)}) collective-permute-start(bf16[320,128]{1,0:T(8,128)(2,1)S(1)} %constant_dynamic-update-slice_fusion.refs_0_), channel_id=1, source_target_pairs={{0,128},{2,130},{4,132},{6,134},{8,136},{10,138},{12,140},{14,142}... | collective-permute-start | bytes 245768 | tf_op jit(solution)/shard_map/ppermute | solution.py:19
  19.5 7.1 %collective-permute-start.6 = (bf16[320,128]{1,0:T(8,128)(2,1)S(1)}, bf16[320,128]{1,0:T(8,128)(2,1)S(1)}, u32[]{:S(2)}, u32[]{:S(2)}) collective-permute-start(bf16[320,128]{1,0:T(8,128)(2,1)S(1)} %constant_dynamic-update-slice_fusion.refs_0_), channel_id=1, source_target_pairs={{0,192},{2,194},{4,196},{6,198},{8,200},{10,202},{12,204},{14,206}... | collective-permute-start | bytes 245768 | tf_op jit(solution)/shard_map/ppermute | solution.py:19
  21.2 11.0 %collective-permute-start.12 = (bf16[528,256]{1,0:T(8,128)(2,1)S(1)}, bf16[528,256]{1,0:T(8,128)(2,1)S(1)}, u32[]{:S(2)}, u32[]{:S(2)}) collective-permute-start(bf16[528,256]{1,0:T(8,128)(2,1)S(1)} %get-tuple-element.24), channel_id=1, source_target_pairs={{0,4},{2,6},{4,8},{6,10},{8,12},{10,14},{12,0},{14,2},{16,20},{18,... | collective-permute-start | bytes 811016 | tf_op jit(solution)/shard_map/ppermute | solution.py:27
  21.2 11.0 %collective-permute-start.11 = (bf16[528,256]{1,0:T(8,128)(2,1)S(1)}, bf16[528,256]{1,0:T(8,128)(2,1)S(1)}, u32[]{:S(2)}, u32[]{:S(2)}) collective-permute-start(bf16[528,256]{1,0:T(8,128)(2,1)S(1)} %get-tuple-element.22), channel_id=1, source_target_pairs={{0,12},{2,14},{4,0},{6,2},{8,4},{10,6},{12,8},{14,10},{16,28},{18,... | collective-permute-start | bytes 811016 | tf_op jit(solution)/shard_map/ppermute | solution.py:27
  24.0 2.6 %copy-start.2 = (f32[128]{0:T(128)S(1)}, f32[128]{0:T(128)}, u32[]{:S(2)}) copy-start(f32[128]{0:T(128)} %weights_ref.1) | copy-start | bytes 1540
  24.0 15.3 %collective-permute-start.9 = (bf16[1056,256]{1,0:T(8,128)(2,1)S(1)}, bf16[1056,256]{1,0:T(8,128)(2,1)S(1)}, u32[]{:S(2)}, u32[]{:S(2)}) collective-permute-start(bf16[1056,256]{1,0:T(8,128)(2,1)S(1)} %get-tuple-element.58), channel_id=1, source_target_pairs={{0,2},{2,0},{4,6},{6,4},{8,10},{10,8},{12,14},{14,12},{16,18},{18,... | collective-permute-start | bytes 1622024 | tf_op jit(solution)/shard_map/ppermute | solution.py:19
  26.3 13.0 %collective-permute-start.10 = (bf16[1056,256]{1,0:T(8,128)(2,1)S(1)}, bf16[1056,256]{1,0:T(8,128)(2,1)S(1)}, u32[]{:S(2)}, u32[]{:S(2)}) collective-permute-start(bf16[1056,256]{1,0:T(8,128)(2,1)S(1)} %get-tuple-element.57), channel_id=1, source_target_pairs={{0,2},{2,0},{4,6},{6,4},{8,10},{10,8},{12,14},{14,12},{16,18},{18,... | collective-permute-start | bytes 1622024 | tf_op jit(solution)/shard_map/ppermute | solution.py:19
  32.3 7.0 %collective-permute-start.13 = (bf16[528,256]{1,0:T(8,128)(2,1)S(1)}, bf16[528,256]{1,0:T(8,128)(2,1)S(1)}, u32[]{:S(2)}, u32[]{:S(2)}) collective-permute-start(bf16[528,256]{1,0:T(8,128)(2,1)S(1)} %get-tuple-element.56.refs_2_.refs_3_), channel_id=1, source_target_pairs={{0,2},{2,0},{4,6},{6,4},{8,10},{10,8},{12,14},{14,12},{16,18},{18,... | collective-permute-start | bytes 811016 | tf_op jit(solution)/shard_map/ppermute | solution.py:19
  33.5 5.8 %collective-permute-start.14 = (bf16[528,256]{1,0:T(8,128)(2,1)S(1)}, bf16[528,256]{1,0:T(8,128)(2,1)S(1)}, u32[]{:S(2)}, u32[]{:S(2)}) collective-permute-start(bf16[528,256]{1,0:T(8,128)(2,1)S(1)} %get-tuple-element.55.refs_3_.refs_4_), channel_id=1, source_target_pairs={{0,2},{2,0},{4,6},{6,4},{8,10},{10,8},{12,14},{14,12},{16,18},{18,... | collective-permute-start | bytes 811016 | tf_op jit(solution)/shard_map/ppermute | solution.py:19
  33.6 14.6 %collective-permute-start.18 = (bf16[256,128]{1,0:T(8,128)(2,1)S(1)}, bf16[256,128]{1,0:T(8,128)(2,1)S(1)}, u32[]{:S(2)}, u32[]{:S(2)}) collective-permute-start(bf16[256,128]{1,0:T(8,128)(2,1)S(1)} %get-tuple-element.29.refs_3_), channel_id=1, source_target_pairs={{0,1},{1,0},{2,3},{3,2},{4,5},{5,4},{6,7},{7,6},{8,9},{9,8},{10,11... | collective-permute-start | bytes 196616 | tf_op jit(solution)/shard_map/ppermute | solution.py:31
  41.8 10.2 %copy-start = (f32[128,256]{1,0:T(8,128)S(1)}, f32[128,256]{1,0:T(8,128)}, u32[]{:S(2)}) copy-start(f32[128,256]{1,0:T(8,128)} %refs_5_.1) | copy-start | bytes 393220
  41.8 7.2 %collective-permute-start.16 = (bf16[256,128]{1,0:T(8,128)(2,1)S(1)}, bf16[256,128]{1,0:T(8,128)(2,1)S(1)}, u32[]{:S(2)}, u32[]{:S(2)}) collective-permute-start(bf16[256,128]{1,0:T(8,128)(2,1)S(1)} %get-tuple-element.25.refs_0_), channel_id=1, source_target_pairs={{0,32},{2,34},{4,36},{6,38},{8,40},{10,42},{12,44},{14,46},{16,48}... | collective-permute-start | bytes 196616 | tf_op jit(solution)/shard_map/ppermute | solution.py:19
  45.7 3.2 %collective-permute-start.15 = (bf16[256,128]{1,0:T(8,128)(2,1)S(1)}, bf16[256,128]{1,0:T(8,128)(2,1)S(1)}, u32[]{:S(2)}, u32[]{:S(2)}) collective-permute-start(bf16[256,128]{1,0:T(8,128)(2,1)S(1)} %get-tuple-element.27), channel_id=1, source_target_pairs={{0,16},{2,18},{4,20},{6,22},{8,24},{10,26},{12,28},{14,30},{16,0},... | collective-permute-start | bytes 196616 | tf_op jit(solution)/shard_map/ppermute | solution.py:19
  46.6 5.4 %collective-permute-start.17 = (bf16[256,128]{1,0:T(8,128)(2,1)S(1)}, bf16[256,128]{1,0:T(8,128)(2,1)S(1)}, u32[]{:S(2)}, u32[]{:S(2)}) collective-permute-start(bf16[256,128]{1,0:T(8,128)(2,1)S(1)} %get-tuple-element.28), channel_id=1, source_target_pairs={{0,48},{2,50},{4,52},{6,54},{8,56},{10,58},{12,60},{14,62},{16,32}... | collective-permute-start | bytes 196616 | tf_op jit(solution)/shard_map/ppermute | solution.py:19
  52.4 3.1 %collective-permute-start.20 = (f32[64,256]{1,0:T(8,128)S(1)}, f32[64,256]{1,0:T(8,128)S(1)}, u32[]{:S(2)}, u32[]{:S(2)}) collective-permute-start(f32[64,256]{1,0:T(8,128)S(1)} %get-tuple-element.33), channel_id=1, source_target_pairs={{0,2},{2,0},{4,6},{6,4},{8,10},{10,8},{12,14},{14,12},{16,18},{18,... | collective-permute-start | bytes 196616 | tf_op jit(solution)/shard_map/ppermute | solution.py:19
  54.3 8.9 %collective-permute-start.19 = (bf16[256,128]{1,0:T(8,128)(2,1)S(1)}, bf16[256,128]{1,0:T(8,128)(2,1)S(1)}, u32[]{:S(2)}, u32[]{:S(2)}) collective-permute-start(bf16[256,128]{1,0:T(8,128)(2,1)S(1)} %get-tuple-element.31), channel_id=1, source_target_pairs={{0,1},{1,0},{2,3},{3,2},{4,5},{5,4},{6,7},{7,6},{8,9},{9,8},{10,11... | collective-permute-start | bytes 196616 | tf_op jit(solution)/shard_map/ppermute | solution.py:31
  55.5 7.7 %collective-permute-start.22 = (f32[64,256]{1,0:T(8,128)S(1)}, f32[64,256]{1,0:T(8,128)S(1)}, u32[]{:S(2)}, u32[]{:S(2)}) collective-permute-start(f32[64,256]{1,0:T(8,128)S(1)} %add.83), channel_id=1, source_target_pairs={{0,8},{2,10},{4,12},{6,14},{8,0},{10,2},{12,4},{14,6},{16,24},{18,... | collective-permute-start | bytes 196616 | tf_op jit(solution)/shard_map/ppermute | solution.py:19
  56.2 7.0 %collective-permute-start.23 = (f32[64,256]{1,0:T(8,128)S(1)}, f32[64,256]{1,0:T(8,128)S(1)}, u32[]{:S(2)}, u32[]{:S(2)}) collective-permute-start(f32[64,256]{1,0:T(8,128)S(1)} %add.83), channel_id=1, source_target_pairs={{0,12},{2,14},{4,8},{6,10},{8,4},{10,6},{12,0},{14,2},{16,28},{18,... | collective-permute-start | bytes 196616 | tf_op jit(solution)/shard_map/ppermute | solution.py:19
  57.7 5.6 %collective-permute-start.21 = (f32[64,256]{1,0:T(8,128)S(1)}, f32[64,256]{1,0:T(8,128)S(1)}, u32[]{:S(2)}, u32[]{:S(2)}) collective-permute-start(f32[64,256]{1,0:T(8,128)S(1)} %add.83), channel_id=1, source_target_pairs={{0,4},{2,6},{4,0},{6,2},{8,12},{10,14},{12,8},{14,10},{16,20},{18,... | collective-permute-start | bytes 196616 | tf_op jit(solution)/shard_map/ppermute | solution.py:19
  63.3 4.8 %collective-permute-start.26 = (bf16[64,256]{1,0:T(8,128)(2,1)S(1)}, bf16[64,256]{1,0:T(8,128)(2,1)S(1)}, u32[]{:S(2)}, u32[]{:S(2)}) collective-permute-start(bf16[64,256]{1,0:T(8,128)(2,1)S(1)} %add_convert_fusion.1), channel_id=1, source_target_pairs={{0,48},{2,50},{4,52},{6,54},{8,56},{10,58},{12,60},{14,62},{16,32}... | collective-permute-start | bytes 98312 | tf_op jit(solution)/shard_map/ppermute | solution.py:19
  64.2 4.9 %collective-permute-start.25 = (bf16[64,256]{1,0:T(8,128)(2,1)S(1)}, bf16[64,256]{1,0:T(8,128)(2,1)S(1)}, u32[]{:S(2)}, u32[]{:S(2)}) collective-permute-start(bf16[64,256]{1,0:T(8,128)(2,1)S(1)} %add_convert_fusion.1), channel_id=1, source_target_pairs={{0,32},{2,34},{4,36},{6,38},{8,40},{10,42},{12,44},{14,46},{16,48}... | collective-permute-start | bytes 98312 | tf_op jit(solution)/shard_map/ppermute | solution.py:19
  64.2 4.9 %collective-permute-start.24 = (bf16[64,256]{1,0:T(8,128)(2,1)S(1)}, bf16[64,256]{1,0:T(8,128)(2,1)S(1)}, u32[]{:S(2)}, u32[]{:S(2)}) collective-permute-start(bf16[64,256]{1,0:T(8,128)(2,1)S(1)} %add_convert_fusion.1), channel_id=1, source_target_pairs={{0,16},{2,18},{4,20},{6,22},{8,24},{10,26},{12,28},{14,30},{16,0},... | collective-permute-start | bytes 98312 | tf_op jit(solution)/shard_map/ppermute | solution.py:19
  69.1 4.3 %collective-permute-start.29 = (bf16[64,384]{1,0:T(8,128)(2,1)S(1)}, bf16[64,384]{1,0:T(8,128)(2,1)S(1)}, u32[]{:S(2)}, u32[]{:S(2)}) collective-permute-start(bf16[64,384]{1,0:T(8,128)(2,1)S(1)} %get-tuple-element.45), channel_id=1, source_target_pairs={{0,192},{2,194},{4,196},{6,198},{8,200},{10,202},{12,204},{14,206}... | collective-permute-start | bytes 147464 | tf_op jit(solution)/shard_map/ppermute | solution.py:19
  71.9 4.4 %collective-permute-start.28 = (bf16[64,384]{1,0:T(8,128)(2,1)S(1)}, bf16[64,384]{1,0:T(8,128)(2,1)S(1)}, u32[]{:S(2)}, u32[]{:S(2)}) collective-permute-start(bf16[64,384]{1,0:T(8,128)(2,1)S(1)} %get-tuple-element.44), channel_id=1, source_target_pairs={{0,128},{2,130},{4,132},{6,134},{8,136},{10,138},{12,140},{14,142}... | collective-permute-start | bytes 147464 | tf_op jit(solution)/shard_map/ppermute | solution.py:19
  72.3 4.1 %collective-permute-start.27 = (bf16[64,384]{1,0:T(8,128)(2,1)S(1)}, bf16[64,384]{1,0:T(8,128)(2,1)S(1)}, u32[]{:S(2)}, u32[]{:S(2)}) collective-permute-start(bf16[64,384]{1,0:T(8,128)(2,1)S(1)} %get-tuple-element.43), channel_id=1, source_target_pairs={{0,64},{2,66},{4,68},{6,70},{8,72},{10,74},{12,76},{14,78},{16,80}... | collective-permute-start | bytes 147464 | tf_op jit(solution)/shard_map/ppermute | solution.py:19
  76.4 3.7 %collective-permute-start.30 = (f32[64,256]{1,0:T(8,128)S(1)}, f32[64,256]{1,0:T(8,128)S(1)}, u32[]{:S(2)}, u32[]{:S(2)}) collective-permute-start(f32[64,256]{1,0:T(8,128)S(1)} %fusion.5.own_ref), channel_id=1, source_target_pairs={{0,2},{2,0},{4,6},{6,4},{8,10},{10,8},{12,14},{14,12},{16,18},{18,... | collective-permute-start | bytes 196616 | tf_op jit(solution)/shard_map/ppermute | solution.py:19

commit v5 on v4

--- a/solution.py
+++ b/solution.py
@@ -46,18 +46,15 @@
 
 
 def prepare_kernel(weights_ref, *refs):
-    part_refs, (rows_ref, term_ref, cot_ref, zero_ref) = refs[:4], refs[4:]
+    part_refs, (rows_ref, term_ref) = refs[:4], refs[4:]
     weights = weights_ref[...].reshape(1, 128) * (-1.0 / 64.0)
     for d, ref in enumerate(part_refs):
-        for m in range(4):
-            place = pl.ds(256 * m + 64 * d, 64)
-            part = ref[64 * m : 64 * m + 64, :]
-            wide = part.astype(F32)
-            rows_ref[place, :] = part
-            term = jnp.sum(wide * wide * weights, axis=1, keepdims=True)
-            term_ref[place, :] = jnp.broadcast_to(term, (64, 128))
-        cot_ref[64 * d : 64 * d + 64, :] = ref[256:320, :]
-    zero_ref[...] = jnp.zeros_like(zero_ref)
+        place = slice(256 * d, 256 * d + 256)
+        part = ref[...]
+        wide = part.astype(F32)
+        rows_ref[place, :] = part
+        term = jnp.sum(wide * wide * weights, axis=1, keepdims=True)
+        term_ref[place, :] = jnp.broadcast_to(term, (256, 128))
 
 
 def first_kernel(rows_ref, term_ref, *refs):
@@ -70,9 +67,9 @@
     zero_ref[...] = jnp.zeros_like(zero_ref)
 
 
-def last_kernel(first, rows_ref, term_ref, start, *refs):
-    packs, outs = refs[-8:-2], refs[-2:]
-    place = slice(256 * first, 256 * first + 512)
+def last_kernel(blocks, rows_ref, term_ref, start, *refs):
+    packs, outs = refs[-6 - len(blocks) : -len(blocks)], refs[-len(blocks) :]
+    place = slice(256 * blocks[0], 256 * blocks[-1] + 256)
     total = start[place, :]
     for pack in packs:
         total = accumulate(total, rows_ref[place, :], term_ref[place, 0:1], pack)
@@ -99,16 +96,11 @@
 ZEROS = jax.ShapeDtypeStruct((16, 256), BF16)
 
 
-def prepare(weights, rows):
+def prepare(weights, parts):
     return in_vmem(
         prepare_kernel,
-        (
-            jax.ShapeDtypeStruct((1024, 128), BF16),
-            jax.ShapeDtypeStruct((1024, 128), F32),
-            jax.ShapeDtypeStruct((256, 128), BF16),
-            ZEROS,
-        ),
-        [weights, *rows],
+        (jax.ShapeDtypeStruct((1024, 128), BF16), jax.ShapeDtypeStruct((1024, 128), F32)),
+        [weights, *parts],
     )
 
 
@@ -118,14 +110,15 @@
     )
 
 
-def cross_last(first, rows, term, total, packs, earlier=()):
-    outs = [jax.ShapeDtypeStruct((256, 128), BF16 if m else F32) for m in (first, first + 1)]
+def cross_last(blocks, rows, term, total, packs, earlier=()):
+    outs = [jax.ShapeDtypeStruct((256, 128), BF16 if m else F32) for m in blocks]
     args = [rows, term, total, *earlier, *packs]
-    return in_vmem(functools.partial(last_kernel, first), outs, args)
-
-
-def gate_kernel(value_ref, _, out_ref):
-    out_ref[...] = value_ref[...]
+    return in_vmem(functools.partial(last_kernel, blocks), outs, args)
+
+
+def gate_kernel(slab_ref, cotangent_ref, _, out_ref):
+    out_ref[0:64, :] = slab_ref[...]
+    out_ref[64:128, :] = cotangent_ref[...]
 
 
 def halves_kernel(right_ref, left_ref, *refs):
@@ -164,7 +157,6 @@
 
 
 def local(slab_points, key_points, length_weights, adjoint, label_cov, cotangent):
-
     keys = key_points.astype(F32)
     scaled = (keys * length_weights * (1.0 / 32.0)).astype(BF16)
     key_term = jnp.sum(keys * keys * length_weights, axis=1) * (-1.0 / 64.0)
@@ -183,10 +175,13 @@
     right, left = swap_ring(pack, X, 1), swap_ring(pack, X, 3)
     own_far = swap(pack, CORE, 1)
 
-    own = in_vmem(gate_kernel, jax.ShapeDtypeStruct((64, 128), BF16), [slab_points, own_far])
-    part = jnp.concatenate([own] + [swap(own, Z, m) for m in (1, 2, 3)] + [cotangent], axis=0)
+    own = jax.ShapeDtypeStruct((128, 128), BF16)
+    own = in_vmem(gate_kernel, own, [slab_points, cotangent, own_far])
+    over_z = [own] + [swap(own, Z, m) for m in (1, 2, 3)]
+    part = jnp.concatenate([o[:64] for o in over_z], axis=0)
+    cot = jnp.concatenate([o[64:] for o in over_z], axis=0)
     parts = [part] + [swap(part, Y, m) for m in (1, 2, 3)]
-    rows, term, cot, _ = prepare(length_weights, parts)
+    rows, term = prepare(length_weights, parts)
 
     half = jax.ShapeDtypeStruct((528, 256), BF16)
     upper, lower, zeros = in_vmem(halves_kernel, (half, half, ZEROS), [right, left, parts[1]])
@@ -197,9 +192,9 @@
     upper, lower = upper + zeros[0:1], lower + zeros[0:1]
     cot_far = swap_lab(cot)
     packs = [right_far, left_far, upper, lower, swap(upper, CORE, 1), swap(lower, CORE, 1)]
-    sent = cross_last(2, rows, term, total, packs)
-    sent = cross_last(0, rows, term, total, packs, sent[:1]) + sent
-    back = [swap(sent[m], Z, m) for m in (1, 2, 3)]
+    sent = cross_last((1, 2, 3), rows, term, total, packs)
+    sent = cross_last((0,), rows, term, total, packs, sent[:1]) + sent
+    back = [swap(sent[m], Y, m) for m in (1, 2, 3)]
 
     mixed, mixed_far, grad, grad_far = in_vmem(
         grad_kernel,
@@ -217,12 +212,12 @@
     back = [swap(grad, X, m) for m in (1, 2, 3)]
     grad = ((grad + back[0]) + (back[1] + back[2])).astype(BF16)
 
-    back = [swap(grad, Z, m).astype(F32) for m in (1, 2, 3)]
+    back = [swap(grad, Y, m).astype(F32) for m in (1, 2, 3)]
     grad = ((grad.astype(F32) + back[0]) + (back[1] + back[2])).astype(BF16)
 
     back = [
         swap(
-            jnp.concatenate([mixed[64 * m : 64 * m + 64].astype(BF16), grad], axis=1), Y, m
+            jnp.concatenate([mixed[64 * m : 64 * m + 64].astype(BF16), grad], axis=1), Z, m
         ).astype(F32)
         for m in (1, 2, 3)
     ]

time: 81 us -> 78.7 us (0.972)
  waiting for transfers between devices: 20.9 us -> 18.8 us
    ppermute x25, waiting for transfers between devices: 14.4 us -> 12 us  [swap(): lax.ppermute(value, 'pts', [(i, i ^ mask << place) for i in range(PTS)])]
    ppermute x2, starting transfers between devices: 6.83 us -> 8.04 us  [swap_lab(): return lax.ppermute(value, 'lab', [(0, 1), (1, 0)])]
    ppermute x25, starting transfers between devices: 33.7 us -> 32.8 us  [swap(): lax.ppermute(value, 'pts', [(i, i ^ mask << place) for i in range(PTS)])]
  transfers between devices with their start and end apart: 31 -> 31, of which waited for: 12 -> 14; matrix products, arithmetic and copies ran while one was open for 1% -> 1% of each run, Pallas kernels for 13% -> 13%
where the time goes in v5:
time: 78.7 us; the launch traced here: 78.6 us
  starting transfers between devices  45.1 us (57%)
  waiting for transfers between devices  18.8 us (24%)
  Pallas kernels  11.3 us (14%)
  other arithmetic  2.15 us (3%)
  between operations  0.95 us (1%)
    ppermute x25, starting transfers between devices, swap(): lax.ppermute(value, 'pts', [(i, i ^ mask << place) for i in range(PTS)])  32.8 us
    ppermute x25, waiting for transfers between devices, swap(): lax.ppermute(value, 'pts', [(i, i ^ mask << place) for i in range(PTS)])  12 us
    pallas_call x8, Pallas kernels, in_vmem(): pl.pallas_call(kernel, out_shape=out, in_specs=[pl.BlockSpec(memory_space...  11.3 us
    ppermute x2, starting transfers between devices, swap_lab(): return lax.ppermute(value, 'lab', [(0, 1), (1, 0)])  8.04 us
    ppermute x2, waiting for transfers between devices, swap_lab(): return lax.ppermute(value, 'lab', [(0, 1), (1, 0)])  4.56 us
    ppermute x4, starting transfers between devices, swap_ring(): return lax.ppermute(value, 'pts', pairs)  4.22 us
    ppermute x4, waiting for transfers between devices, swap_ring(): return lax.ppermute(value, 'pts', pairs)  2.16 us
  transfers between devices with their start and end apart: 31, of which 14 were waited for; matrix products, arithmetic and copies ran while one was open for 1% of the time, Pallas kernels for 13%

profile of v5, /device:TPU:1, one launch (start us, length us, event | category | flops | bytes accessed | tf_op | source)
XLA Modules:
  0.0 78.6 jit_solution(3951278153982557325)
XLA Ops:
  0.6 1.2 %fusion.3 = (f32[1024]{0:T(1024)S(1)}, bf16[1024,128]{1,0:T(8,128)(2,1)S(1)}) fusion(bf16[1024,128]{1,0:T(8,128)(2,1)} %param.7, f32[128]{0:T(128)} %weights_ref.1), kind=kLoop, calls=%fused_computation.5 | loop fusion | flops 916480 | bytes 528896 | tf_op jit(solution)/shard_map/reduce_sum | solution.py:162
  2.0 0.3 concatenate.27.refs_0_
  2.3 3.3 %collective-permute-start = (bf16[1056,256]{1,0:T(8,128)(2,1)S(1)}, bf16[1056,256]{1,0:T(8,128)(2,1)S(1)}, u32[]{:S(2)}, u32[]{:S(2)}) collective-permute-start(bf16[1056,256]{1,0:T(8,128)(2,1)S(1)} %concatenate.27.refs_0_), channel_id=1, source_target_pairs={{0,2},{2,0},{4,6},{6,4},{8,10},{10,8},{12,14},{14,12},{16,18},{18,... | collective-permute-start | bytes 1622024 | tf_op jit(solution)/shard_map/ppermute | solution.py:19
  5.6 0.8 collective-permute-start.7
  6.4 0.7 collective-permute-start.8
  7.2 3.6 %collective-permute-start.3 = (bf16[128,128]{1,0:T(8,128)(2,1)S(1)}, bf16[128,128]{1,0:T(8,128)(2,1)S(1)}, u32[]{:S(2)}, u32[]{:S(2)}) collective-permute-start(bf16[128,128]{1,0:T(8,128)(2,1)S(1)} %shard_map.77), channel_id=1, source_target_pairs={{0,48},{2,50},{4,52},{6,54},{8,56},{10,58},{12,60},{14,62},{16,32}... | collective-permute-start | bytes 98312 | tf_op jit(solution)/shard_map/ppermute | solution.py:19
  10.9 0.4 collective-permute-start.1
  11.2 0.9 %collective-permute-done.3 = bf16[128,128]{1,0:T(8,128)(2,1)S(1)} collective-permute-done((bf16[128,128]{1,0:T(8,128)(2,1)S(1)}, bf16[128,128]{1,0:T(8,128)(2,1)S(1)}, u32[]{:S(2)}, u32[]{:S(2)}) %collective-permute-start.3) | collective-permute-done | bytes 32800 | tf_op jit(solution)/shard_map/ppermute | solution.py:19
  12.2 2.7 %collective-permute-done.2 = bf16[128,128]{1,0:T(8,128)(2,1)S(1)} collective-permute-done((bf16[128,128]{1,0:T(8,128)(2,1)S(1)}, bf16[128,128]{1,0:T(8,128)(2,1)S(1)}, u32[]{:S(2)}, u32[]{:S(2)}) %collective-permute-start.2) | collective-permute-done | bytes 32800 | tf_op jit(solution)/shard_map/ppermute | solution.py:19
  14.9 1.4 %collective-permute-start.4 = (bf16[256,128]{1,0:T(8,128)(2,1)S(1)}, bf16[256,128]{1,0:T(8,128)(2,1)S(1)}, u32[]{:S(2)}, u32[]{:S(2)}) collective-permute-start(bf16[256,128]{1,0:T(8,128)(2,1)S(1)} %pad_maximum_fusion.1.refs_0_), channel_id=1, source_target_pairs={{0,64},{2,66},{4,68},{6,70},{8,72},{10,74},{12,76},{14,78},{16,80}... | collective-permute-start | bytes 196616 | tf_op jit(solution)/shard_map/ppermute | solution.py:19
  16.3 2.6 %collective-permute-start.5 = (bf16[256,128]{1,0:T(8,128)(2,1)S(1)}, bf16[256,128]{1,0:T(8,128)(2,1)S(1)}, u32[]{:S(2)}, u32[]{:S(2)}) collective-permute-start(bf16[256,128]{1,0:T(8,128)(2,1)S(1)} %pad_maximum_fusion.1.refs_0_), channel_id=1, source_target_pairs={{0,128},{2,130},{4,132},{6,134},{8,136},{10,138},{12,140},{14,142}... | collective-permute-start | bytes 196616 | tf_op jit(solution)/shard_map/ppermute | solution.py:19
  18.9 0.5 collective-permute-done.7.refs_2_.right_ref
  19.5 1.6 %collective-permute-done.8.refs_3_.left_ref = bf16[1056,256]{1,0:T(8,128)(2,1)S(1)} collective-permute-done((bf16[1056,256]{1,0:T(8,128)(2,1)S(1)}, bf16[1056,256]{1,0:T(8,128)(2,1)S(1)}, u32[]{:S(2)}, u32[]{:S(2)}) %collective-permute-start.8) | collective-permute-done | bytes 540704 | tf_op jit(solution)/shard_map/ppermute | solution.py:27
  21.3 2.7 %collective-permute-start.11 = (bf16[528,256]{1,0:T(8,128)(2,1)S(1)}, bf16[528,256]{1,0:T(8,128)(2,1)S(1)}, u32[]{:S(2)}, u32[]{:S(2)}) collective-permute-start(bf16[528,256]{1,0:T(8,128)(2,1)S(1)} %get-tuple-element.20), channel_id=1, source_target_pairs={{0,12},{2,14},{4,0},{6,2},{8,4},{10,6},{12,8},{14,10},{16,28},{18,... | collective-permute-start | bytes 811016 | tf_op jit(solution)/shard_map/ppermute | solution.py:27
  24.0 1.8 %collective-permute-start.9 = (bf16[1056,256]{1,0:T(8,128)(2,1)S(1)}, bf16[1056,256]{1,0:T(8,128)(2,1)S(1)}, u32[]{:S(2)}, u32[]{:S(2)}) collective-permute-start(bf16[1056,256]{1,0:T(8,128)(2,1)S(1)} %get-tuple-element.62), channel_id=1, source_target_pairs={{0,2},{2,0},{4,6},{6,4},{8,10},{10,8},{12,14},{14,12},{16,18},{18,... | collective-permute-start | bytes 1622024 | tf_op jit(solution)/shard_map/ppermute | solution.py:19
  25.8 0.3 collective-permute-start.10
  26.1 0.2 shard_map.78
  26.4 4.8 %shard_map.79 = (f32[1024,128]{1,0:T(8,128)S(1)}, bf16[16,256]{1,0:T(8,128)(2,1)S(1)}) custom-call(bf16[1024,128]{1,0:T(8,128)(2,1)S(1)} %get-tuple-element.16.rows_ref, f32[1024,128]{1,0:T(8,128)S(1)} %get-tuple-element.17.term_ref, bf16[1056,256]{1,0:T(8,128)(2,1)S(1)} %concatenate.27.refs_0_, bf16[1056,256]{1,0:T(8,128)(2,1)S(1)} %collective-permute-done._.refs_1_, ...), custom_call_target="tpu_custom_call" | custom-call | flops 1000 | bytes 2097152 | tf_op jit(solution)/shard_map/pallas_call | solution.py:81
  31.3 0.3 collective-permute-start.13
  31.6 0.2 collective-permute-start.14
  31.9 6.9 %collective-permute-start.18 = (bf16[256,128]{1,0:T(8,128)(2,1)S(1)}, bf16[256,128]{1,0:T(8,128)(2,1)S(1)}, u32[]{:S(2)}, u32[]{:S(2)}) collective-permute-start(bf16[256,128]{1,0:T(8,128)(2,1)S(1)} %pad_maximum_fusion.2.refs_3_), channel_id=1, source_target_pairs={{0,1},{1,0},{2,3},{3,2},{4,5},{5,4},{6,7},{7,6},{8,9},{9,8},{10,11... | collective-permute-start | bytes 196616 | tf_op jit(solution)/shard_map/ppermute | solution.py:31
  38.8 3.6 %shard_map.81 = (bf16[256,128]{1,0:T(8,128)(2,1)S(1)}, bf16[256,128]{1,0:T(8,128)(2,1)S(1)}, bf16[256,128]{1,0:T(8,128)(2,1)S(1)}) custom-call(bf16[1024,128]{1,0:T(8,128)(2,1)S(1)} %get-tuple-element.16.rows_ref, f32[1024,128]{1,0:T(8,128)S(1)} %get-tuple-element.17.term_ref, f32[1024,128]{1,0:T(8,128)S(1)} %get-tuple-element.18.start, ...), custom_call_target="tpu_custom_call" | custom-call | flops 1000 | bytes 2097152 | tf_op jit(solution)/shard_map/pallas_call | solution.py:81
  42.4 1.4 %collective-permute-start.15 = (bf16[256,128]{1,0:T(8,128)(2,1)S(1)}, bf16[256,128]{1,0:T(8,128)(2,1)S(1)}, u32[]{:S(2)}, u32[]{:S(2)}) collective-permute-start(bf16[256,128]{1,0:T(8,128)(2,1)S(1)} %get-tuple-element.23.refs_0_), channel_id=1, source_target_pairs={{0,64},{2,66},{4,68},{6,70},{8,72},{10,74},{12,76},{14,78},{16,80}... | collective-permute-start | bytes 196616 | tf_op jit(solution)/shard_map/ppermute | solution.py:19
  43.7 2.6 %collective-permute-start.16 = (bf16[256,128]{1,0:T(8,128)(2,1)S(1)}, bf16[256,128]{1,0:T(8,128)(2,1)S(1)}, u32[]{:S(2)}, u32[]{:S(2)}) collective-permute-start(bf16[256,128]{1,0:T(8,128)(2,1)S(1)} %get-tuple-element.24), channel_id=1, source_target_pairs={{0,128},{2,130},{4,132},{6,134},{8,136},{10,138},{12,140},{14,142}... | collective-permute-start | bytes 196616 | tf_op jit(solution)/shard_map/ppermute | solution.py:19
  46.4 1.5 %shard_map.82.own = f32[256,128]{1,0:T(8,128)S(1)} custom-call(bf16[1024,128]{1,0:T(8,128)(2,1)S(1)} %get-tuple-element.16.rows_ref, f32[1024,128]{1,0:T(8,128)S(1)} %get-tuple-element.17.term_ref, f32[1024,128]{1,0:T(8,128)S(1)} %get-tuple-element.18.start, bf16[256,128]{1,0:T(8,128)(2,1)S(1)} %get-tuple-element.23.refs_0_, ...), custom_call_target="tpu_custom_call" | custom-call | flops 1000 | bytes 2097152 | tf_op jit(solution)/shard_map/pallas_call | solution.py:81
  47.9 1.2 %collective-permute-done.16.refs_1_ = bf16[256,128]{1,0:T(8,128)(2,1)S(1)} collective-permute-done((bf16[256,128]{1,0:T(8,128)(2,1)S(1)}, bf16[256,128]{1,0:T(8,128)(2,1)S(1)}, u32[]{:S(2)}, u32[]{:S(2)}) %collective-permute-start.16) | collective-permute-done | bytes 65568 | tf_op jit(solution)/shard_map/ppermute | solution.py:19
  49.1 1.7 %collective-permute-done.17.refs_2_ = bf16[256,128]{1,0:T(8,128)(2,1)S(1)} collective-permute-done((bf16[256,128]{1,0:T(8,128)(2,1)S(1)}, bf16[256,128]{1,0:T(8,128)(2,1)S(1)}, u32[]{:S(2)}, u32[]{:S(2)}) %collective-permute-start.17) | collective-permute-done | bytes 65568 | tf_op jit(solution)/shard_map/ppermute | solution.py:19
  50.8 0.5 shard_map.83
  51.3 2.2 %collective-permute-start.20 = (f32[64,256]{1,0:T(8,128)S(1)}, f32[64,256]{1,0:T(8,128)S(1)}, u32[]{:S(2)}, u32[]{:S(2)}) collective-permute-start(f32[64,256]{1,0:T(8,128)S(1)} %get-tuple-element.29), channel_id=1, source_target_pairs={{0,2},{2,0},{4,6},{6,4},{8,10},{10,8},{12,14},{14,12},{16,18},{18,... | collective-permute-start | bytes 196616 | tf_op jit(solution)/shard_map/ppermute | solution.py:19
  53.5 1.1 %collective-permute-start.19 = (bf16[256,128]{1,0:T(8,128)(2,1)S(1)}, bf16[256,128]{1,0:T(8,128)(2,1)S(1)}, u32[]{:S(2)}, u32[]{:S(2)}) collective-permute-start(bf16[256,128]{1,0:T(8,128)(2,1)S(1)} %get-tuple-element.27), channel_id=1, source_target_pairs={{0,1},{1,0},{2,3},{3,2},{4,5},{5,4},{6,7},{7,6},{8,9},{9,8},{10,11... | collective-permute-start | bytes 196616 | tf_op jit(solution)/shard_map/ppermute | solution.py:31
  54.6 1.1 %collective-permute-start.22 = (f32[64,256]{1,0:T(8,128)S(1)}, f32[64,256]{1,0:T(8,128)S(1)}, u32[]{:S(2)}, u32[]{:S(2)}) collective-permute-start(f32[64,256]{1,0:T(8,128)S(1)} %add.83), channel_id=1, source_target_pairs={{0,8},{2,10},{4,12},{6,14},{8,0},{10,2},{12,4},{14,6},{16,24},{18,... | collective-permute-start | bytes 196616 | tf_op jit(solution)/shard_map/ppermute | solution.py:19
  55.8 1.6 %collective-permute-start.23 = (f32[64,256]{1,0:T(8,128)S(1)}, f32[64,256]{1,0:T(8,128)S(1)}, u32[]{:S(2)}, u32[]{:S(2)}) collective-permute-start(f32[64,256]{1,0:T(8,128)S(1)} %add.83), channel_id=1, source_target_pairs={{0,12},{2,14},{4,8},{6,10},{8,4},{10,6},{12,0},{14,2},{16,28},{18,... | collective-permute-start | bytes 196616 | tf_op jit(solution)/shard_map/ppermute | solution.py:19
  57.4 0.5 collective-permute-start.21
  57.9 4.6 %collective-permute-done.19 = bf16[256,128]{1,0:T(8,128)(2,1)S(1)} collective-permute-done((bf16[256,128]{1,0:T(8,128)(2,1)S(1)}, bf16[256,128]{1,0:T(8,128)(2,1)S(1)}, u32[]{:S(2)}, u32[]{:S(2)}) %collective-permute-start.19) | collective-permute-done | bytes 65568 | tf_op jit(solution)/shard_map/ppermute | solution.py:31
  62.5 0.1 collective-permute-start.26
  62.6 0.1 collective-permute-start.25
  62.7 3.1 %collective-permute-start.24 = (bf16[64,256]{1,0:T(8,128)(2,1)S(1)}, bf16[64,256]{1,0:T(8,128)(2,1)S(1)}, u32[]{:S(2)}, u32[]{:S(2)}) collective-permute-start(bf16[64,256]{1,0:T(8,128)(2,1)S(1)} %add_convert_fusion.1), channel_id=1, source_target_pairs={{0,64},{2,66},{4,68},{6,70},{8,72},{10,74},{12,76},{14,78},{16,80}... | collective-permute-start | bytes 98312 | tf_op jit(solution)/shard_map/ppermute | solution.py:19
  65.8 0.7 collective-permute-done.26
  66.6 0.4 collective-permute-done.25
  67.0 0.8 %collective-permute-done.24 = bf16[64,256]{1,0:T(8,128)(2,1)S(1)} collective-permute-done((bf16[64,256]{1,0:T(8,128)(2,1)S(1)}, bf16[64,256]{1,0:T(8,128)(2,1)S(1)}, u32[]{:S(2)}, u32[]{:S(2)}) %collective-permute-start.24) | collective-permute-done | bytes 32800 | tf_op jit(solution)/shard_map/ppermute | solution.py:19
  67.8 1.8 %collective-permute-start.29 = (bf16[64,384]{1,0:T(8,128)(2,1)S(1)}, bf16[64,384]{1,0:T(8,128)(2,1)S(1)}, u32[]{:S(2)}, u32[]{:S(2)}) collective-permute-start(bf16[64,384]{1,0:T(8,128)(2,1)S(1)} %get-tuple-element.41), channel_id=1, source_target_pairs={{0,48},{2,50},{4,52},{6,54},{8,56},{10,58},{12,60},{14,62},{16,32}... | collective-permute-start | bytes 147464 | tf_op jit(solution)/shard_map/ppermute | solution.py:19
  69.6 1.9 %collective-permute-start.27 = (bf16[64,384]{1,0:T(8,128)(2,1)S(1)}, bf16[64,384]{1,0:T(8,128)(2,1)S(1)}, u32[]{:S(2)}, u32[]{:S(2)}) collective-permute-start(bf16[64,384]{1,0:T(8,128)(2,1)S(1)} %get-tuple-element.39), channel_id=1, source_target_pairs={{0,16},{2,18},{4,20},{6,22},{8,24},{10,26},{12,28},{14,30},{16,0},... | collective-permute-start | bytes 147464 | tf_op jit(solution)/shard_map/ppermute | solution.py:19
  71.5 1.3 %collective-permute-done.29 = bf16[64,384]{1,0:T(8,128)(2,1)S(1)} collective-permute-done((bf16[64,384]{1,0:T(8,128)(2,1)S(1)}, bf16[64,384]{1,0:T(8,128)(2,1)S(1)}, u32[]{:S(2)}, u32[]{:S(2)}) %collective-permute-start.29) | collective-permute-done | bytes 49184 | tf_op jit(solution)/shard_map/ppermute | solution.py:19
  72.8 1.8 %collective-permute-done.28 = bf16[64,384]{1,0:T(8,128)(2,1)S(1)} collective-permute-done((bf16[64,384]{1,0:T(8,128)(2,1)S(1)}, bf16[64,384]{1,0:T(8,128)(2,1)S(1)}, u32[]{:S(2)}, u32[]{:S(2)}) %collective-permute-start.28) | collective-permute-done | bytes 49184 | tf_op jit(solution)/shard_map/ppermute | solution.py:19
  74.7 2.4 %collective-permute-start.30 = (f32[64,256]{1,0:T(8,128)S(1)}, f32[64,256]{1,0:T(8,128)S(1)}, u32[]{:S(2)}, u32[]{:S(2)}) collective-permute-start(f32[64,256]{1,0:T(8,128)S(1)} %fusion.5.own_ref), channel_id=1, source_target_pairs={{0,2},{2,0},{4,6},{6,4},{8,10},{10,8},{12,14},{14,12},{16,18},{18,... | collective-permute-start | bytes 196616 | tf_op jit(solution)/shard_map/ppermute | solution.py:19
  77.1 0.6 fusion.7
  77.7 0.3 collective-permute-done.30.other_ref
  78.0 0.7 shard_map.84
  (63 shorter events, 0.7 us)
Async XLA Ops:
  0.6 1.3 %copy-start.4 = (bf16[1024,128]{1,0:T(8,128)(2,1)S(1)}, bf16[1024,128]{1,0:T(8,128)(2,1)}, u32[]{:S(2)}) copy-start(bf16[1024,128]{1,0:T(8,128)(2,1)} %param.9) | copy-start | bytes 786436
  2.0 5.2 %copy-start.1 = (bf16[64,128]{1,0:T(8,128)(2,1)S(1)}, bf16[64,128]{1,0:T(8,128)(2,1)}, u32[]{:S(2)}) copy-start(bf16[64,128]{1,0:T(8,128)(2,1)} %slab_ref.1) | copy-start | bytes 49156
  2.0 5.2 %copy-start.2 = (bf16[64,128]{1,0:T(8,128)(2,1)S(1)}, bf16[64,128]{1,0:T(8,128)(2,1)}, u32[]{:S(2)}) copy-start(bf16[64,128]{1,0:T(8,128)(2,1)} %cotangent_ref.1) | copy-start | bytes 49156
  2.3 4.9 %collective-permute-start = (bf16[1056,256]{1,0:T(8,128)(2,1)S(1)}, bf16[1056,256]{1,0:T(8,128)(2,1)S(1)}, u32[]{:S(2)}, u32[]{:S(2)}) collective-permute-start(bf16[1056,256]{1,0:T(8,128)(2,1)S(1)} %concatenate.27.refs_0_), channel_id=1, source_target_pairs={{0,2},{2,0},{4,6},{6,4},{8,10},{10,8},{12,14},{14,12},{16,18},{18,... | collective-permute-start | bytes 1622024 | tf_op jit(solution)/shard_map/ppermute | solution.py:19
  5.6 13.8 %collective-permute-start.7 = (bf16[1056,256]{1,0:T(8,128)(2,1)S(1)}, bf16[1056,256]{1,0:T(8,128)(2,1)S(1)}, u32[]{:S(2)}, u32[]{:S(2)}) collective-permute-start(bf16[1056,256]{1,0:T(8,128)(2,1)S(1)} %concatenate.27.refs_0_), channel_id=1, source_target_pairs={{0,12},{2,14},{4,0},{6,2},{8,4},{10,6},{12,8},{14,10},{16,28},{18,... | collective-permute-start | bytes 1622024 | tf_op jit(solution)/shard_map/ppermute | solution.py:27
  6.4 14.7 %collective-permute-start.8 = (bf16[1056,256]{1,0:T(8,128)(2,1)S(1)}, bf16[1056,256]{1,0:T(8,128)(2,1)S(1)}, u32[]{:S(2)}, u32[]{:S(2)}) collective-permute-start(bf16[1056,256]{1,0:T(8,128)(2,1)S(1)} %concatenate.27.refs_0_), channel_id=1, source_target_pairs={{0,4},{2,6},{4,8},{6,10},{8,12},{10,14},{12,0},{14,2},{16,20},{18,... | collective-permute-start | bytes 1622024 | tf_op jit(solution)/shard_map/ppermute | solution.py:27
  7.2 5.0 %collective-permute-start.3 = (bf16[128,128]{1,0:T(8,128)(2,1)S(1)}, bf16[128,128]{1,0:T(8,128)(2,1)S(1)}, u32[]{:S(2)}, u32[]{:S(2)}) collective-permute-start(bf16[128,128]{1,0:T(8,128)(2,1)S(1)} %shard_map.77), channel_id=1, source_target_pairs={{0,48},{2,50},{4,52},{6,54},{8,56},{10,58},{12,60},{14,62},{16,32}... | collective-permute-start | bytes 98312 | tf_op jit(solution)/shard_map/ppermute | solution.py:19
  10.8 4.1 %collective-permute-start.2 = (bf16[128,128]{1,0:T(8,128)(2,1)S(1)}, bf16[128,128]{1,0:T(8,128)(2,1)S(1)}, u32[]{:S(2)}, u32[]{:S(2)}) collective-permute-start(bf16[128,128]{1,0:T(8,128)(2,1)S(1)} %shard_map.77), channel_id=1, source_target_pairs={{0,32},{2,34},{4,36},{6,38},{8,40},{10,42},{12,44},{14,46},{16,48}... | collective-permute-start | bytes 98312 | tf_op jit(solution)/shard_map/ppermute | solution.py:19
  10.9 4.1 %collective-permute-start.1 = (bf16[128,128]{1,0:T(8,128)(2,1)S(1)}, bf16[128,128]{1,0:T(8,128)(2,1)S(1)}, u32[]{:S(2)}, u32[]{:S(2)}) collective-permute-start(bf16[128,128]{1,0:T(8,128)(2,1)S(1)} %shard_map.77), channel_id=1, source_target_pairs={{0,16},{2,18},{4,20},{6,22},{8,24},{10,26},{12,28},{14,30},{16,0},... | collective-permute-start | bytes 98312 | tf_op jit(solution)/shard_map/ppermute | solution.py:19
  14.9 6.2 %collective-permute-start.4 = (bf16[256,128]{1,0:T(8,128)(2,1)S(1)}, bf16[256,128]{1,0:T(8,128)(2,1)S(1)}, u32[]{:S(2)}, u32[]{:S(2)}) collective-permute-start(bf16[256,128]{1,0:T(8,128)(2,1)S(1)} %pad_maximum_fusion.1.refs_0_), channel_id=1, source_target_pairs={{0,64},{2,66},{4,68},{6,70},{8,72},{10,74},{12,76},{14,78},{16,80}... | collective-permute-start | bytes 196616 | tf_op jit(solution)/shard_map/ppermute | solution.py:19
  16.3 9.5 %collective-permute-start.5 = (bf16[256,128]{1,0:T(8,128)(2,1)S(1)}, bf16[256,128]{1,0:T(8,128)(2,1)S(1)}, u32[]{:S(2)}, u32[]{:S(2)}) collective-permute-start(bf16[256,128]{1,0:T(8,128)(2,1)S(1)} %pad_maximum_fusion.1.refs_0_), channel_id=1, source_target_pairs={{0,128},{2,130},{4,132},{6,134},{8,136},{10,138},{12,140},{14,142}... | collective-permute-start | bytes 196616 | tf_op jit(solution)/shard_map/ppermute | solution.py:19
  18.9 7.2 %collective-permute-start.6 = (bf16[256,128]{1,0:T(8,128)(2,1)S(1)}, bf16[256,128]{1,0:T(8,128)(2,1)S(1)}, u32[]{:S(2)}, u32[]{:S(2)}) collective-permute-start(bf16[256,128]{1,0:T(8,128)(2,1)S(1)} %pad_maximum_fusion.1.refs_0_), channel_id=1, source_target_pairs={{0,192},{2,194},{4,196},{6,198},{8,200},{10,202},{12,204},{14,206}... | collective-permute-start | bytes 196616 | tf_op jit(solution)/shard_map/ppermute | solution.py:19
  21.2 10.0 %collective-permute-start.12 = (bf16[528,256]{1,0:T(8,128)(2,1)S(1)}, bf16[528,256]{1,0:T(8,128)(2,1)S(1)}, u32[]{:S(2)}, u32[]{:S(2)}) collective-permute-start(bf16[528,256]{1,0:T(8,128)(2,1)S(1)} %get-tuple-element.22), channel_id=1, source_target_pairs={{0,4},{2,6},{4,8},{6,10},{8,12},{10,14},{12,0},{14,2},{16,20},{18,... | collective-permute-start | bytes 811016 | tf_op jit(solution)/shard_map/ppermute | solution.py:27
  21.3 10.0 %collective-permute-start.11 = (bf16[528,256]{1,0:T(8,128)(2,1)S(1)}, bf16[528,256]{1,0:T(8,128)(2,1)S(1)}, u32[]{:S(2)}, u32[]{:S(2)}) collective-permute-start(bf16[528,256]{1,0:T(8,128)(2,1)S(1)} %get-tuple-element.20), channel_id=1, source_target_pairs={{0,12},{2,14},{4,0},{6,2},{8,4},{10,6},{12,8},{14,10},{16,28},{18,... | collective-permute-start | bytes 811016 | tf_op jit(solution)/shard_map/ppermute | solution.py:27
  24.0 2.1 %copy-start.3 = (f32[128]{0:T(128)S(1)}, f32[128]{0:T(128)}, u32[]{:S(2)}) copy-start(f32[128]{0:T(128)} %weights_ref.1) | copy-start | bytes 1540
  24.0 14.8 %collective-permute-start.9 = (bf16[1056,256]{1,0:T(8,128)(2,1)S(1)}, bf16[1056,256]{1,0:T(8,128)(2,1)S(1)}, u32[]{:S(2)}, u32[]{:S(2)}) collective-permute-start(bf16[1056,256]{1,0:T(8,128)(2,1)S(1)} %get-tuple-element.62), channel_id=1, source_target_pairs={{0,2},{2,0},{4,6},{6,4},{8,10},{10,8},{12,14},{14,12},{16,18},{18,... | collective-permute-start | bytes 1622024 | tf_op jit(solution)/shard_map/ppermute | solution.py:19
  25.8 12.9 %collective-permute-start.10 = (bf16[1056,256]{1,0:T(8,128)(2,1)S(1)}, bf16[1056,256]{1,0:T(8,128)(2,1)S(1)}, u32[]{:S(2)}, u32[]{:S(2)}) collective-permute-start(bf16[1056,256]{1,0:T(8,128)(2,1)S(1)} %get-tuple-element.61), channel_id=1, source_target_pairs={{0,2},{2,0},{4,6},{6,4},{8,10},{10,8},{12,14},{14,12},{16,18},{18,... | collective-permute-start | bytes 1622024 | tf_op jit(solution)/shard_map/ppermute | solution.py:19
  31.3 7.5 %collective-permute-start.13 = (bf16[528,256]{1,0:T(8,128)(2,1)S(1)}, bf16[528,256]{1,0:T(8,128)(2,1)S(1)}, u32[]{:S(2)}, u32[]{:S(2)}) collective-permute-start(bf16[528,256]{1,0:T(8,128)(2,1)S(1)} %get-tuple-element.60.refs_2_.refs_3_), channel_id=1, source_target_pairs={{0,2},{2,0},{4,6},{6,4},{8,10},{10,8},{12,14},{14,12},{16,18},{18,... | collective-permute-start | bytes 811016 | tf_op jit(solution)/shard_map/ppermute | solution.py:19
  31.6 7.2 %collective-permute-start.14 = (bf16[528,256]{1,0:T(8,128)(2,1)S(1)}, bf16[528,256]{1,0:T(8,128)(2,1)S(1)}, u32[]{:S(2)}, u32[]{:S(2)}) collective-permute-start(bf16[528,256]{1,0:T(8,128)(2,1)S(1)} %get-tuple-element.59.refs_3_.refs_4_), channel_id=1, source_target_pairs={{0,2},{2,0},{4,6},{6,4},{8,10},{10,8},{12,14},{14,12},{16,18},{18,... | collective-permute-start | bytes 811016 | tf_op jit(solution)/shard_map/ppermute | solution.py:19
  31.9 16.0 %collective-permute-start.18 = (bf16[256,128]{1,0:T(8,128)(2,1)S(1)}, bf16[256,128]{1,0:T(8,128)(2,1)S(1)}, u32[]{:S(2)}, u32[]{:S(2)}) collective-permute-start(bf16[256,128]{1,0:T(8,128)(2,1)S(1)} %pad_maximum_fusion.2.refs_3_), channel_id=1, source_target_pairs={{0,1},{1,0},{2,3},{3,2},{4,5},{5,4},{6,7},{7,6},{8,9},{9,8},{10,11... | collective-permute-start | bytes 196616 | tf_op jit(solution)/shard_map/ppermute | solution.py:31
  42.4 5.5 %collective-permute-start.15 = (bf16[256,128]{1,0:T(8,128)(2,1)S(1)}, bf16[256,128]{1,0:T(8,128)(2,1)S(1)}, u32[]{:S(2)}, u32[]{:S(2)}) collective-permute-start(bf16[256,128]{1,0:T(8,128)(2,1)S(1)} %get-tuple-element.23.refs_0_), channel_id=1, source_target_pairs={{0,64},{2,66},{4,68},{6,70},{8,72},{10,74},{12,76},{14,78},{16,80}... | collective-permute-start | bytes 196616 | tf_op jit(solution)/shard_map/ppermute | solution.py:19
  43.7 5.4 %collective-permute-start.16 = (bf16[256,128]{1,0:T(8,128)(2,1)S(1)}, bf16[256,128]{1,0:T(8,128)(2,1)S(1)}, u32[]{:S(2)}, u32[]{:S(2)}) collective-permute-start(bf16[256,128]{1,0:T(8,128)(2,1)S(1)} %get-tuple-element.24), channel_id=1, source_target_pairs={{0,128},{2,130},{4,132},{6,134},{8,136},{10,138},{12,140},{14,142}... | collective-permute-start | bytes 196616 | tf_op jit(solution)/shard_map/ppermute | solution.py:19
  46.4 4.5 %copy-start = (f32[128,256]{1,0:T(8,128)S(1)}, f32[128,256]{1,0:T(8,128)}, u32[]{:S(2)}) copy-start(f32[128,256]{1,0:T(8,128)} %refs_5_.1) | copy-start | bytes 393220
  46.4 4.5 %collective-permute-start.17 = (bf16[256,128]{1,0:T(8,128)(2,1)S(1)}, bf16[256,128]{1,0:T(8,128)(2,1)S(1)}, u32[]{:S(2)}, u32[]{:S(2)}) collective-permute-start(bf16[256,128]{1,0:T(8,128)(2,1)S(1)} %get-tuple-element.25), channel_id=1, source_target_pairs={{0,192},{2,194},{4,196},{6,198},{8,200},{10,202},{12,204},{14,206}... | collective-permute-start | bytes 196616 | tf_op jit(solution)/shard_map/ppermute | solution.py:19
  51.3 3.3 %collective-permute-start.20 = (f32[64,256]{1,0:T(8,128)S(1)}, f32[64,256]{1,0:T(8,128)S(1)}, u32[]{:S(2)}, u32[]{:S(2)}) collective-permute-start(f32[64,256]{1,0:T(8,128)S(1)} %get-tuple-element.29), channel_id=1, source_target_pairs={{0,2},{2,0},{4,6},{6,4},{8,10},{10,8},{12,14},{14,12},{16,18},{18,... | collective-permute-start | bytes 196616 | tf_op jit(solution)/shard_map/ppermute | solution.py:19
  53.5 8.9 %collective-permute-start.19 = (bf16[256,128]{1,0:T(8,128)(2,1)S(1)}, bf16[256,128]{1,0:T(8,128)(2,1)S(1)}, u32[]{:S(2)}, u32[]{:S(2)}) collective-permute-start(bf16[256,128]{1,0:T(8,128)(2,1)S(1)} %get-tuple-element.27), channel_id=1, source_target_pairs={{0,1},{1,0},{2,3},{3,2},{4,5},{5,4},{6,7},{7,6},{8,9},{9,8},{10,11... | collective-permute-start | bytes 196616 | tf_op jit(solution)/shard_map/ppermute | solution.py:31
  54.6 7.8 %collective-permute-start.22 = (f32[64,256]{1,0:T(8,128)S(1)}, f32[64,256]{1,0:T(8,128)S(1)}, u32[]{:S(2)}, u32[]{:S(2)}) collective-permute-start(f32[64,256]{1,0:T(8,128)S(1)} %add.83), channel_id=1, source_target_pairs={{0,8},{2,10},{4,12},{6,14},{8,0},{10,2},{12,4},{14,6},{16,24},{18,... | collective-permute-start | bytes 196616 | tf_op jit(solution)/shard_map/ppermute | solution.py:19
  55.8 6.7 %collective-permute-start.23 = (f32[64,256]{1,0:T(8,128)S(1)}, f32[64,256]{1,0:T(8,128)S(1)}, u32[]{:S(2)}, u32[]{:S(2)}) collective-permute-start(f32[64,256]{1,0:T(8,128)S(1)} %add.83), channel_id=1, source_target_pairs={{0,12},{2,14},{4,8},{6,10},{8,4},{10,6},{12,0},{14,2},{16,28},{18,... | collective-permute-start | bytes 196616 | tf_op jit(solution)/shard_map/ppermute | solution.py:19
  57.4 5.1 %collective-permute-start.21 = (f32[64,256]{1,0:T(8,128)S(1)}, f32[64,256]{1,0:T(8,128)S(1)}, u32[]{:S(2)}, u32[]{:S(2)}) collective-permute-start(f32[64,256]{1,0:T(8,128)S(1)} %add.83), channel_id=1, source_target_pairs={{0,4},{2,6},{4,0},{6,2},{8,12},{10,14},{12,8},{14,10},{16,20},{18,... | collective-permute-start | bytes 196616 | tf_op jit(solution)/shard_map/ppermute | solution.py:19
  62.5 4.1 %collective-permute-start.26 = (bf16[64,256]{1,0:T(8,128)(2,1)S(1)}, bf16[64,256]{1,0:T(8,128)(2,1)S(1)}, u32[]{:S(2)}, u32[]{:S(2)}) collective-permute-start(bf16[64,256]{1,0:T(8,128)(2,1)S(1)} %add_convert_fusion.1), channel_id=1, source_target_pairs={{0,192},{2,194},{4,196},{6,198},{8,200},{10,202},{12,204},{14,206}... | collective-permute-start | bytes 98312 | tf_op jit(solution)/shard_map/ppermute | solution.py:19
  62.6 4.4 %collective-permute-start.25 = (bf16[64,256]{1,0:T(8,128)(2,1)S(1)}, bf16[64,256]{1,0:T(8,128)(2,1)S(1)}, u32[]{:S(2)}, u32[]{:S(2)}) collective-permute-start(bf16[64,256]{1,0:T(8,128)(2,1)S(1)} %add_convert_fusion.1), channel_id=1, source_target_pairs={{0,128},{2,130},{4,132},{6,134},{8,136},{10,138},{12,140},{14,142}... | collective-permute-start | bytes 98312 | tf_op jit(solution)/shard_map/ppermute | solution.py:19
  62.7 5.0 %collective-permute-start.24 = (bf16[64,256]{1,0:T(8,128)(2,1)S(1)}, bf16[64,256]{1,0:T(8,128)(2,1)S(1)}, u32[]{:S(2)}, u32[]{:S(2)}) collective-permute-start(bf16[64,256]{1,0:T(8,128)(2,1)S(1)} %add_convert_fusion.1), channel_id=1, source_target_pairs={{0,64},{2,66},{4,68},{6,70},{8,72},{10,74},{12,76},{14,78},{16,80}... | collective-permute-start | bytes 98312 | tf_op jit(solution)/shard_map/ppermute | solution.py:19
  67.8 4.9 %collective-permute-start.29 = (bf16[64,384]{1,0:T(8,128)(2,1)S(1)}, bf16[64,384]{1,0:T(8,128)(2,1)S(1)}, u32[]{:S(2)}, u32[]{:S(2)}) collective-permute-start(bf16[64,384]{1,0:T(8,128)(2,1)S(1)} %get-tuple-element.41), channel_id=1, source_target_pairs={{0,48},{2,50},{4,52},{6,54},{8,56},{10,58},{12,60},{14,62},{16,32}... | collective-permute-start | bytes 147464 | tf_op jit(solution)/shard_map/ppermute | solution.py:19
  69.6 5.0 %collective-permute-start.28 = (bf16[64,384]{1,0:T(8,128)(2,1)S(1)}, bf16[64,384]{1,0:T(8,128)(2,1)S(1)}, u32[]{:S(2)}, u32[]{:S(2)}) collective-permute-start(bf16[64,384]{1,0:T(8,128)(2,1)S(1)} %get-tuple-element.40), channel_id=1, source_target_pairs={{0,32},{2,34},{4,36},{6,38},{8,40},{10,42},{12,44},{14,46},{16,48}... | collective-permute-start | bytes 147464 | tf_op jit(solution)/shard_map/ppermute | solution.py:19
  69.6 5.0 %collective-permute-start.27 = (bf16[64,384]{1,0:T(8,128)(2,1)S(1)}, bf16[64,384]{1,0:T(8,128)(2,1)S(1)}, u32[]{:S(2)}, u32[]{:S(2)}) collective-permute-start(bf16[64,384]{1,0:T(8,128)(2,1)S(1)} %get-tuple-element.39), channel_id=1, source_target_pairs={{0,16},{2,18},{4,20},{6,22},{8,24},{10,26},{12,28},{14,30},{16,0},... | collective-permute-start | bytes 147464 | tf_op jit(solution)/shard_map/ppermute | solution.py:19
  74.7 3.3 %collective-permute-start.30 = (f32[64,256]{1,0:T(8,128)S(1)}, f32[64,256]{1,0:T(8,128)S(1)}, u32[]{:S(2)}, u32[]{:S(2)}) collective-permute-start(f32[64,256]{1,0:T(8,128)S(1)} %fusion.5.own_ref), channel_id=1, source_target_pairs={{0,2},{2,0},{4,6},{6,4},{8,10},{10,8},{12,14},{14,12},{16,18},{18,... | collective-permute-start | bytes 196616 | tf_op jit(solution)/shard_map/ppermute | solution.py:19

commit v6 on v5

--- a/solution.py
+++ b/solution.py
@@ -150,7 +150,8 @@
     grad_far_ref[...] = held[pl.ds(pl.multiple_of(64 - core * 64, 64), 64), :]
 
 
-def join_kernel(own_ref, other_ref, out_ref):
+def join_kernel(own_ref, other_ref, mixed_ref, mixed_out_ref, out_ref):
+    mixed_out_ref[...] = mixed_ref[...].astype(BF16)
     core = lax.axis_index("pts") & 1
     out_ref[pl.ds(pl.multiple_of(core * 64, 64), 64), :] = own_ref[...]
     out_ref[pl.ds(pl.multiple_of(64 - core * 64, 64), 64), :] = other_ref[...]
@@ -224,10 +225,11 @@
     mixed = (mixed[:64] + back[0][:, :128]) + (back[1][:, :128] + back[2][:, :128])
     back = [b[:, 128:] for b in back]
     grad = (grad.astype(F32) + back[0]) + (back[1] + back[2])
-    grad = in_vmem(
-        join_kernel, jax.ShapeDtypeStruct((128, 256), F32), [grad, swap(grad, CORE, 1)]
-    )
-    return mixed.astype(BF16), grad
+    return in_vmem(
+        join_kernel,
+        (jax.ShapeDtypeStruct((64, 128), BF16), jax.ShapeDtypeStruct((128, 256), F32)),
+        [grad, swap(grad, CORE, 1), mixed],
+    )
 
 
 def solution(mesh):

time: 78.7 us -> 78.7 us (level)
  transfers between devices with their start and end apart: 31 -> 31, of which waited for: 14 -> 14; matrix products, arithmetic and copies ran while one was open for 1% -> 0% of each run, Pallas kernels for 13% -> 13%
where the time goes in v6:
time: 78.7 us; the launch traced here: 78.6 us
  starting transfers between devices  45.1 us (57%)
  waiting for transfers between devices  19.4 us (25%)
  Pallas kernels  11.3 us (14%)
  other arithmetic  1.55 us (2%)
  between operations  0.95 us (1%)
    ppermute x25, starting transfers between devices, swap(): lax.ppermute(value, 'pts', [(i, i ^ mask << place) for i in range(PTS)])  32.8 us
    ppermute x25, waiting for transfers between devices, swap(): lax.ppermute(value, 'pts', [(i, i ^ mask << place) for i in range(PTS)])  12.6 us
    pallas_call x8, Pallas kernels, in_vmem(): pl.pallas_call(kernel, out_shape=out, in_specs=[pl.BlockSpec(memory_space...  11.3 us
    ppermute x2, starting transfers between devices, swap_lab(): return lax.ppermute(value, 'lab', [(0, 1), (1, 0)])  8.04 us
    ppermute x2, waiting for transfers between devices, swap_lab(): return lax.ppermute(value, 'lab', [(0, 1), (1, 0)])  4.56 us
    ppermute x4, starting transfers between devices, swap_ring(): return lax.ppermute(value, 'pts', pairs)  4.22 us
    ppermute x4, waiting for transfers between devices, swap_ring(): return lax.ppermute(value, 'pts', pairs)  2.16 us
  transfers between devices with their start and end apart: 31, of which 14 were waited for; matrix products, arithmetic and copies ran while one was open for 0% of the time, Pallas kernels for 13%

profile of v6, /device:TPU:1, one launch (start us, length us, event | category | flops | bytes accessed | tf_op | source)
XLA Modules:
  0.0 78.6 jit_solution(13987097282466491649)
XLA Ops:
  0.6 1.2 %fusion.3 = (f32[1024]{0:T(1024)S(1)}, bf16[1024,128]{1,0:T(8,128)(2,1)S(1)}) fusion(bf16[1024,128]{1,0:T(8,128)(2,1)} %param.7, f32[128]{0:T(128)} %weights_ref.1), kind=kLoop, calls=%fused_computation.5 | loop fusion | flops 916480 | bytes 528896 | tf_op jit(solution)/shard_map/reduce_sum | solution.py:163
  2.0 0.3 concatenate.27.refs_0_
  2.3 3.3 %collective-permute-start = (bf16[1056,256]{1,0:T(8,128)(2,1)S(1)}, bf16[1056,256]{1,0:T(8,128)(2,1)S(1)}, u32[]{:S(2)}, u32[]{:S(2)}) collective-permute-start(bf16[1056,256]{1,0:T(8,128)(2,1)S(1)} %concatenate.27.refs_0_), channel_id=1, source_target_pairs={{0,2},{2,0},{4,6},{6,4},{8,10},{10,8},{12,14},{14,12},{16,18},{18,... | collective-permute-start | bytes 1622024 | tf_op jit(solution)/shard_map/ppermute | solution.py:19
  5.6 0.8 collective-permute-start.7
  6.4 0.7 collective-permute-start.8
  7.1 0.1 collective-permute-done._.refs_1_
  7.2 3.6 %collective-permute-start.3 = (bf16[128,128]{1,0:T(8,128)(2,1)S(1)}, bf16[128,128]{1,0:T(8,128)(2,1)S(1)}, u32[]{:S(2)}, u32[]{:S(2)}) collective-permute-start(bf16[128,128]{1,0:T(8,128)(2,1)S(1)} %shard_map.77), channel_id=1, source_target_pairs={{0,48},{2,50},{4,52},{6,54},{8,56},{10,58},{12,60},{14,62},{16,32}... | collective-permute-start | bytes 98312 | tf_op jit(solution)/shard_map/ppermute | solution.py:19
  10.9 0.4 collective-permute-start.1
  11.2 0.9 %collective-permute-done.3 = bf16[128,128]{1,0:T(8,128)(2,1)S(1)} collective-permute-done((bf16[128,128]{1,0:T(8,128)(2,1)S(1)}, bf16[128,128]{1,0:T(8,128)(2,1)S(1)}, u32[]{:S(2)}, u32[]{:S(2)}) %collective-permute-start.3) | collective-permute-done | bytes 32800 | tf_op jit(solution)/shard_map/ppermute | solution.py:19
  12.2 2.7 %collective-permute-done.2 = bf16[128,128]{1,0:T(8,128)(2,1)S(1)} collective-permute-done((bf16[128,128]{1,0:T(8,128)(2,1)S(1)}, bf16[128,128]{1,0:T(8,128)(2,1)S(1)}, u32[]{:S(2)}, u32[]{:S(2)}) %collective-permute-start.2) | collective-permute-done | bytes 32800 | tf_op jit(solution)/shard_map/ppermute | solution.py:19
  14.9 1.4 %collective-permute-start.4 = (bf16[256,128]{1,0:T(8,128)(2,1)S(1)}, bf16[256,128]{1,0:T(8,128)(2,1)S(1)}, u32[]{:S(2)}, u32[]{:S(2)}) collective-permute-start(bf16[256,128]{1,0:T(8,128)(2,1)S(1)} %pad_maximum_fusion.1.refs_0_), channel_id=1, source_target_pairs={{0,64},{2,66},{4,68},{6,70},{8,72},{10,74},{12,76},{14,78},{16,80}... | collective-permute-start | bytes 196616 | tf_op jit(solution)/shard_map/ppermute | solution.py:19
  16.3 2.6 %collective-permute-start.5 = (bf16[256,128]{1,0:T(8,128)(2,1)S(1)}, bf16[256,128]{1,0:T(8,128)(2,1)S(1)}, u32[]{:S(2)}, u32[]{:S(2)}) collective-permute-start(bf16[256,128]{1,0:T(8,128)(2,1)S(1)} %pad_maximum_fusion.1.refs_0_), channel_id=1, source_target_pairs={{0,128},{2,130},{4,132},{6,134},{8,136},{10,138},{12,140},{14,142}... | collective-permute-start | bytes 196616 | tf_op jit(solution)/shard_map/ppermute | solution.py:19
  18.9 0.5 collective-permute-done.7.refs_2_.right_ref
  19.5 1.6 %collective-permute-done.8.refs_3_.left_ref = bf16[1056,256]{1,0:T(8,128)(2,1)S(1)} collective-permute-done((bf16[1056,256]{1,0:T(8,128)(2,1)S(1)}, bf16[1056,256]{1,0:T(8,128)(2,1)S(1)}, u32[]{:S(2)}, u32[]{:S(2)}) %collective-permute-start.8) | collective-permute-done | bytes 540704 | tf_op jit(solution)/shard_map/ppermute | solution.py:27
  21.3 2.7 %collective-permute-start.11 = (bf16[528,256]{1,0:T(8,128)(2,1)S(1)}, bf16[528,256]{1,0:T(8,128)(2,1)S(1)}, u32[]{:S(2)}, u32[]{:S(2)}) collective-permute-start(bf16[528,256]{1,0:T(8,128)(2,1)S(1)} %get-tuple-element.20), channel_id=1, source_target_pairs={{0,12},{2,14},{4,0},{6,2},{8,4},{10,6},{12,8},{14,10},{16,28},{18,... | collective-permute-start | bytes 811016 | tf_op jit(solution)/shard_map/ppermute | solution.py:27
  24.0 1.8 %collective-permute-start.9 = (bf16[1056,256]{1,0:T(8,128)(2,1)S(1)}, bf16[1056,256]{1,0:T(8,128)(2,1)S(1)}, u32[]{:S(2)}, u32[]{:S(2)}) collective-permute-start(bf16[1056,256]{1,0:T(8,128)(2,1)S(1)} %get-tuple-element.62), channel_id=1, source_target_pairs={{0,2},{2,0},{4,6},{6,4},{8,10},{10,8},{12,14},{14,12},{16,18},{18,... | collective-permute-start | bytes 1622024 | tf_op jit(solution)/shard_map/ppermute | solution.py:19
  25.8 0.3 collective-permute-start.10
  26.1 0.2 shard_map.78
  26.4 4.8 %shard_map.79 = (f32[1024,128]{1,0:T(8,128)S(1)}, bf16[16,256]{1,0:T(8,128)(2,1)S(1)}) custom-call(bf16[1024,128]{1,0:T(8,128)(2,1)S(1)} %get-tuple-element.16.rows_ref, f32[1024,128]{1,0:T(8,128)S(1)} %get-tuple-element.17.term_ref, bf16[1056,256]{1,0:T(8,128)(2,1)S(1)} %concatenate.27.refs_0_, bf16[1056,256]{1,0:T(8,128)(2,1)S(1)} %collective-permute-done._.refs_1_, ...), custom_call_target="tpu_custom_call" | custom-call | flops 1000 | bytes 2097152 | tf_op jit(solution)/shard_map/pallas_call | solution.py:81
  31.3 0.3 collective-permute-start.13
  31.6 0.2 collective-permute-start.14
  31.9 6.9 %collective-permute-start.18 = (bf16[256,128]{1,0:T(8,128)(2,1)S(1)}, bf16[256,128]{1,0:T(8,128)(2,1)S(1)}, u32[]{:S(2)}, u32[]{:S(2)}) collective-permute-start(bf16[256,128]{1,0:T(8,128)(2,1)S(1)} %pad_maximum_fusion.2.refs_3_), channel_id=1, source_target_pairs={{0,1},{1,0},{2,3},{3,2},{4,5},{5,4},{6,7},{7,6},{8,9},{9,8},{10,11... | collective-permute-start | bytes 196616 | tf_op jit(solution)/shard_map/ppermute | solution.py:31
  38.8 3.6 %shard_map.81 = (bf16[256,128]{1,0:T(8,128)(2,1)S(1)}, bf16[256,128]{1,0:T(8,128)(2,1)S(1)}, bf16[256,128]{1,0:T(8,128)(2,1)S(1)}) custom-call(bf16[1024,128]{1,0:T(8,128)(2,1)S(1)} %get-tuple-element.16.rows_ref, f32[1024,128]{1,0:T(8,128)S(1)} %get-tuple-element.17.term_ref, f32[1024,128]{1,0:T(8,128)S(1)} %get-tuple-element.18.start, ...), custom_call_target="tpu_custom_call" | custom-call | flops 1000 | bytes 2097152 | tf_op jit(solution)/shard_map/pallas_call | solution.py:81
  42.4 1.4 %collective-permute-start.15 = (bf16[256,128]{1,0:T(8,128)(2,1)S(1)}, bf16[256,128]{1,0:T(8,128)(2,1)S(1)}, u32[]{:S(2)}, u32[]{:S(2)}) collective-permute-start(bf16[256,128]{1,0:T(8,128)(2,1)S(1)} %get-tuple-element.23.refs_0_), channel_id=1, source_target_pairs={{0,64},{2,66},{4,68},{6,70},{8,72},{10,74},{12,76},{14,78},{16,80}... | collective-permute-start | bytes 196616 | tf_op jit(solution)/shard_map/ppermute | solution.py:19
  43.7 2.6 %collective-permute-start.16 = (bf16[256,128]{1,0:T(8,128)(2,1)S(1)}, bf16[256,128]{1,0:T(8,128)(2,1)S(1)}, u32[]{:S(2)}, u32[]{:S(2)}) collective-permute-start(bf16[256,128]{1,0:T(8,128)(2,1)S(1)} %get-tuple-element.24), channel_id=1, source_target_pairs={{0,128},{2,130},{4,132},{6,134},{8,136},{10,138},{12,140},{14,142}... | collective-permute-start | bytes 196616 | tf_op jit(solution)/shard_map/ppermute | solution.py:19
  46.4 1.5 %shard_map.82.own = f32[256,128]{1,0:T(8,128)S(1)} custom-call(bf16[1024,128]{1,0:T(8,128)(2,1)S(1)} %get-tuple-element.16.rows_ref, f32[1024,128]{1,0:T(8,128)S(1)} %get-tuple-element.17.term_ref, f32[1024,128]{1,0:T(8,128)S(1)} %get-tuple-element.18.start, bf16[256,128]{1,0:T(8,128)(2,1)S(1)} %get-tuple-element.23.refs_0_, ...), custom_call_target="tpu_custom_call" | custom-call | flops 1000 | bytes 2097152 | tf_op jit(solution)/shard_map/pallas_call | solution.py:81
  47.9 1.2 %collective-permute-done.16.refs_1_ = bf16[256,128]{1,0:T(8,128)(2,1)S(1)} collective-permute-done((bf16[256,128]{1,0:T(8,128)(2,1)S(1)}, bf16[256,128]{1,0:T(8,128)(2,1)S(1)}, u32[]{:S(2)}, u32[]{:S(2)}) %collective-permute-start.16) | collective-permute-done | bytes 65568 | tf_op jit(solution)/shard_map/ppermute | solution.py:19
  49.1 1.7 %collective-permute-done.17.refs_2_ = bf16[256,128]{1,0:T(8,128)(2,1)S(1)} collective-permute-done((bf16[256,128]{1,0:T(8,128)(2,1)S(1)}, bf16[256,128]{1,0:T(8,128)(2,1)S(1)}, u32[]{:S(2)}, u32[]{:S(2)}) %collective-permute-start.17) | collective-permute-done | bytes 65568 | tf_op jit(solution)/shard_map/ppermute | solution.py:19
  50.8 0.5 shard_map.83
  51.3 2.2 %collective-permute-start.19 = (f32[64,256]{1,0:T(8,128)S(1)}, f32[64,256]{1,0:T(8,128)S(1)}, u32[]{:S(2)}, u32[]{:S(2)}) collective-permute-start(f32[64,256]{1,0:T(8,128)S(1)} %get-tuple-element.27), channel_id=1, source_target_pairs={{0,2},{2,0},{4,6},{6,4},{8,10},{10,8},{12,14},{14,12},{16,18},{18,... | collective-permute-start | bytes 196616 | tf_op jit(solution)/shard_map/ppermute | solution.py:19
  53.5 1.1 %collective-permute-start.26 = (bf16[256,128]{1,0:T(8,128)(2,1)S(1)}, bf16[256,128]{1,0:T(8,128)(2,1)S(1)}, u32[]{:S(2)}, u32[]{:S(2)}) collective-permute-start(bf16[256,128]{1,0:T(8,128)(2,1)S(1)} %get-tuple-element.29), channel_id=1, source_target_pairs={{0,1},{1,0},{2,3},{3,2},{4,5},{5,4},{6,7},{7,6},{8,9},{9,8},{10,11... | collective-permute-start | bytes 196616 | tf_op jit(solution)/shard_map/ppermute | solution.py:31
  54.6 1.1 %collective-permute-start.21 = (f32[64,256]{1,0:T(8,128)S(1)}, f32[64,256]{1,0:T(8,128)S(1)}, u32[]{:S(2)}, u32[]{:S(2)}) collective-permute-start(f32[64,256]{1,0:T(8,128)S(1)} %add.82), channel_id=1, source_target_pairs={{0,8},{2,10},{4,12},{6,14},{8,0},{10,2},{12,4},{14,6},{16,24},{18,... | collective-permute-start | bytes 196616 | tf_op jit(solution)/shard_map/ppermute | solution.py:19
  55.8 1.6 %collective-permute-start.22 = (f32[64,256]{1,0:T(8,128)S(1)}, f32[64,256]{1,0:T(8,128)S(1)}, u32[]{:S(2)}, u32[]{:S(2)}) collective-permute-start(f32[64,256]{1,0:T(8,128)S(1)} %add.82), channel_id=1, source_target_pairs={{0,12},{2,14},{4,8},{6,10},{8,4},{10,6},{12,0},{14,2},{16,28},{18,... | collective-permute-start | bytes 196616 | tf_op jit(solution)/shard_map/ppermute | solution.py:19
  57.4 0.5 collective-permute-start.20
  57.9 4.6 %collective-permute-done.26 = bf16[256,128]{1,0:T(8,128)(2,1)S(1)} collective-permute-done((bf16[256,128]{1,0:T(8,128)(2,1)S(1)}, bf16[256,128]{1,0:T(8,128)(2,1)S(1)}, u32[]{:S(2)}, u32[]{:S(2)}) %collective-permute-start.26) | collective-permute-done | bytes 65568 | tf_op jit(solution)/shard_map/ppermute | solution.py:31
  62.5 0.1 collective-permute-start.25
  62.6 0.1 collective-permute-start.24
  62.7 3.1 %collective-permute-start.23 = (bf16[64,256]{1,0:T(8,128)(2,1)S(1)}, bf16[64,256]{1,0:T(8,128)(2,1)S(1)}, u32[]{:S(2)}, u32[]{:S(2)}) collective-permute-start(bf16[64,256]{1,0:T(8,128)(2,1)S(1)} %add_convert_fusion.1), channel_id=1, source_target_pairs={{0,64},{2,66},{4,68},{6,70},{8,72},{10,74},{12,76},{14,78},{16,80}... | collective-permute-start | bytes 98312 | tf_op jit(solution)/shard_map/ppermute | solution.py:19
  65.8 0.7 collective-permute-done.25
  66.6 0.4 collective-permute-done.24
  67.0 0.8 %collective-permute-done.23 = bf16[64,256]{1,0:T(8,128)(2,1)S(1)} collective-permute-done((bf16[64,256]{1,0:T(8,128)(2,1)S(1)}, bf16[64,256]{1,0:T(8,128)(2,1)S(1)}, u32[]{:S(2)}, u32[]{:S(2)}) %collective-permute-start.23) | collective-permute-done | bytes 32800 | tf_op jit(solution)/shard_map/ppermute | solution.py:19
  67.8 1.8 %collective-permute-start.29 = (bf16[64,384]{1,0:T(8,128)(2,1)S(1)}, bf16[64,384]{1,0:T(8,128)(2,1)S(1)}, u32[]{:S(2)}, u32[]{:S(2)}) collective-permute-start(bf16[64,384]{1,0:T(8,128)(2,1)S(1)} %get-tuple-element.41), channel_id=1, source_target_pairs={{0,48},{2,50},{4,52},{6,54},{8,56},{10,58},{12,60},{14,62},{16,32}... | collective-permute-start | bytes 147464 | tf_op jit(solution)/shard_map/ppermute | solution.py:19
  69.6 1.9 %collective-permute-start.27 = (bf16[64,384]{1,0:T(8,128)(2,1)S(1)}, bf16[64,384]{1,0:T(8,128)(2,1)S(1)}, u32[]{:S(2)}, u32[]{:S(2)}) collective-permute-start(bf16[64,384]{1,0:T(8,128)(2,1)S(1)} %get-tuple-element.39), channel_id=1, source_target_pairs={{0,16},{2,18},{4,20},{6,22},{8,24},{10,26},{12,28},{14,30},{16,0},... | collective-permute-start | bytes 147464 | tf_op jit(solution)/shard_map/ppermute | solution.py:19
  71.5 1.3 %collective-permute-done.29 = bf16[64,384]{1,0:T(8,128)(2,1)S(1)} collective-permute-done((bf16[64,384]{1,0:T(8,128)(2,1)S(1)}, bf16[64,384]{1,0:T(8,128)(2,1)S(1)}, u32[]{:S(2)}, u32[]{:S(2)}) %collective-permute-start.29) | collective-permute-done | bytes 49184 | tf_op jit(solution)/shard_map/ppermute | solution.py:19
  72.8 1.8 %collective-permute-done.28 = bf16[64,384]{1,0:T(8,128)(2,1)S(1)} collective-permute-done((bf16[64,384]{1,0:T(8,128)(2,1)S(1)}, bf16[64,384]{1,0:T(8,128)(2,1)S(1)}, u32[]{:S(2)}, u32[]{:S(2)}) %collective-permute-start.28) | collective-permute-done | bytes 49184 | tf_op jit(solution)/shard_map/ppermute | solution.py:19
  74.7 2.4 %collective-permute-start.30 = (f32[64,256]{1,0:T(8,128)S(1)}, f32[64,256]{1,0:T(8,128)S(1)}, u32[]{:S(2)}, u32[]{:S(2)}) collective-permute-start(f32[64,256]{1,0:T(8,128)S(1)} %fusion.5.own_ref), channel_id=1, source_target_pairs={{0,2},{2,0},{4,6},{6,4},{8,10},{10,8},{12,14},{14,12},{16,18},{18,... | collective-permute-start | bytes 196616 | tf_op jit(solution)/shard_map/ppermute | solution.py:19
  77.1 0.9 %collective-permute-done.30.other_ref = f32[64,256]{1,0:T(8,128)S(1)} collective-permute-done((f32[64,256]{1,0:T(8,128)S(1)}, f32[64,256]{1,0:T(8,128)S(1)}, u32[]{:S(2)}, u32[]{:S(2)}) %collective-permute-start.30) | collective-permute-done | bytes 65568 | tf_op jit(solution)/shard_map/ppermute | solution.py:19
  78.0 0.7 shard_map.84
  (63 shorter events, 0.6 us)
Async XLA Ops:
  0.6 1.3 %copy-start.4 = (bf16[1024,128]{1,0:T(8,128)(2,1)S(1)}, bf16[1024,128]{1,0:T(8,128)(2,1)}, u32[]{:S(2)}) copy-start(bf16[1024,128]{1,0:T(8,128)(2,1)} %param.9) | copy-start | bytes 786436
  2.0 5.2 %copy-start.1 = (bf16[64,128]{1,0:T(8,128)(2,1)S(1)}, bf16[64,128]{1,0:T(8,128)(2,1)}, u32[]{:S(2)}) copy-start(bf16[64,128]{1,0:T(8,128)(2,1)} %slab_ref.1) | copy-start | bytes 49156
  2.0 5.2 %copy-start.2 = (bf16[64,128]{1,0:T(8,128)(2,1)S(1)}, bf16[64,128]{1,0:T(8,128)(2,1)}, u32[]{:S(2)}) copy-start(bf16[64,128]{1,0:T(8,128)(2,1)} %cotangent_ref.1) | copy-start | bytes 49156
  2.3 4.9 %collective-permute-start = (bf16[1056,256]{1,0:T(8,128)(2,1)S(1)}, bf16[1056,256]{1,0:T(8,128)(2,1)S(1)}, u32[]{:S(2)}, u32[]{:S(2)}) collective-permute-start(bf16[1056,256]{1,0:T(8,128)(2,1)S(1)} %concatenate.27.refs_0_), channel_id=1, source_target_pairs={{0,2},{2,0},{4,6},{6,4},{8,10},{10,8},{12,14},{14,12},{16,18},{18,... | collective-permute-start | bytes 1622024 | tf_op jit(solution)/shard_map/ppermute | solution.py:19
  5.6 13.8 %collective-permute-start.7 = (bf16[1056,256]{1,0:T(8,128)(2,1)S(1)}, bf16[1056,256]{1,0:T(8,128)(2,1)S(1)}, u32[]{:S(2)}, u32[]{:S(2)}) collective-permute-start(bf16[1056,256]{1,0:T(8,128)(2,1)S(1)} %concatenate.27.refs_0_), channel_id=1, source_target_pairs={{0,12},{2,14},{4,0},{6,2},{8,4},{10,6},{12,8},{14,10},{16,28},{18,... | collective-permute-start | bytes 1622024 | tf_op jit(solution)/shard_map/ppermute | solution.py:27
  6.4 14.7 %collective-permute-start.8 = (bf16[1056,256]{1,0:T(8,128)(2,1)S(1)}, bf16[1056,256]{1,0:T(8,128)(2,1)S(1)}, u32[]{:S(2)}, u32[]{:S(2)}) collective-permute-start(bf16[1056,256]{1,0:T(8,128)(2,1)S(1)} %concatenate.27.refs_0_), channel_id=1, source_target_pairs={{0,4},{2,6},{4,8},{6,10},{8,12},{10,14},{12,0},{14,2},{16,20},{18,... | collective-permute-start | bytes 1622024 | tf_op jit(solution)/shard_map/ppermute | solution.py:27
  7.2 5.0 %collective-permute-start.3 = (bf16[128,128]{1,0:T(8,128)(2,1)S(1)}, bf16[128,128]{1,0:T(8,128)(2,1)S(1)}, u32[]{:S(2)}, u32[]{:S(2)}) collective-permute-start(bf16[128,128]{1,0:T(8,128)(2,1)S(1)} %shard_map.77), channel_id=1, source_target_pairs={{0,48},{2,50},{4,52},{6,54},{8,56},{10,58},{12,60},{14,62},{16,32}... | collective-permute-start | bytes 98312 | tf_op jit(solution)/shard_map/ppermute | solution.py:19
  10.8 4.1 %collective-permute-start.2 = (bf16[128,128]{1,0:T(8,128)(2,1)S(1)}, bf16[128,128]{1,0:T(8,128)(2,1)S(1)}, u32[]{:S(2)}, u32[]{:S(2)}) collective-permute-start(bf16[128,128]{1,0:T(8,128)(2,1)S(1)} %shard_map.77), channel_id=1, source_target_pairs={{0,32},{2,34},{4,36},{6,38},{8,40},{10,42},{12,44},{14,46},{16,48}... | collective-permute-start | bytes 98312 | tf_op jit(solution)/shard_map/ppermute | solution.py:19
  10.9 4.1 %collective-permute-start.1 = (bf16[128,128]{1,0:T(8,128)(2,1)S(1)}, bf16[128,128]{1,0:T(8,128)(2,1)S(1)}, u32[]{:S(2)}, u32[]{:S(2)}) collective-permute-start(bf16[128,128]{1,0:T(8,128)(2,1)S(1)} %shard_map.77), channel_id=1, source_target_pairs={{0,16},{2,18},{4,20},{6,22},{8,24},{10,26},{12,28},{14,30},{16,0},... | collective-permute-start | bytes 98312 | tf_op jit(solution)/shard_map/ppermute | solution.py:19
  14.9 6.2 %collective-permute-start.4 = (bf16[256,128]{1,0:T(8,128)(2,1)S(1)}, bf16[256,128]{1,0:T(8,128)(2,1)S(1)}, u32[]{:S(2)}, u32[]{:S(2)}) collective-permute-start(bf16[256,128]{1,0:T(8,128)(2,1)S(1)} %pad_maximum_fusion.1.refs_0_), channel_id=1, source_target_pairs={{0,64},{2,66},{4,68},{6,70},{8,72},{10,74},{12,76},{14,78},{16,80}... | collective-permute-start | bytes 196616 | tf_op jit(solution)/shard_map/ppermute | solution.py:19
  16.3 9.5 %collective-permute-start.5 = (bf16[256,128]{1,0:T(8,128)(2,1)S(1)}, bf16[256,128]{1,0:T(8,128)(2,1)S(1)}, u32[]{:S(2)}, u32[]{:S(2)}) collective-permute-start(bf16[256,128]{1,0:T(8,128)(2,1)S(1)} %pad_maximum_fusion.1.refs_0_), channel_id=1, source_target_pairs={{0,128},{2,130},{4,132},{6,134},{8,136},{10,138},{12,140},{14,142}... | collective-permute-start | bytes 196616 | tf_op jit(solution)/shard_map/ppermute | solution.py:19
  18.9 7.2 %collective-permute-start.6 = (bf16[256,128]{1,0:T(8,128)(2,1)S(1)}, bf16[256,128]{1,0:T(8,128)(2,1)S(1)}, u32[]{:S(2)}, u32[]{:S(2)}) collective-permute-start(bf16[256,128]{1,0:T(8,128)(2,1)S(1)} %pad_maximum_fusion.1.refs_0_), channel_id=1, source_target_pairs={{0,192},{2,194},{4,196},{6,198},{8,200},{10,202},{12,204},{14,206}... | collective-permute-start | bytes 196616 | tf_op jit(solution)/shard_map/ppermute | solution.py:19
  21.2 10.0 %collective-permute-start.12 = (bf16[528,256]{1,0:T(8,128)(2,1)S(1)}, bf16[528,256]{1,0:T(8,128)(2,1)S(1)}, u32[]{:S(2)}, u32[]{:S(2)}) collective-permute-start(bf16[528,256]{1,0:T(8,128)(2,1)S(1)} %get-tuple-element.22), channel_id=1, source_target_pairs={{0,4},{2,6},{4,8},{6,10},{8,12},{10,14},{12,0},{14,2},{16,20},{18,... | collective-permute-start | bytes 811016 | tf_op jit(solution)/shard_map/ppermute | solution.py:27
  21.3 10.0 %collective-permute-start.11 = (bf16[528,256]{1,0:T(8,128)(2,1)S(1)}, bf16[528,256]{1,0:T(8,128)(2,1)S(1)}, u32[]{:S(2)}, u32[]{:S(2)}) collective-permute-start(bf16[528,256]{1,0:T(8,128)(2,1)S(1)} %get-tuple-element.20), channel_id=1, source_target_pairs={{0,12},{2,14},{4,0},{6,2},{8,4},{10,6},{12,8},{14,10},{16,28},{18,... | collective-permute-start | bytes 811016 | tf_op jit(solution)/shard_map/ppermute | solution.py:27
  24.0 2.1 %copy-start.3 = (f32[128]{0:T(128)S(1)}, f32[128]{0:T(128)}, u32[]{:S(2)}) copy-start(f32[128]{0:T(128)} %weights_ref.1) | copy-start | bytes 1540
  24.0 14.8 %collective-permute-start.9 = (bf16[1056,256]{1,0:T(8,128)(2,1)S(1)}, bf16[1056,256]{1,0:T(8,128)(2,1)S(1)}, u32[]{:S(2)}, u32[]{:S(2)}) collective-permute-start(bf16[1056,256]{1,0:T(8,128)(2,1)S(1)} %get-tuple-element.62), channel_id=1, source_target_pairs={{0,2},{2,0},{4,6},{6,4},{8,10},{10,8},{12,14},{14,12},{16,18},{18,... | collective-permute-start | bytes 1622024 | tf_op jit(solution)/shard_map/ppermute | solution.py:19
  25.8 12.9 %collective-permute-start.10 = (bf16[1056,256]{1,0:T(8,128)(2,1)S(1)}, bf16[1056,256]{1,0:T(8,128)(2,1)S(1)}, u32[]{:S(2)}, u32[]{:S(2)}) collective-permute-start(bf16[1056,256]{1,0:T(8,128)(2,1)S(1)} %get-tuple-element.61), channel_id=1, source_target_pairs={{0,2},{2,0},{4,6},{6,4},{8,10},{10,8},{12,14},{14,12},{16,18},{18,... | collective-permute-start | bytes 1622024 | tf_op jit(solution)/shard_map/ppermute | solution.py:19
  31.3 7.5 %collective-permute-start.13 = (bf16[528,256]{1,0:T(8,128)(2,1)S(1)}, bf16[528,256]{1,0:T(8,128)(2,1)S(1)}, u32[]{:S(2)}, u32[]{:S(2)}) collective-permute-start(bf16[528,256]{1,0:T(8,128)(2,1)S(1)} %get-tuple-element.60.refs_2_.refs_3_), channel_id=1, source_target_pairs={{0,2},{2,0},{4,6},{6,4},{8,10},{10,8},{12,14},{14,12},{16,18},{18,... | collective-permute-start | bytes 811016 | tf_op jit(solution)/shard_map/ppermute | solution.py:19
  31.6 7.2 %collective-permute-start.14 = (bf16[528,256]{1,0:T(8,128)(2,1)S(1)}, bf16[528,256]{1,0:T(8,128)(2,1)S(1)}, u32[]{:S(2)}, u32[]{:S(2)}) collective-permute-start(bf16[528,256]{1,0:T(8,128)(2,1)S(1)} %get-tuple-element.59.refs_3_.refs_4_), channel_id=1, source_target_pairs={{0,2},{2,0},{4,6},{6,4},{8,10},{10,8},{12,14},{14,12},{16,18},{18,... | collective-permute-start | bytes 811016 | tf_op jit(solution)/shard_map/ppermute | solution.py:19
  31.9 16.0 %collective-permute-start.18 = (bf16[256,128]{1,0:T(8,128)(2,1)S(1)}, bf16[256,128]{1,0:T(8,128)(2,1)S(1)}, u32[]{:S(2)}, u32[]{:S(2)}) collective-permute-start(bf16[256,128]{1,0:T(8,128)(2,1)S(1)} %pad_maximum_fusion.2.refs_3_), channel_id=1, source_target_pairs={{0,1},{1,0},{2,3},{3,2},{4,5},{5,4},{6,7},{7,6},{8,9},{9,8},{10,11... | collective-permute-start | bytes 196616 | tf_op jit(solution)/shard_map/ppermute | solution.py:31
  42.4 5.5 %collective-permute-start.15 = (bf16[256,128]{1,0:T(8,128)(2,1)S(1)}, bf16[256,128]{1,0:T(8,128)(2,1)S(1)}, u32[]{:S(2)}, u32[]{:S(2)}) collective-permute-start(bf16[256,128]{1,0:T(8,128)(2,1)S(1)} %get-tuple-element.23.refs_0_), channel_id=1, source_target_pairs={{0,64},{2,66},{4,68},{6,70},{8,72},{10,74},{12,76},{14,78},{16,80}... | collective-permute-start | bytes 196616 | tf_op jit(solution)/shard_map/ppermute | solution.py:19
  43.7 5.4 %collective-permute-start.16 = (bf16[256,128]{1,0:T(8,128)(2,1)S(1)}, bf16[256,128]{1,0:T(8,128)(2,1)S(1)}, u32[]{:S(2)}, u32[]{:S(2)}) collective-permute-start(bf16[256,128]{1,0:T(8,128)(2,1)S(1)} %get-tuple-element.24), channel_id=1, source_target_pairs={{0,128},{2,130},{4,132},{6,134},{8,136},{10,138},{12,140},{14,142}... | collective-permute-start | bytes 196616 | tf_op jit(solution)/shard_map/ppermute | solution.py:19
  46.4 4.5 %copy-start = (f32[128,256]{1,0:T(8,128)S(1)}, f32[128,256]{1,0:T(8,128)}, u32[]{:S(2)}) copy-start(f32[128,256]{1,0:T(8,128)} %refs_5_.1) | copy-start | bytes 393220
  46.4 4.5 %collective-permute-start.17 = (bf16[256,128]{1,0:T(8,128)(2,1)S(1)}, bf16[256,128]{1,0:T(8,128)(2,1)S(1)}, u32[]{:S(2)}, u32[]{:S(2)}) collective-permute-start(bf16[256,128]{1,0:T(8,128)(2,1)S(1)} %get-tuple-element.25), channel_id=1, source_target_pairs={{0,192},{2,194},{4,196},{6,198},{8,200},{10,202},{12,204},{14,206}... | collective-permute-start | bytes 196616 | tf_op jit(solution)/shard_map/ppermute | solution.py:19
  51.3 3.3 %collective-permute-start.19 = (f32[64,256]{1,0:T(8,128)S(1)}, f32[64,256]{1,0:T(8,128)S(1)}, u32[]{:S(2)}, u32[]{:S(2)}) collective-permute-start(f32[64,256]{1,0:T(8,128)S(1)} %get-tuple-element.27), channel_id=1, source_target_pairs={{0,2},{2,0},{4,6},{6,4},{8,10},{10,8},{12,14},{14,12},{16,18},{18,... | collective-permute-start | bytes 196616 | tf_op jit(solution)/shard_map/ppermute | solution.py:19
  53.5 8.9 %collective-permute-start.26 = (bf16[256,128]{1,0:T(8,128)(2,1)S(1)}, bf16[256,128]{1,0:T(8,128)(2,1)S(1)}, u32[]{:S(2)}, u32[]{:S(2)}) collective-permute-start(bf16[256,128]{1,0:T(8,128)(2,1)S(1)} %get-tuple-element.29), channel_id=1, source_target_pairs={{0,1},{1,0},{2,3},{3,2},{4,5},{5,4},{6,7},{7,6},{8,9},{9,8},{10,11... | collective-permute-start | bytes 196616 | tf_op jit(solution)/shard_map/ppermute | solution.py:31
  54.6 7.8 %collective-permute-start.21 = (f32[64,256]{1,0:T(8,128)S(1)}, f32[64,256]{1,0:T(8,128)S(1)}, u32[]{:S(2)}, u32[]{:S(2)}) collective-permute-start(f32[64,256]{1,0:T(8,128)S(1)} %add.82), channel_id=1, source_target_pairs={{0,8},{2,10},{4,12},{6,14},{8,0},{10,2},{12,4},{14,6},{16,24},{18,... | collective-permute-start | bytes 196616 | tf_op jit(solution)/shard_map/ppermute | solution.py:19
  55.8 6.7 %collective-permute-start.22 = (f32[64,256]{1,0:T(8,128)S(1)}, f32[64,256]{1,0:T(8,128)S(1)}, u32[]{:S(2)}, u32[]{:S(2)}) collective-permute-start(f32[64,256]{1,0:T(8,128)S(1)} %add.82), channel_id=1, source_target_pairs={{0,12},{2,14},{4,8},{6,10},{8,4},{10,6},{12,0},{14,2},{16,28},{18,... | collective-permute-start | bytes 196616 | tf_op jit(solution)/shard_map/ppermute | solution.py:19
  57.4 5.1 %collective-permute-start.20 = (f32[64,256]{1,0:T(8,128)S(1)}, f32[64,256]{1,0:T(8,128)S(1)}, u32[]{:S(2)}, u32[]{:S(2)}) collective-permute-start(f32[64,256]{1,0:T(8,128)S(1)} %add.82), channel_id=1, source_target_pairs={{0,4},{2,6},{4,0},{6,2},{8,12},{10,14},{12,8},{14,10},{16,20},{18,... | collective-permute-start | bytes 196616 | tf_op jit(solution)/shard_map/ppermute | solution.py:19
  62.5 4.1 %collective-permute-start.25 = (bf16[64,256]{1,0:T(8,128)(2,1)S(1)}, bf16[64,256]{1,0:T(8,128)(2,1)S(1)}, u32[]{:S(2)}, u32[]{:S(2)}) collective-permute-start(bf16[64,256]{1,0:T(8,128)(2,1)S(1)} %add_convert_fusion.1), channel_id=1, source_target_pairs={{0,192},{2,194},{4,196},{6,198},{8,200},{10,202},{12,204},{14,206}... | collective-permute-start | bytes 98312 | tf_op jit(solution)/shard_map/ppermute | solution.py:19
  62.6 4.4 %collective-permute-start.24 = (bf16[64,256]{1,0:T(8,128)(2,1)S(1)}, bf16[64,256]{1,0:T(8,128)(2,1)S(1)}, u32[]{:S(2)}, u32[]{:S(2)}) collective-permute-start(bf16[64,256]{1,0:T(8,128)(2,1)S(1)} %add_convert_fusion.1), channel_id=1, source_target_pairs={{0,128},{2,130},{4,132},{6,134},{8,136},{10,138},{12,140},{14,142}... | collective-permute-start | bytes 98312 | tf_op jit(solution)/shard_map/ppermute | solution.py:19
  62.7 5.0 %collective-permute-start.23 = (bf16[64,256]{1,0:T(8,128)(2,1)S(1)}, bf16[64,256]{1,0:T(8,128)(2,1)S(1)}, u32[]{:S(2)}, u32[]{:S(2)}) collective-permute-start(bf16[64,256]{1,0:T(8,128)(2,1)S(1)} %add_convert_fusion.1), channel_id=1, source_target_pairs={{0,64},{2,66},{4,68},{6,70},{8,72},{10,74},{12,76},{14,78},{16,80}... | collective-permute-start | bytes 98312 | tf_op jit(solution)/shard_map/ppermute | solution.py:19
  67.8 4.9 %collective-permute-start.29 = (bf16[64,384]{1,0:T(8,128)(2,1)S(1)}, bf16[64,384]{1,0:T(8,128)(2,1)S(1)}, u32[]{:S(2)}, u32[]{:S(2)}) collective-permute-start(bf16[64,384]{1,0:T(8,128)(2,1)S(1)} %get-tuple-element.41), channel_id=1, source_target_pairs={{0,48},{2,50},{4,52},{6,54},{8,56},{10,58},{12,60},{14,62},{16,32}... | collective-permute-start | bytes 147464 | tf_op jit(solution)/shard_map/ppermute | solution.py:19
  69.6 5.0 %collective-permute-start.28 = (bf16[64,384]{1,0:T(8,128)(2,1)S(1)}, bf16[64,384]{1,0:T(8,128)(2,1)S(1)}, u32[]{:S(2)}, u32[]{:S(2)}) collective-permute-start(bf16[64,384]{1,0:T(8,128)(2,1)S(1)} %get-tuple-element.40), channel_id=1, source_target_pairs={{0,32},{2,34},{4,36},{6,38},{8,40},{10,42},{12,44},{14,46},{16,48}... | collective-permute-start | bytes 147464 | tf_op jit(solution)/shard_map/ppermute | solution.py:19
  69.6 5.0 %collective-permute-start.27 = (bf16[64,384]{1,0:T(8,128)(2,1)S(1)}, bf16[64,384]{1,0:T(8,128)(2,1)S(1)}, u32[]{:S(2)}, u32[]{:S(2)}) collective-permute-start(bf16[64,384]{1,0:T(8,128)(2,1)S(1)} %get-tuple-element.39), channel_id=1, source_target_pairs={{0,16},{2,18},{4,20},{6,22},{8,24},{10,26},{12,28},{14,30},{16,0},... | collective-permute-start | bytes 147464 | tf_op jit(solution)/shard_map/ppermute | solution.py:19
  74.7 3.3 %collective-permute-start.30 = (f32[64,256]{1,0:T(8,128)S(1)}, f32[64,256]{1,0:T(8,128)S(1)}, u32[]{:S(2)}, u32[]{:S(2)}) collective-permute-start(f32[64,256]{1,0:T(8,128)S(1)} %fusion.5.own_ref), channel_id=1, source_target_pairs={{0,2},{2,0},{4,6},{6,4},{8,10},{10,8},{12,14},{14,12},{16,18},{18,... | collective-permute-start | bytes 196616 | tf_op jit(solution)/shard_map/ppermute | solution.py:19
